TPU v7x, 32 devices: a whole 2x2x4 slice. The times are simulated.
32 devices in a mesh: grp: 2 (over y), pb: 4 (over z), re: 2 (over x), ka: 2 (over core).
Axes of the slice: x: 2, y: 2, z: 4, core: 2. Of those that a mesh axis runs over, the one named last changes fastest.
Arguments:
- g_wann: bfloat16 [2, 1024, 128, 256], P(None, 'pb', ('grp', 're'), 'ka'), parts along dimension 2, may hold values from -0.0234375 to 0.0234375
- phonon_phase: bfloat16 [2, 2048, 1024], P(None, 'pb'), may hold values from -1 to 1, as said below
- electron_phase: bfloat16 [2, 8, 64], replicated, may hold values from -1 to 1, as said below
Outputs:
- coupling: float32 [16, 2, 2048, 256], P(('grp', 're'), None, 'pb', 'ka'), parts along dimension 0
There are 2 independent parts, one for each index of `grp`. A program takes and returns all parts, laid end to end along the dimension named above; an argument that names none is the same for every part. Nothing has to cross between parts.
Inputs may be any that keep to these rules, and one draw needn't show every extreme that they name: `phonon_phase`: entries 0 and 1 along the first dimension are the cosine and sine of one angle. `electron_phase`: entries 0 and 1 along the first dimension are the cosine and sine of one angle.
All inputs are finite; a program needn't handle non-finite values.
Results may differ from a plain program's by a relative error of at most 0.0029.
Values may be sent and summed in bfloat16 or wider, within the bound.
No kernel may reach another device: no remote copies, remote signals or barrier semaphores. Data moves between devices by JAX's collectives and lax.ppermute only.
A program may use at most 64 MiB of HBM per device.

v0:
```python
import jax
import jax.numpy as jnp
from jax import lax
from jax.sharding import PartitionSpec as P


def electron_term(phase, wann_real, wann_imag):
    real_part = jnp.einsum(
        "ke,peb->kpb", phase[0], wann_real, preferred_element_type=jnp.float32
    ) - jnp.einsum("ke,peb->kpb", phase[1], wann_imag, preferred_element_type=jnp.float32)
    imag_part = jnp.einsum(
        "ke,peb->kpb", phase[0], wann_imag, preferred_element_type=jnp.float32
    ) + jnp.einsum("ke,peb->kpb", phase[1], wann_real, preferred_element_type=jnp.float32)
    return jnp.stack([real_part, imag_part])


def body(g_wann, phonon_phase, electron_phase):
    local_vectors = g_wann.shape[2]
    offset = lax.axis_index("re") * local_vectors
    own_phase = lax.dynamic_slice_in_dim(electron_phase, offset, local_vectors, 2)
    partial_value = electron_term(own_phase, g_wann[0], g_wann[1])
    summed = lax.psum_scatter(partial_value, "re", scatter_dimension=1, tiled=True)
    bloch = summed.astype(jnp.bfloat16)
    cos_table = phonon_phase[0]
    sin_table = phonon_phase[1]
    piece = lax.all_gather(bloch, "pb", axis=2, tiled=True)
    acc_real = jnp.einsum(
        "qp,kpb->kqb", cos_table, piece[0], preferred_element_type=jnp.float32
    ) - jnp.einsum("qp,kpb->kqb", sin_table, piece[1], preferred_element_type=jnp.float32)
    acc_imag = jnp.einsum(
        "qp,kpb->kqb", cos_table, piece[1], preferred_element_type=jnp.float32
    ) + jnp.einsum("qp,kpb->kqb", sin_table, piece[0], preferred_element_type=jnp.float32)
    acc_real, acc_imag = (acc_real, acc_imag)
    return jnp.stack([acc_real, acc_imag], axis=1)


def solution(mesh):
    placed = (P(None, "pb", ("grp", "re"), "ka"), P(None, "pb", None), P())
    return jax.shard_map(
        body,
        mesh=mesh,
        in_specs=placed,
        out_specs=P(("grp", "re"), None, "pb", "ka"),
        check_vma=False,
    )
```

profile of v0, /device:TPU:0, one launch (start us, length us, event | category | flops | bytes accessed | tf_op | source)
XLA Modules:
  0.0 110.8 jit_solution(2155230755220057174)
XLA Ops:
  6.5 0.0 copy-start
  6.5 0.0 reduce-scatter.2.cloned.1.call-start
  6.5 0.7 copy-done
  7.2 2.2 %fusion = f32[8,256,128]{2,0,1:T(8,128)S(1)} fusion(bf16[2,256,32,128]{3,2,1,0:T(8,128)(2,1)} %param.3, bf16[2,8,64]{2,1,0:T(8,128)(2,1)S(1)} %copy-done, s32[]{:T(128)S(6)} %select_n.3), kind=kOutput, calls=%fused_computation.2 | convolution fusion | flops 16777216 | bytes 3147780 | tf_op jit(solution)/shard_map/ke,peb->kpb/dot_general | solution.py:11
  9.4 2.0 %fusion.2 = f32[8,256,128]{2,0,1:T(8,128)S(1)} fusion(bf16[2,256,32,128]{3,2,1,0:T(8,128)(2,1)} %param.3, bf16[2,8,64]{2,1,0:T(8,128)(2,1)S(1)} %copy-done, s32[]{:T(128)S(6)} %add.18, s32[]{:T(128)S(6)} %select_n.3), kind=kOutput, calls=%fused_computation.4 | convolution fusion | flops 16777216 | bytes 3147784 | tf_op jit(solution)/shard_map/ke,peb->kpb/dot_general | solution.py:10
  11.5 0.0 copy-done.1
  11.5 0.5 fusion.21
  11.9 0.5 fusion.15
  12.4 0.1 pad_maximum_fusion
  12.5 1.7 %copy.9 = f32[2,8,256,128]{3,2,0,1:T(8,128)} copy(f32[2,8,256,128]{3,1,2,0:T(8,128)S(1)} %pad_maximum_fusion) | data formatting | bytes 4194304 | tf_op jit(solution)/shard_map/stack | solution.py:14
  14.2 0.0 reduce-scatter.2.cloned.1.call-update
  14.3 0.0 all-gather.2.cloned.1.call-start
  14.3 34.6 %reduce-scatter.2.cloned.1.call-done = f32[2,4,256,128]{3,2,0,1:T(8,128)} async-done(((f32[2,8,256,128]{3,2,0,1:T(8,128)}), f32[2,4,256,128]{3,2,0,1:T(8,128)}) %reduce-scatter.2.cloned.1.call-update) | async-done | bytes 1048592 | tf_op jit(solution)/shard_map/reduce_scatter | solution.py:22
  48.9 2.2 %copy.10 = bf16[2,4,256,128]{2,3,1,0:T(8,128)(2,1)} copy(f32[2,4,256,128]{3,2,0,1:T(8,128)} %reduce-scatter.2.cloned.1.call-done) | data formatting | bytes 1572864 | tf_op jit(solution)/shard_map/reduce_scatter | solution.py:22
  51.1 0.0 all-gather.2.cloned.1.call-update
  51.2 46.4 %all-gather.2.cloned.1.call-done = bf16[2,4,1024,128]{2,3,1,0:T(8,128)(2,1)} async-done(((bf16[2,4,256,128]{2,3,1,0:T(8,128)(2,1)}), bf16[2,4,1024,128]{2,3,1,0:T(8,128)(2,1)}) %all-gather.2.cloned.1.call-update) | async-done | bytes 2097168 | tf_op jit(solution)/shard_map/all_gather | solution.py:26
  97.6 0.0 copy-done.2
  97.6 2.1 %fusion.28 = f32[4,128,512]{2,1,0:T(8,128)S(1)} fusion(bf16[2,4,1024,128]{2,3,1,0:T(8,128)(2,1)} %all-gather.2.cloned.1.call-done, bf16[2,512,1024]{2,1,0:T(8,128)(2,1)S(1)} %copy-done.2), kind=kOutput, calls=%fused_computation.26 | convolution fusion | flops 536870912 | bytes 3145728 | tf_op jit(solution)/shard_map/qp,kpb->kqb/dot_general | solution.py:30
  99.7 0.0 copy-done.3
  99.7 0.7 fusion.30
  100.5 0.7 fusion.24
  101.2 0.7 fusion.25
  102.0 0.2 pad_maximum_fusion.1
  102.1 1.8 %copy.11 = f32[4,2,512,128]{3,2,1,0:T(8,128)} copy(f32[4,2,512,128]{2,3,0,1:T(8,128)S(1)} %pad_maximum_fusion.1) | data formatting | bytes 4194304 | tf_op jit(solution)/shard_map/stack | solution.py:34
  (3 shorter events, 0.0 us)
Async XLA Ops:
  6.5 0.7 copy-start
  6.5 42.4 %reduce-scatter.2.cloned.1.call-start = ((), (), s32[]{:S(2)}) async-start(), calls=%async_computation.1 | async-start | bytes 3145728 | tf_op jit(solution)/shard_map/reduce_scatter | solution.py:22
  7.2 4.2 %copy-start.1 = (bf16[2,256,32,128]{3,2,1,0:T(8,128)(2,1)S(1)}, bf16[2,256,32,128]{3,2,1,0:T(8,128)(2,1)}, u32[]{:S(2)}) copy-start(bf16[2,256,32,128]{3,2,1,0:T(8,128)(2,1)} %param.3) | copy-start | bytes 12582916
  14.2 83.3 %copy-start.2 = (bf16[2,512,1024]{2,1,0:T(8,128)(2,1)S(1)}, bf16[2,512,1024]{2,1,0:T(8,128)(2,1)}, u32[]{:S(2)}) copy-start(bf16[2,512,1024]{2,1,0:T(8,128)(2,1)} %param.4) | copy-start | bytes 6291460
  14.3 83.3 %all-gather.2.cloned.1.call-start = ((), (), s32[]{:S(2)}) async-start(), calls=%async_computation.2 | async-start | bytes 2621440 | tf_op jit(solution)/shard_map/all_gather | solution.py:26
  97.6 2.1 %copy-start.3 = (bf16[2,4,1024,128]{2,3,1,0:T(8,128)(2,1)S(1)}, bf16[2,4,1024,128]{2,3,1,0:T(8,128)(2,1)}, u32[]{:S(2)}) copy-start(bf16[2,4,1024,128]{2,3,1,0:T(8,128)(2,1)} %all-gather.2.cloned.1.call-done) | copy-start | bytes 6291460
Sparse Core Ops, SparseCore 0:
  14.4 34.4 reduce-scatter.1
  51.3 46.2 all-gather.1
where the time goes:
time: 111 us
  waiting for transfers between devices  81.1 us (73%)
  between operations  13.5 us (12%)
  matrix products  9.49 us (9%)
  local copies, waits for them, and re-layouts  6.43 us (6%)
    all_gather x1, waiting for transfers between devices, body(): piece = lax.all_gather(bloch, 'pb', axis=2, tiled=True)  46.4 us
    reduce_scatter x1, waiting for transfers between devices, body(): lax.psum_scatter(partial_value, 're', scatter_dimension=1, tiled=True)  34.6 us
    reduce_scatter x1, local copies, waits for them, and re-layouts, body(): lax.psum_scatter(partial_value, 're', scatter_dimension=1, tiled=True)  2.22 us
  transfers between devices with their start and end apart: 2, of which 2 were waited for; matrix products, arithmetic and copies ran while one was open for 0% of the time, Pallas kernels for 0%

commit v1 on v0

v1 whole, which is shorter than its diff:
```python
import functools

import jax
import jax.numpy as jnp
from jax import lax
from jax.experimental import pallas as pl
from jax.experimental.pallas import tpu as pltpu
from jax.sharding import PartitionSpec as P

GROUP = 8
CHUNKS = 2


def phase_matrix(phase, n_re):
    k_all, e_all = phase.shape[1:]
    me = lax.axis_index("re")
    e_own, k_own = e_all // n_re, k_all // n_re
    own = lax.dynamic_slice_in_dim(phase, me * e_own, e_own, 2)
    cos, sin = own[0], own[1]
    rows = jnp.stack([jnp.stack([cos, -sin], 1), jnp.stack([sin, cos], 1)])
    rows = rows.reshape(2, n_re, k_own, 2, e_own).transpose(1, 0, 2, 3, 4)
    rows = jnp.roll(rows, -me, 0)
    eye = jnp.eye(GROUP, dtype=phase.dtype)
    big = rows[:, :, :, None, :, None, :] * eye[None, None, None, :, None, :, None]
    return big.reshape(n_re * 2 * k_own * GROUP, 2 * GROUP * e_own)


def electron_kernel(sizes, w_ref, g_ref, *out_refs):
    n_re, k_own = sizes
    p_block, e_own, b = g_ref.shape[1:]
    depth = GROUP * e_own
    for i in range(p_block // GROUP):
        at = pl.ds(i * GROUP, GROUP)
        real = g_ref[0, at].reshape(depth, b)
        imag = g_ref[1, at].reshape(depth, b)
        out = jnp.dot(w_ref[:, :depth], real, preferred_element_type=jnp.float32)
        out += jnp.dot(w_ref[:, depth:], imag, preferred_element_type=jnp.float32)
        out = out.reshape(n_re, 2, k_own, GROUP, b)
        for s in range(n_re):
            first = 0
            for ref in out_refs[s * CHUNKS : (s + 1) * CHUNKS]:
                ref[:, :, at] = out[s, :, first : first + ref.shape[1]]
                first += ref.shape[1]


def electron_sums(weights, g_wann, n_re, k_own, cuts):
    _, p_own, e_own, b = g_wann.shape
    block = min(64, p_own)
    shapes = [jax.ShapeDtypeStruct((2, size, p_own, b), jnp.float32) for _ in range(n_re) for size in cuts]
    outs = pl.pallas_call(
        functools.partial(electron_kernel, (n_re, k_own)),
        grid=(p_own // block,),
        in_specs=[
            pl.BlockSpec(weights.shape, lambda i: (0, 0)),
            pl.BlockSpec((2, block, e_own, b), lambda i: (0, i, 0, 0)),
        ],
        out_specs=[pl.BlockSpec((2, s.shape[1], block, b), lambda i: (0, 0, i, 0)) for s in shapes],
        out_shape=shapes,
        compiler_params=pltpu.CompilerParams(vmem_limit_bytes=32 * 2**20),
        cost_estimate=pl.CostEstimate(flops=2 * 2 * weights.shape[0] * e_own * p_own * b, bytes_accessed=2 * g_wann.size * 2, transcendentals=0),
    )(weights, g_wann)
    return [outs[s * len(cuts) : (s + 1) * len(cuts)] for s in range(n_re)]


def phonon_kernel(n_blocks, sorted_table, order_ref, table_ref, *refs):
    blocks = refs[:n_blocks]
    out_ref = refs[-1]
    p_own, b = blocks[0].shape[2:]
    total = None
    for n, ref in enumerate(blocks):
        at = pl.ds(n * p_own, p_own) if sorted_table else pl.ds(pl.multiple_of(order_ref[n] * p_own, p_own), p_own)
        real, imag = ref[0, 0], ref[1, 0]
        part = jnp.dot(table_ref[0, :, at], jnp.concatenate([real, imag], 1), preferred_element_type=jnp.float32)
        part += jnp.dot(table_ref[1, :, at], jnp.concatenate([-imag, real], 1), preferred_element_type=jnp.float32)
        total = part if total is None else total + part
    out_ref[0, 0] = total[:, :b]
    out_ref[0, 1] = total[:, b:]


def phonon_sums(order, table, blocks, prior, first, k_own):
    _, q, p_all = table.shape
    _, size, p_own, b = blocks[0].shape
    extra = [] if prior is None else [prior]
    sorted_table = p_own % 128 != 0
    if sorted_table:
        table = table.reshape(2, q, len(blocks), p_own)[:, :, order].reshape(table.shape)
    return pl.pallas_call(
        functools.partial(phonon_kernel, len(blocks), sorted_table),
        grid_spec=pltpu.PrefetchScalarGridSpec(
            num_scalar_prefetch=1,
            grid=(size,),
            in_specs=[pl.BlockSpec(table.shape, lambda k, o: (0, 0, 0))]
            + [pl.BlockSpec((2, 1, p_own, b), lambda k, o: (0, k, 0, 0)) for _ in blocks]
            + [pl.BlockSpec(memory_space=pl.ANY) for _ in extra],
            out_specs=pl.BlockSpec((1, 2, q, b), lambda k, o: (first + k, 0, 0, 0)),
        ),
        out_shape=jax.ShapeDtypeStruct((k_own, 2, q, b), jnp.float32),
        input_output_aliases={2 + len(blocks): 0} if extra else {},
        compiler_params=pltpu.CompilerParams(vmem_limit_bytes=32 * 2**20),
        cost_estimate=pl.CostEstimate(flops=8 * q * p_all * b * size, bytes_accessed=table.size * 2 + size * q * b * 8, transcendentals=0),
    )(order, table, *blocks, *extra)


def gather_line(block, n):
    me = lax.axis_index("pb")
    if n == 4:
        near = lax.ppermute(block, "pb", [(i, i ^ 1) for i in range(n)])
        far = lax.ppermute(block, "pb", [(i, i ^ 3) for i in range(n)])
        middle = (me == 1) | (me == 2)
        last = lax.ppermute(jnp.where(middle, far, block), "pb", [(0, 2), (3, 1), (1, 0), (2, 3)])
        order = jnp.stack([me, me ^ 1, me ^ 3, me ^ 2])
        return [block, near, far, last], order
    blocks = [block] + [lax.ppermute(block, "pb", [(i, (i + s) % n) for i in range(n)]) for s in range(1, n)]
    return blocks, jnp.stack([(me - s) % n for s in range(n)])


def body(n_re, n_pb, g_wann, phonon_phase, electron_phase):
    k_own = electron_phase.shape[1] // n_re
    cuts = [k_own // CHUNKS] * CHUNKS
    weights = phase_matrix(electron_phase, n_re)
    partial_sums = electron_sums(weights, g_wann, n_re, k_own, cuts)
    result, first = None, 0
    for c, size in enumerate(cuts):
        total = partial_sums[0][c]
        for s in range(1, n_re):
            total = total + lax.ppermute(partial_sums[s][c], "re", [(i, (i + s) % n_re) for i in range(n_re)])
        blocks, order = gather_line(total.astype(jnp.bfloat16), n_pb)
        result = phonon_sums(order.astype(jnp.int32), phonon_phase, blocks, result, first, k_own)
        first += size
    return result


def solution(mesh):
    return jax.shard_map(
        functools.partial(body, mesh.shape["re"], mesh.shape["pb"]),
        mesh=mesh,
        in_specs=(P(None, "pb", ("grp", "re"), "ka"), P(None, "pb", None), P()),
        out_specs=P(("grp", "re"), None, "pb", "ka"),
        check_vma=False,
    )
```

time: 111 us -> 68 us (0.61)
  waiting for transfers between devices: 81.1 us -> 35 us
  starting transfers between devices: 0.04 us -> 17.8 us
  between operations: 13.5 us -> 0.06 us
  Pallas kernels: 0 us -> 9.72 us
  matrix products: 9.49 us -> 0 us
  local copies, waits for them, and re-layouts: 6.43 us -> 3.41 us
  other arithmetic: 0.31 us -> 1.81 us
    all_gather x1 -> x0, waiting for transfers between devices: 46.4 us -> none  [body(): piece = lax.all_gather(bloch, 'pb', axis=2, tiled=True)]
    ppermute x0 -> x8, waiting for transfers between devices: none -> 35 us  [the longest x2 18.8 us: body(): lax.ppermute(partial_sums[s][c], 're', [(i, (i + s) % n_re) for i in rang...]
    reduce_scatter x1 -> x0, waiting for transfers between devices: 34.6 us -> none  [body(): lax.psum_scatter(partial_value, 're', scatter_dimension=1, tiled=True)]
    ppermute x0 -> x8, starting transfers between devices: none -> 17.8 us  [the longest x2 8.15 us: gather_line(): far = lax.ppermute(block, 'pb', [(i, i ^ 3) for i in range(n)])]
    pallas_call x0 -> x3, Pallas kernels: none -> 9.72 us  [the longest x2 7.57 us: phonon_sums(): pl.pallas_call(functools.partial(phonon_kernel, len(blocks), sorted_table...]
    dot_general x8 -> x0, matrix products: 9.49 us -> none  [the longest x1 2.19 us: electron_term(): jnp.einsum('ke,peb->kpb', phase[0], wann_imag, preferred_element_type=jnp...]
    another operation x2 -> x0, local copies, waits for them, and re-layouts: 3.51 us -> none  [the longest x1 1.81 us: body(): return jnp.stack([acc_real, acc_imag], axis=1)]
    reduce_scatter x1 -> x0, local copies, waits for them, and re-layouts: 2.22 us -> none  [body(): lax.psum_scatter(partial_value, 're', scatter_dimension=1, tiled=True)]
  transfers between devices with their start and end apart: 2 -> 8, of which waited for: 2 -> 6; matrix products, arithmetic and copies ran while one was open for 0% -> 2% of each run, Pallas kernels for 0% -> 6%
where the time goes in v1:
time: 68 us; the launch traced here: 67.8 us
  waiting for transfers between devices  35 us (51%)
  starting transfers between devices  17.8 us (26%)
  Pallas kernels  9.72 us (14%)
  local copies, waits for them, and re-layouts  3.41 us (5%)
  other arithmetic  1.81 us (3%)
    ppermute x2, waiting for transfers between devices, body(): lax.ppermute(partial_sums[s][c], 're', [(i, (i + s) % n_re) for i in rang...  18.8 us
    ppermute x2, starting transfers between devices, gather_line(): far = lax.ppermute(block, 'pb', [(i, i ^ 3) for i in range(n)])  8.15 us
    pallas_call x2, Pallas kernels, phonon_sums(): pl.pallas_call(functools.partial(phonon_kernel, len(blocks), sorted_table...  7.57 us
    ppermute x2, waiting for transfers between devices, gather_line(): lax.ppermute(jnp.where(middle, far, block), 'pb', [(0, 2), (3, 1), (1, 0)...  6.36 us
    ppermute x2, waiting for transfers between devices, gather_line(): near = lax.ppermute(block, 'pb', [(i, i ^ 1) for i in range(n)])  5.41 us
    ppermute x2, starting transfers between devices, gather_line(): lax.ppermute(jnp.where(middle, far, block), 'pb', [(0, 2), (3, 1), (1, 0)...  4.55 us
    ppermute x2, waiting for transfers between devices, gather_line(): far = lax.ppermute(block, 'pb', [(i, i ^ 3) for i in range(n)])  4.47 us
    ppermute x2, starting transfers between devices, body(): lax.ppermute(partial_sums[s][c], 're', [(i, (i + s) % n_re) for i in rang...  3.08 us
  transfers between devices with their start and end apart: 8, of which 6 were waited for; matrix products, arithmetic and copies ran while one was open for 2% of the time, Pallas kernels for 6%

profile of v1, /device:TPU:0, one launch (start us, length us, event | category | flops | bytes accessed | tf_op | source)
XLA Modules:
  0.0 67.8 jit_solution(6034397970421085716)
XLA Ops:
  0.0 0.8 %constant_dynamic-slice_fusion.1 = (bf16[1,8,32]{2,1,0:T(8,128)(2,1)S(1)}, bf16[1,8,32]{2,1,0:T(8,128)(2,1)S(1)}) fusion(bf16[2,8,64]{2,1,0:T(8,128)(2,1)} %param.5, s32[]{:T(128)S(6)} %add.27, s32[]{:T(128)S(6)} %select_n.28), kind=kLoop, calls=%fused_computation.12 | loop fusion | bytes 2056 | tf_op jit(solution)/shard_map/slice | solution.py:19
  0.9 0.1 broadcast_multiply_fusion
  1.0 0.4 mul.24.w_ref
  1.4 2.2 %copy-done.1 = bf16[2,256,32,128]{3,2,1,0:T(8,128)(2,1)S(1)} copy-done((bf16[2,256,32,128]{3,2,1,0:T(8,128)(2,1)S(1)}, bf16[2,256,32,128]{3,2,1,0:T(8,128)(2,1)}, u32[]{:S(2)}) %copy-start.1) | copy-done | bytes 4194328
  3.6 2.1 %shard_map.37 = (f32[2,2,256,128]{3,2,1,0:T(8,128)S(1)}, f32[2,2,256,128]{3,2,1,0:T(8,128)S(1)}, f32[2,2,256,128]{3,2,1,0:T(8,128)S(1)}, f32[2,2,256,128]{3,2,1,0:T(8,128)S(1)}) custom-call(bf16[128,512]{1,0:T(8,128)(2,1)S(1)} %mul.24.w_ref, bf16[2,256,32,128]{3,2,1,0:T(8,128)(2,1)S(1)} %copy-done.1), custom_call_target="tpu_custom_call" | custom-call | flops 536870912 | bytes 8388608 | tf_op jit(solution)/shard_map/pallas_call | solution.py:50
  5.8 3.0 %collective-permute-start.4 = (f32[2,2,256,128]{3,2,1,0:T(8,128)S(1)}, f32[2,2,256,128]{3,2,1,0:T(8,128)S(1)}, u32[]{:S(2)}, u32[]{:S(2)}) collective-permute-start(f32[2,2,256,128]{3,2,1,0:T(8,128)S(1)} %get-tuple-element.12), channel_id=1, source_target_pairs={{0,2},{2,0},{1,3},{3,1},{4,6},{6,4},{5,7},{7,5},{8,10},{10,8},{9,1... | collective-permute-start | bytes 1572872 | tf_op jit(solution)/shard_map/ppermute | solution.py:126
  8.8 0.1 collective-permute-start
  8.9 12.7 %collective-permute-done.4 = f32[2,2,256,128]{3,2,1,0:T(8,128)S(1)} collective-permute-done((f32[2,2,256,128]{3,2,1,0:T(8,128)S(1)}, f32[2,2,256,128]{3,2,1,0:T(8,128)S(1)}, u32[]{:S(2)}, u32[]{:S(2)}) %collective-permute-start.4) | collective-permute-done | bytes 524320 | tf_op jit(solution)/shard_map/ppermute | solution.py:126
  21.5 0.1 add_convert_fusion.refs_0_
  21.6 4.2 %collective-permute-start.6 = (bf16[2,2,256,128]{3,2,1,0:T(8,128)(2,1)S(1)}, bf16[2,2,256,128]{3,2,1,0:T(8,128)(2,1)S(1)}, u32[]{:S(2)}, u32[]{:S(2)}) collective-permute-start(bf16[2,2,256,128]{3,2,1,0:T(8,128)(2,1)S(1)} %add_convert_fusion.refs_0_), channel_id=1, source_target_pairs={{0,12},{4,8},{8,4},{12,0},{1,13},{5,9},{9,5},{13,1},{2,14},{6,10},... | collective-permute-start | bytes 786440 | tf_op jit(solution)/shard_map/ppermute | solution.py:108
  25.8 6.1 %collective-permute-done = f32[2,2,256,128]{3,2,1,0:T(8,128)S(1)} collective-permute-done((f32[2,2,256,128]{3,2,1,0:T(8,128)S(1)}, f32[2,2,256,128]{3,2,1,0:T(8,128)S(1)}, u32[]{:S(2)}, u32[]{:S(2)}) %collective-permute-start) | collective-permute-done | bytes 524320 | tf_op jit(solution)/shard_map/ppermute | solution.py:126
  31.9 0.1 add_convert_fusion.1.refs_0_
  32.0 3.9 %collective-permute-start.2 = (bf16[2,2,256,128]{3,2,1,0:T(8,128)(2,1)S(1)}, bf16[2,2,256,128]{3,2,1,0:T(8,128)(2,1)S(1)}, u32[]{:S(2)}, u32[]{:S(2)}) collective-permute-start(bf16[2,2,256,128]{3,2,1,0:T(8,128)(2,1)S(1)} %add_convert_fusion.1.refs_0_), channel_id=1, source_target_pairs={{0,12},{4,8},{8,4},{12,0},{1,13},{5,9},{9,5},{13,1},{2,14},{6,10},... | collective-permute-start | bytes 786440 | tf_op jit(solution)/shard_map/ppermute | solution.py:108
  35.9 2.0 %collective-permute-start.5 = (bf16[2,2,256,128]{3,2,1,0:T(8,128)(2,1)S(1)}, bf16[2,2,256,128]{3,2,1,0:T(8,128)(2,1)S(1)}, u32[]{:S(2)}, u32[]{:S(2)}) collective-permute-start(bf16[2,2,256,128]{3,2,1,0:T(8,128)(2,1)S(1)} %add_convert_fusion.refs_0_), channel_id=1, source_target_pairs={{0,4},{4,0},{8,12},{12,8},{1,5},{5,1},{9,13},{13,9},{2,6},{6,2},{1... | collective-permute-start | bytes 786440 | tf_op jit(solution)/shard_map/ppermute | solution.py:107
  37.9 0.7 %broadcast_select_fusion = bf16[2,2,256,128]{3,2,1,0:T(8,128)(2,1)} fusion(bf16[2,2,256,128]{3,2,1,0:T(8,128)(2,1)S(1)} %collective-permute-done.6.refs_2_, bf16[2,2,256,128]{3,2,1,0:T(8,128)(2,1)S(1)} %add_convert_fusion.refs_0_, pred[]{:T(512)S(6)} %or.4), kind=kLoop, calls=%fused_computation.3 | loop fusion | flops 131072 | bytes 786433 | tf_op jit(solution)/shard_map/jit(_where)/select_n | solution.py:110
  38.7 4.5 %collective-permute-done.2.refs_2_ = bf16[2,2,256,128]{3,2,1,0:T(8,128)(2,1)S(1)} collective-permute-done((bf16[2,2,256,128]{3,2,1,0:T(8,128)(2,1)S(1)}, bf16[2,2,256,128]{3,2,1,0:T(8,128)(2,1)S(1)}, u32[]{:S(2)}, u32[]{:S(2)}) %collective-permute-start.2) | collective-permute-done | bytes 262176 | tf_op jit(solution)/shard_map/ppermute | solution.py:108
  43.1 0.7 %broadcast_select_fusion.1 = bf16[2,2,256,128]{3,2,1,0:T(8,128)(2,1)} fusion(bf16[2,2,256,128]{3,2,1,0:T(8,128)(2,1)S(1)} %collective-permute-done.2.refs_2_, bf16[2,2,256,128]{3,2,1,0:T(8,128)(2,1)S(1)} %add_convert_fusion.1.refs_0_, pred[]{:T(512)S(6)} %or.4), kind=kLoop, calls=%fused_computation.4 | loop fusion | flops 131072 | bytes 786433 | tf_op jit(solution)/shard_map/jit(_where)/select_n | solution.py:110
  43.9 4.5 %collective-permute-start.3 = (bf16[2,2,256,128]{3,2,1,0:T(8,128)(2,1)}, bf16[2,2,256,128]{3,2,1,0:T(8,128)(2,1)}, u32[]{:S(2)}, u32[]{:S(2)}) collective-permute-start(bf16[2,2,256,128]{3,2,1,0:T(8,128)(2,1)} %broadcast_select_fusion.1), channel_id=1, source_target_pairs={{0,8},{12,4},{4,0},{8,12},{1,9},{13,5},{5,1},{9,13},{2,10},{14,6},... | collective-permute-start | bytes 786440 | tf_op jit(solution)/shard_map/ppermute | solution.py:110
  48.4 0.1 pad_add_fusion.order_ref
  48.5 5.4 %collective-permute-done.5.refs_1_ = bf16[2,2,256,128]{3,2,1,0:T(8,128)(2,1)S(1)} collective-permute-done((bf16[2,2,256,128]{3,2,1,0:T(8,128)(2,1)S(1)}, bf16[2,2,256,128]{3,2,1,0:T(8,128)(2,1)S(1)}, u32[]{:S(2)}, u32[]{:S(2)}) %collective-permute-start.5) | collective-permute-done | bytes 262176 | tf_op jit(solution)/shard_map/ppermute | solution.py:107
  53.9 5.7 %collective-permute-done.7.refs_3_ = bf16[2,2,256,128]{3,2,1,0:T(8,128)(2,1)} collective-permute-done((bf16[2,2,256,128]{3,2,1,0:T(8,128)(2,1)}, bf16[2,2,256,128]{3,2,1,0:T(8,128)(2,1)}, u32[]{:S(2)}, u32[]{:S(2)}) %collective-permute-start.7) | collective-permute-done | bytes 262176 | tf_op jit(solution)/shard_map/ppermute | solution.py:110
  59.6 3.8 %shard_map.38.refs_4_ = f32[4,2,512,128]{3,2,1,0:T(8,128)} custom-call(s32[4]{0:T(128)S(1)} %pad_add_fusion.order_ref, bf16[2,512,1024]{2,1,0:T(8,128)(2,1)S(1)} %copy-done, bf16[2,2,256,128]{3,2,1,0:T(8,128)(2,1)S(1)} %add_convert_fusion.refs_0_, bf16[2,2,256,128]{3,2,1,0:T(8,128)(2,1)S(1)} %collective-permute-done.5.refs_1_, ...), custom_call_target="tpu_custom_call" | custom-call | flops 1073741824 | bytes 3145728 | tf_op jit(solution)/shard_map/pallas_call | solution.py:87
  63.4 0.6 collective-permute-done.3.refs_3_
  64.0 3.8 %shard_map.39 = f32[4,2,512,128]{3,2,1,0:T(8,128)} custom-call(s32[4]{0:T(128)S(1)} %pad_add_fusion.order_ref, bf16[2,512,1024]{2,1,0:T(8,128)(2,1)S(1)} %copy-done, bf16[2,2,256,128]{3,2,1,0:T(8,128)(2,1)S(1)} %add_convert_fusion.1.refs_0_, bf16[2,2,256,128]{3,2,1,0:T(8,128)(2,1)} %collective-permute-done.1.refs_1_, ...), custom_call_target="tpu_custom_call", output_to_operand_aliasing={{}: (6, {})} | custom-call | flops 1073741824 | bytes 3145728 | tf_op jit(solution)/shard_map/pallas_call | solution.py:87
  (12 shorter events, 0.1 us)
Async XLA Ops:
  1.4 2.2 %copy-start.1 = (bf16[2,256,32,128]{3,2,1,0:T(8,128)(2,1)S(1)}, bf16[2,256,32,128]{3,2,1,0:T(8,128)(2,1)}, u32[]{:S(2)}) copy-start(bf16[2,256,32,128]{3,2,1,0:T(8,128)(2,1)} %g_ref.1) | copy-start | bytes 12582916
  5.8 15.8 %collective-permute-start.4 = (f32[2,2,256,128]{3,2,1,0:T(8,128)S(1)}, f32[2,2,256,128]{3,2,1,0:T(8,128)S(1)}, u32[]{:S(2)}, u32[]{:S(2)}) collective-permute-start(f32[2,2,256,128]{3,2,1,0:T(8,128)S(1)} %get-tuple-element.12), channel_id=1, source_target_pairs={{0,2},{2,0},{1,3},{3,1},{4,6},{6,4},{5,7},{7,5},{8,10},{10,8},{9,1... | collective-permute-start | bytes 1572872 | tf_op jit(solution)/shard_map/ppermute | solution.py:126
  8.8 23.2 %collective-permute-start = (f32[2,2,256,128]{3,2,1,0:T(8,128)S(1)}, f32[2,2,256,128]{3,2,1,0:T(8,128)S(1)}, u32[]{:S(2)}, u32[]{:S(2)}) collective-permute-start(f32[2,2,256,128]{3,2,1,0:T(8,128)S(1)} %get-tuple-element.10), channel_id=1, source_target_pairs={{0,2},{2,0},{1,3},{3,1},{4,6},{6,4},{5,7},{7,5},{8,10},{10,8},{9,1... | collective-permute-start | bytes 1572872 | tf_op jit(solution)/shard_map/ppermute | solution.py:126
  21.5 38.1 %copy-start = (bf16[2,512,1024]{2,1,0:T(8,128)(2,1)S(1)}, bf16[2,512,1024]{2,1,0:T(8,128)(2,1)}, u32[]{:S(2)}) copy-start(bf16[2,512,1024]{2,1,0:T(8,128)(2,1)} %table_ref.3) | copy-start | bytes 6291460
  21.6 16.3 %collective-permute-start.6 = (bf16[2,2,256,128]{3,2,1,0:T(8,128)(2,1)S(1)}, bf16[2,2,256,128]{3,2,1,0:T(8,128)(2,1)S(1)}, u32[]{:S(2)}, u32[]{:S(2)}) collective-permute-start(bf16[2,2,256,128]{3,2,1,0:T(8,128)(2,1)S(1)} %add_convert_fusion.refs_0_), channel_id=1, source_target_pairs={{0,12},{4,8},{8,4},{12,0},{1,13},{5,9},{9,5},{13,1},{2,14},{6,10},... | collective-permute-start | bytes 786440 | tf_op jit(solution)/shard_map/ppermute | solution.py:108
  32.0 11.2 %collective-permute-start.2 = (bf16[2,2,256,128]{3,2,1,0:T(8,128)(2,1)S(1)}, bf16[2,2,256,128]{3,2,1,0:T(8,128)(2,1)S(1)}, u32[]{:S(2)}, u32[]{:S(2)}) collective-permute-start(bf16[2,2,256,128]{3,2,1,0:T(8,128)(2,1)S(1)} %add_convert_fusion.1.refs_0_), channel_id=1, source_target_pairs={{0,12},{4,8},{8,4},{12,0},{1,13},{5,9},{9,5},{13,1},{2,14},{6,10},... | collective-permute-start | bytes 786440 | tf_op jit(solution)/shard_map/ppermute | solution.py:108
  35.9 27.5 %collective-permute-start.1 = (bf16[2,2,256,128]{3,2,1,0:T(8,128)(2,1)S(1)}, bf16[2,2,256,128]{3,2,1,0:T(8,128)(2,1)}, u32[]{:S(2)}, u32[]{:S(2)}) collective-permute-start(bf16[2,2,256,128]{3,2,1,0:T(8,128)(2,1)S(1)} %add_convert_fusion.1.refs_0_), channel_id=1, source_target_pairs={{0,4},{4,0},{8,12},{12,8},{1,5},{5,1},{9,13},{13,9},{2,6},{6,2},{1... | collective-permute-start | bytes 786440 | tf_op jit(solution)/shard_map/ppermute | solution.py:107
  35.9 18.0 %collective-permute-start.5 = (bf16[2,2,256,128]{3,2,1,0:T(8,128)(2,1)S(1)}, bf16[2,2,256,128]{3,2,1,0:T(8,128)(2,1)S(1)}, u32[]{:S(2)}, u32[]{:S(2)}) collective-permute-start(bf16[2,2,256,128]{3,2,1,0:T(8,128)(2,1)S(1)} %add_convert_fusion.refs_0_), channel_id=1, source_target_pairs={{0,4},{4,0},{8,12},{12,8},{1,5},{5,1},{9,13},{13,9},{2,6},{6,2},{1... | collective-permute-start | bytes 786440 | tf_op jit(solution)/shard_map/ppermute | solution.py:107
  38.7 21.0 %collective-permute-start.7 = (bf16[2,2,256,128]{3,2,1,0:T(8,128)(2,1)}, bf16[2,2,256,128]{3,2,1,0:T(8,128)(2,1)}, u32[]{:S(2)}, u32[]{:S(2)}) collective-permute-start(bf16[2,2,256,128]{3,2,1,0:T(8,128)(2,1)} %broadcast_select_fusion), channel_id=1, source_target_pairs={{0,8},{12,4},{4,0},{8,12},{1,9},{13,5},{5,1},{9,13},{2,10},{14,6},... | collective-permute-start | bytes 786440 | tf_op jit(solution)/shard_map/ppermute | solution.py:110
  43.9 20.1 %collective-permute-start.3 = (bf16[2,2,256,128]{3,2,1,0:T(8,128)(2,1)}, bf16[2,2,256,128]{3,2,1,0:T(8,128)(2,1)}, u32[]{:S(2)}, u32[]{:S(2)}) collective-permute-start(bf16[2,2,256,128]{3,2,1,0:T(8,128)(2,1)} %broadcast_select_fusion.1), channel_id=1, source_target_pairs={{0,8},{12,4},{4,0},{8,12},{1,9},{13,5},{5,1},{9,13},{2,10},{14,6},... | collective-permute-start | bytes 786440 | tf_op jit(solution)/shard_map/ppermute | solution.py:110

commit v2 on v0

v2 whole, which is shorter than its diff:
```python
import functools

import jax
import jax.numpy as jnp
from jax import lax
from jax.experimental import pallas as pl
from jax.experimental.pallas import tpu as pltpu
from jax.sharding import PartitionSpec as P

GROUP = 8
SIDE = 2
PIECES = 4
TAIL = 16
FULL = 32768.0
POWERS = (64, 32, 16, 8, 4, 2)
HEAD = 4
CUTS = (2, 2)
ADDCOST = [0, 10**10, 10**10]
GATES = {('block', 2): [('near', 0), ('far', 0)], ('last', 0): [('near', 0)], ('received', 1): [('block', 0)], ('received', 2): [('block', 0)]}
RELCOST = [0, 0, 0]
PHON = 80
SMALL = 16 * 2**20
LARGE = 50 * 2**20
VMEM = pl.BlockSpec(memory_space=pltpu.VMEM)
HBM = pl.BlockSpec(memory_space=pltpu.HBM)


def pick(me, n, choices):
    out = choices[0]
    for i in range(1, n):
        out = jnp.where(me == i, choices[i], out)
    return out


def phase_rows(me, n_re, phase_ref):
    k_all, e_all = phase_ref.shape[1:]
    e_own, k_own = e_all // n_re, k_all // n_re
    width = GROUP * e_own
    tables = []
    for part in range(2):
        full = phase_ref[part].astype(jnp.float32)
        own = pick(me, n_re, [full[:, r * e_own : (r + 1) * e_own] for r in range(n_re)])
        tables.append(jnp.concatenate([own] * GROUP, 1))
    row = lax.broadcasted_iota(jnp.int32, (k_own * GROUP, width), 0) % GROUP
    column = lax.broadcasted_iota(jnp.int32, (k_own * GROUP, width), 1) // e_own
    spread = []
    for table in tables:
        groups = [table[r * k_own : (r + 1) * k_own] for r in range(n_re)]
        moved = [pick(me, n_re, groups[s:] + groups[:s]) for s in range(n_re)]
        spread.append([
            jnp.where(row == column, jnp.broadcast_to(m[:, None], (k_own, GROUP, width)).reshape(k_own * GROUP, width), 0.0)
            for m in moved
        ])
    cos, sin = spread
    left = jnp.concatenate([x for s in range(n_re) for x in (cos[s], sin[s])], 0)
    right = jnp.concatenate([x for s in range(n_re) for x in (-sin[s], cos[s])], 0)
    return left.astype(jnp.bfloat16), right.astype(jnp.bfloat16)


def electron_kernel(n_re, cuts, pieces, start, phase_ref, g_ref, *refs):
    n = len(cuts)
    own_refs, send_refs = refs[:n], refs[n : n_re * n]
    g_vmem, left_ref, right_ref, sems = refs[n_re * n :]
    _, rows, e_own, b = g_vmem.shape
    size = rows // pieces
    copies = [
        pltpu.make_async_copy(g_ref.at[:, pl.ds(start + i * size, size)], g_vmem.at[:, pl.ds(i * size, size)], sems.at[i])
        for i in range(pieces)
    ]
    for copy in copies:
        copy.start()
    left_ref[...], right_ref[...] = phase_rows(lax.axis_index("re"), n_re, phase_ref)
    depth = GROUP * e_own
    step = SIDE * GROUP
    largest = jnp.zeros((GROUP, b), jnp.float32)
    for i in range(rows // step):
        if i * step % size == 0:
            copies[i * step // size].wait()
        groups = [pl.ds(i * step + j * GROUP, GROUP) for j in range(SIDE)]
        real = jnp.concatenate([g_vmem[0, at].reshape(depth, b) for at in groups], 1)
        imag = jnp.concatenate([g_vmem[1, at].reshape(depth, b) for at in groups], 1)
        out = jnp.dot(left_ref[...], real, preferred_element_type=jnp.float32)
        out += jnp.dot(right_ref[...], imag, preferred_element_type=jnp.float32)
        out = out.reshape(n_re, 2, -1, GROUP, SIDE * b)
        if n_re > 1:
            sent = jnp.max(jnp.abs(out[1:].reshape(-1, GROUP, SIDE * b)), 0)
            for j in range(SIDE):
                largest = jnp.maximum(largest, sent[:, j * b : (j + 1) * b])
        for j, at in enumerate(groups):
            first = 0
            for c, kept in enumerate(cuts):
                own_refs[c][:, :, at] = out[0, :, first : first + kept, :, j * b : (j + 1) * b]
                for s in range(1, n_re):
                    for part in range(2):
                        for k in range(kept):
                            row = (part * kept + k) * rows + i * step + j * GROUP
                            send_refs[(s - 1) * n + c][pl.ds(row, GROUP)] = out[s, part, first + k, :, j * b : (j + 1) * b]
                first += kept
    if n_re > 1:
        top = jnp.max(largest, keepdims=True)
        scale, exponent = jnp.ones((1, 1), jnp.float32), jnp.zeros((1, 1), jnp.float32)
        for bit in POWERS:
            fits = top * scale * 2.0**bit <= FULL
            scale = jnp.where(fits, scale * 2.0**bit, scale)
            exponent = jnp.where(fits, exponent + bit, exponent)
        for ref in send_refs:
            last = ref.shape[0] - TAIL
            ref[pl.ds(0, last)] = ref[pl.ds(0, last)] * scale
            ref[pl.ds(last, TAIL)] = jnp.broadcast_to(exponent, (TAIL, b))


def electron_sums(phase, g_wann, n_re, cuts, start, rows):
    _, _, e_own, b = g_wann.shape
    k_all = phase.shape[1]
    pieces = PIECES if rows % (PIECES * SIDE * GROUP) == 0 else 1
    own = [jax.ShapeDtypeStruct((2, size, rows, b), jnp.float32) for size in cuts]
    send = [jax.ShapeDtypeStruct((2 * size * rows + TAIL, b), jnp.float32) for _ in range(n_re - 1) for size in cuts]
    outs = pl.pallas_call(
        functools.partial(electron_kernel, n_re, cuts, pieces, start),
        in_specs=[VMEM, HBM],
        out_specs=[VMEM] * len(own + send),
        out_shape=own + send,
        scratch_shapes=[
            pltpu.VMEM((2, rows, e_own, b), g_wann.dtype),
            pltpu.VMEM((2 * k_all * GROUP, GROUP * e_own), jnp.bfloat16),
            pltpu.VMEM((2 * k_all * GROUP, GROUP * e_own), jnp.bfloat16),
            pltpu.SemaphoreType.DMA((pieces,)),
        ],
        compiler_params=pltpu.CompilerParams(vmem_limit_bytes=LARGE),
        cost_estimate=pl.CostEstimate(flops=8 * k_all * e_own * rows * b, bytes_accessed=4 * rows * e_own * b, transcendentals=0),
    )(phase, g_wann)
    return outs[: len(cuts)], [outs[s * len(cuts) : (s + 1) * len(cuts)] for s in range(1, n_re)]


def add_kernel(own_ref, *refs):
    out_ref = refs[-1]
    _, kept, rows, _ = own_ref.shape
    factors = []
    for ref in refs[:-1]:
        exponent = ref[pl.ds(ref.shape[0] - TAIL, 1)]
        factor = jnp.ones_like(exponent)
        for bit in POWERS:
            taken = exponent >= bit
            exponent = jnp.where(taken, exponent - bit, exponent)
            factor = jnp.where(taken, factor * 2.0**-bit, factor)
        factors.append(factor)
    for part in range(2):
        for k in range(kept):
            total = own_ref[part, k]
            for ref, factor in zip(refs[:-1], factors):
                total = total + ref[pl.ds((part * kept + k) * rows, rows)] * factor
            out_ref[part, k] = total.astype(out_ref.dtype)


def add_up(own, received, cost):
    return pl.pallas_call(
        add_kernel,
        in_specs=[VMEM] * (1 + len(received)),
        out_specs=VMEM,
        out_shape=jax.ShapeDtypeStruct(own.shape, jnp.bfloat16),
        compiler_params=pltpu.CompilerParams(vmem_limit_bytes=SMALL),
        cost_estimate=pl.CostEstimate(flops=cost, bytes_accessed=0, transcendentals=0),
    )(own, *received)


def block_order(n):
    me = lax.axis_index("pb")
    if n == 4:
        return [me, me ^ 1, me ^ 3, me ^ 2]
    return [(me - s) % n for s in range(n)]


def relay_kernel(block_ref, far_ref, out_ref):
    me = lax.axis_index("pb")
    middle = (me == 1) | (me == 2)
    for c in range(2):
        out_ref[c] = jnp.where(middle, far_ref[c], block_ref[c])


def relay(block, far, cost):
    return pl.pallas_call(
        relay_kernel,
        in_specs=[VMEM, VMEM],
        out_specs=VMEM,
        out_shape=jax.ShapeDtypeStruct(block.shape, block.dtype),
        compiler_params=pltpu.CompilerParams(vmem_limit_bytes=SMALL),
        cost_estimate=pl.CostEstimate(flops=cost, bytes_accessed=0, transcendentals=0),
    )(block, far)


def after(x, *others):
    return lax.optimization_barrier((x, *others))[0] if others else x


def phonon_part(order, table_ref, blocks, first, k):
    total = None
    for n, (head_ref, rest_ref) in enumerate(blocks):
        p_own = head_ref.shape[2] + rest_ref.shape[2]
        at = pl.ds(n * p_own, p_own) if order is None else pl.ds(pl.multiple_of(order[n] * p_own, p_own), p_own)
        real, imag = [jnp.concatenate([head_ref[c, first + k], rest_ref[c, k]], 0) for c in range(2)]
        part = jnp.dot(table_ref[0, :, at], jnp.concatenate([real, imag], 1), preferred_element_type=jnp.float32)
        part += jnp.dot(table_ref[1, :, at], jnp.concatenate([-imag, real], 1), preferred_element_type=jnp.float32)
        total = part if total is None else total + part
    return total


def main_kernel(n, order_of, first, table_ref, *refs):
    blocks = [refs[2 * i : 2 * i + 2] for i in range(n)]
    order, out_ref = order_of(), refs[2 * n]
    for k in range(out_ref.shape[0]):
        out_ref[k] = phonon_part(order, table_ref, blocks, first, k)


def final_kernel(n, order_of, first, has_acc, has_prior, table_ref, *refs):
    blocks = [refs[2 * i : 2 * i + 2] for i in range(n)]
    order = order_of()
    acc_ref = refs[2 * n] if has_acc else None
    out_ref, staged, sems = refs[2 * n + has_acc + has_prior :]
    size, b = staged.shape[0], staged.shape[3]
    copies = []
    for k in range(size):
        total = phonon_part(order, table_ref, blocks, first, k)
        if has_acc:
            total += acc_ref[k]
        staged[k, 0] = total[:, :b]
        staged[k, 1] = total[:, b:]
        copies.append(pltpu.make_async_copy(staged.at[k], out_ref.at[first + k], sems.at[k]))
        copies[-1].start()
    for copy in copies:
        copy.wait()


def phonon_main(order_of, table, blocks, first):
    q = table.shape[1]
    _, size, rows, b = blocks[0][1].shape
    flat = [x for block in blocks for x in block]
    return pl.pallas_call(
        functools.partial(main_kernel, len(blocks), order_of, first),
        in_specs=[VMEM] * (1 + len(flat)),
        out_specs=VMEM,
        out_shape=jax.ShapeDtypeStruct((size, q, 2 * b), jnp.float32),
        compiler_params=pltpu.CompilerParams(vmem_limit_bytes=SMALL),
        cost_estimate=pl.CostEstimate(flops=PHON * q * rows * len(blocks) * b * size, bytes_accessed=0, transcendentals=0),
    )(table, *flat)


def phonon_final(order_of, table, blocks, acc, prior, first, k_own):
    q = table.shape[1]
    _, size, rows, b = blocks[0][1].shape
    flat = [x for block in blocks for x in block]
    more = [] if acc is None else [acc]
    alias = [] if prior is None else [prior]
    return pl.pallas_call(
        functools.partial(final_kernel, len(blocks), order_of, first, len(more), len(alias)),
        in_specs=[VMEM] * (1 + len(flat) + len(more)) + [HBM] * len(alias),
        out_specs=HBM,
        out_shape=jax.ShapeDtypeStruct((k_own, 2, q, b), jnp.float32),
        scratch_shapes=[pltpu.VMEM((size, 2, q, b), jnp.float32), pltpu.SemaphoreType.DMA((size,))],
        input_output_aliases={1 + len(flat) + len(more): 0} if alias else {},
        compiler_params=pltpu.CompilerParams(vmem_limit_bytes=SMALL),
        cost_estimate=pl.CostEstimate(flops=PHON * q * rows * len(blocks) * b * size, bytes_accessed=size * q * b * 8, transcendentals=0),
    )(table, *flat, *more, *alias)


class Transfers:
    def __init__(self, n_re, n_pb, own, send):
        self.n_re, self.n_pb, self.own, self.send = n_re, n_pb, own, send
        self.made = {}

    def get(self, kind, c):
        if (kind, c) not in self.made:
            self.made[kind, c] = None
            self.made[kind, c] = getattr(self, kind)(c)
        return self.made[kind, c]

    def gated(self, x, kind, c):
        return after(x, *[self.get(*other) for other in GATES.get((kind, c), [])])

    def received(self, c):
        out = []
        for s in range(1, self.n_re):
            message = self.gated(self.send[s - 1][c].astype(jnp.float16), "received", c)
            got = lax.ppermute(message, "re", [(i, (i + s) % self.n_re) for i in range(self.n_re)])
            out.append(got.astype(jnp.float32))
        return out

    def block(self, c):
        return add_up(self.own[c], [self.gated(got, "block", c) for got in self.get("received", c)], ADDCOST[c])

    def near(self, c):
        block = self.gated(self.get("block", c), "near", c)
        return lax.ppermute(block, "pb", [(i, i ^ 1) for i in range(self.n_pb)])

    def far(self, c):
        block = self.gated(self.get("block", c), "far", c)
        return lax.ppermute(block, "pb", [(i, i ^ 3) for i in range(self.n_pb)])

    def last(self, c):
        passed_on = relay(self.get("block", c), self.gated(self.get("far", c), "last", c), RELCOST[c])
        return lax.ppermute(passed_on, "pb", [(0, 2), (3, 1), (1, 0), (2, 3)])

    def gathered(self, c):
        block, n = self.get("block", c), self.n_pb
        if n == 4:
            return [block, self.get("near", c), self.get("far", c), self.get("last", c)]
        return [block] + [lax.ppermute(block, "pb", [(i, (i + s) % n) for i in range(n)]) for s in range(1, n)]


def body(n_re, n_pb, g_wann, phonon_phase, electron_phase):
    k_own = electron_phase.shape[1] // n_re
    p_own = g_wann.shape[1]
    cuts = [k_own * c // sum(CUTS) for c in CUTS]
    ahead = p_own // HEAD
    own, send = electron_sums(electron_phase, g_wann, n_re, [k_own], 0, ahead)
    own_rest, send_rest = electron_sums(electron_phase, g_wann, n_re, cuts, ahead, p_own - ahead)
    transfers = Transfers(n_re, n_pb, own + own_rest, [a + b for a, b in zip(send, send_rest)])
    gathered = [transfers.gathered(c) for c in range(1 + len(cuts))]
    table = phonon_phase
    q = table.shape[1]
    orders = [functools.partial(lambda i: block_order(n_pb)[i:], i) for i in (0, n_pb - 1)]
    if p_own % 128 != 0:
        table = table.reshape(2, q, n_pb, p_own)[:, :, jnp.stack(block_order(n_pb))].reshape(table.shape)
        orders = [lambda: None] * 2
    result, first = None, 0
    for c, size in enumerate(cuts):
        blocks = list(zip(gathered[0], gathered[1 + c]))
        acc, order_of = None, orders[0]
        if c == len(cuts) - 1 and p_own % 128 == 0:
            acc = phonon_main(order_of, table, blocks[:-1], first)
            blocks, order_of = blocks[-1:], orders[1]
        result = phonon_final(order_of, table, blocks, acc, result, first, k_own)
        first += size
    return result


def solution(mesh):
    return jax.shard_map(
        functools.partial(body, mesh.shape["re"], mesh.shape["pb"]),
        mesh=mesh,
        in_specs=(P(None, "pb", ("grp", "re"), "ka"), P(None, "pb", None), P()),
        out_specs=P(("grp", "re"), None, "pb", "ka"),
        check_vma=False,
    )
```

time: 111 us -> 50.5 us (0.45)
  waiting for transfers between devices: 81.1 us -> 2.89 us
  starting transfers between devices: 0.04 us -> 36.9 us
  between operations: 13.5 us -> 0.13 us
  Pallas kernels: 0 us -> 9.6 us
  matrix products: 9.49 us -> 0 us
  local copies, waits for them, and re-layouts: 6.43 us -> 0.69 us
    all_gather x1 -> x0, waiting for transfers between devices: 46.4 us -> none  [body(): piece = lax.all_gather(bloch, 'pb', axis=2, tiled=True)]
    ppermute x0 -> x12, starting transfers between devices: none -> 36.9 us  [the longest x3 11.4 us: last(): return lax.ppermute(passed_on, 'pb', [(0, 2), (3, 1), (1, 0), (2, 3)])]
    reduce_scatter x1 -> x0, waiting for transfers between devices: 34.6 us -> none  [body(): lax.psum_scatter(partial_value, 're', scatter_dimension=1, tiled=True)]
    pallas_call x0 -> x11, Pallas kernels: none -> 9.6 us  [the longest x2 4.61 us: electron_sums(): pl.pallas_call(functools.partial(electron_kernel, n_re, cuts, pieces, sta...]
    dot_general x8 -> x0, matrix products: 9.49 us -> none  [the longest x1 2.19 us: electron_term(): jnp.einsum('ke,peb->kpb', phase[0], wann_imag, preferred_element_type=jnp...]
    another operation x2 -> x0, local copies, waits for them, and re-layouts: 3.51 us -> none  [the longest x1 1.81 us: body(): return jnp.stack([acc_real, acc_imag], axis=1)]
    ppermute x0 -> x12, waiting for transfers between devices: none -> 2.89 us  [the longest x3 1.16 us: last(): return lax.ppermute(passed_on, 'pb', [(0, 2), (3, 1), (1, 0), (2, 3)])]
    reduce_scatter x1 -> x0, local copies, waits for them, and re-layouts: 2.22 us -> none  [body(): lax.psum_scatter(partial_value, 're', scatter_dimension=1, tiled=True)]
  transfers between devices with their start and end apart: 2 -> 12, of which waited for: 2 -> 3; matrix products, arithmetic and copies ran while one was open for 0% -> 0% of each run, Pallas kernels for 0% -> 12%
where the time goes in v2:
time: 50.5 us; the launch traced here: 50.3 us
  starting transfers between devices  36.9 us (73%)
  Pallas kernels  9.6 us (19%)
  waiting for transfers between devices  2.89 us (6%)
  local copies, waits for them, and re-layouts  0.69 us (1%)
    ppermute x3, starting transfers between devices, last(): return lax.ppermute(passed_on, 'pb', [(0, 2), (3, 1), (1, 0), (2, 3)])  11.4 us
    ppermute x3, starting transfers between devices, far(): return lax.ppermute(block, 'pb', [(i, i ^ 3) for i in range(self.n_pb)])  10.3 us
    ppermute x3, starting transfers between devices, near(): return lax.ppermute(block, 'pb', [(i, i ^ 1) for i in range(self.n_pb)])  9.81 us
    ppermute x3, starting transfers between devices, received(): lax.ppermute(message, 're', [(i, (i + s) % self.n_re) for i in range(self...  5.35 us
    pallas_call x2, Pallas kernels, electron_sums(): pl.pallas_call(functools.partial(electron_kernel, n_re, cuts, pieces, sta...  4.61 us
    pallas_call x2, Pallas kernels, phonon_final(): pl.pallas_call(functools.partial(final_kernel, len(blocks), order_of, fir...  3.69 us
    ppermute x3, waiting for transfers between devices, last(): return lax.ppermute(passed_on, 'pb', [(0, 2), (3, 1), (1, 0), (2, 3)])  1.16 us
  transfers between devices with their start and end apart: 12, of which 3 were waited for; matrix products, arithmetic and copies ran while one was open for 0% of the time, Pallas kernels for 12%

profile of v2, /device:TPU:0, one launch (start us, length us, event | category | flops | bytes accessed | tf_op | source)
XLA Modules:
  0.0 50.3 jit_solution(14665096837405650690)
XLA Ops:
  0.0 0.7 %copy-done.1 = bf16[2,8,64]{2,1,0:T(8,128)(2,1)S(1)} copy-done((bf16[2,8,64]{2,1,0:T(8,128)(2,1)S(1)}, bf16[2,8,64]{2,1,0:T(8,128)(2,1)}, u32[]{:S(2)}) %copy-start.1) | copy-done | bytes 2072
  0.7 2.0 %shard_map.37 = (f32[2,4,64,128]{3,2,1,0:T(8,128)S(1)}, f32[528,128]{1,0:T(8,128)S(1)}) custom-call(bf16[2,8,64]{2,1,0:T(8,128)(2,1)S(1)} %copy-done.1, bf16[2,256,32,128]{3,2,1,0:T(8,128)(2,1)} %g_ref.3), custom_call_target="tpu_custom_call" | custom-call | flops 16777216 | bytes 1048576 | tf_op jit(solution)/shard_map/pallas_call | solution.py:118
  2.7 3.0 %collective-permute-start = (f16[528,128]{1,0:T(8,128)(2,1)S(1)}, f16[528,128]{1,0:T(8,128)(2,1)S(1)}, u32[]{:S(2)}, u32[]{:S(2)}) collective-permute-start(f16[528,128]{1,0:T(8,128)(2,1)S(1)} %convert_element_type.18), channel_id=1, source_target_pairs={{0,2},{2,0},{1,3},{3,1},{4,6},{6,4},{5,7},{7,5},{8,10},{10,8},{9,1... | collective-permute-start | bytes 405512 | tf_op jit(solution)/shard_map/ppermute | solution.py:283
  5.7 2.6 %shard_map.40 = (f32[2,2,192,128]{3,2,1,0:T(8,128)S(1)}, f32[2,2,192,128]{3,2,1,0:T(8,128)S(1)}, f32[784,128]{1,0:T(8,128)S(1)}, f32[784,128]{1,0:T(8,128)S(1)}) custom-call(bf16[2,8,64]{2,1,0:T(8,128)(2,1)S(1)} %copy-done.1, bf16[2,256,32,128]{3,2,1,0:T(8,128)(2,1)} %g_ref.3), custom_call_target="tpu_custom_call" | custom-call | flops 50331648 | bytes 3145728 | tf_op jit(solution)/shard_map/pallas_call | solution.py:118
  8.4 0.9 %collective-permute-done = f16[528,128]{1,0:T(8,128)(2,1)S(1)} collective-permute-done((f16[528,128]{1,0:T(8,128)(2,1)S(1)}, f16[528,128]{1,0:T(8,128)(2,1)S(1)}, u32[]{:S(2)}, u32[]{:S(2)}) %collective-permute-start) | collective-permute-done | bytes 135200 | tf_op jit(solution)/shard_map/ppermute | solution.py:283
  9.4 1.8 %collective-permute-start.8 = (f16[784,128]{1,0:T(8,128)(2,1)S(1)}, f16[784,128]{1,0:T(8,128)(2,1)S(1)}, u32[]{:S(2)}, u32[]{:S(2)}) collective-permute-start(f16[784,128]{1,0:T(8,128)(2,1)S(1)} %convert_element_type.22), channel_id=1, source_target_pairs={{0,2},{2,0},{1,3},{3,1},{4,6},{6,4},{5,7},{7,5},{8,10},{10,8},{9,1... | collective-permute-start | bytes 602120 | tf_op jit(solution)/shard_map/ppermute | solution.py:283
  11.2 1.6 %collective-permute-start.2 = (bf16[2,4,64,128]{3,2,1,0:T(8,128)(2,1)S(1)}, bf16[2,4,64,128]{3,2,1,0:T(8,128)(2,1)S(1)}, u32[]{:S(2)}, u32[]{:S(2)}) collective-permute-start(bf16[2,4,64,128]{3,2,1,0:T(8,128)(2,1)S(1)} %shard_map.38.block_ref.refs_0_), channel_id=1, source_target_pairs={{0,4},{4,0},{8,12},{12,8},{1,5},{5,1},{9,13},{13,9},{2,6},{6,2},{1... | collective-permute-start | bytes 393224 | tf_op jit(solution)/shard_map/ppermute | solution.py:292
  12.9 2.5 %collective-permute-start.1 = (bf16[2,4,64,128]{3,2,1,0:T(8,128)(2,1)S(1)}, bf16[2,4,64,128]{3,2,1,0:T(8,128)(2,1)S(1)}, u32[]{:S(2)}, u32[]{:S(2)}) collective-permute-start(bf16[2,4,64,128]{3,2,1,0:T(8,128)(2,1)S(1)} %shard_map.38.block_ref.refs_0_), channel_id=1, source_target_pairs={{0,12},{4,8},{8,4},{12,0},{1,13},{5,9},{9,5},{13,1},{2,14},{6,10},... | collective-permute-start | bytes 393224 | tf_op jit(solution)/shard_map/ppermute | solution.py:296
  15.4 0.5 %collective-permute-start.4 = (f16[784,128]{1,0:T(8,128)(2,1)S(1)}, f16[784,128]{1,0:T(8,128)(2,1)S(1)}, u32[]{:S(2)}, u32[]{:S(2)}) collective-permute-start(f16[784,128]{1,0:T(8,128)(2,1)S(1)} %convert_element_type.20), channel_id=1, source_target_pairs={{0,2},{2,0},{1,3},{3,1},{4,6},{6,4},{5,7},{7,5},{8,10},{10,8},{9,1... | collective-permute-start | bytes 602120 | tf_op jit(solution)/shard_map/ppermute | solution.py:283
  15.9 0.1 shard_map.44.block_ref.refs_1_
  16.0 5.2 %collective-permute-start.10 = (bf16[2,2,192,128]{3,2,1,0:T(8,128)(2,1)S(1)}, bf16[2,2,192,128]{3,2,1,0:T(8,128)(2,1)S(1)}, u32[]{:S(2)}, u32[]{:S(2)}) collective-permute-start(bf16[2,2,192,128]{3,2,1,0:T(8,128)(2,1)S(1)} %shard_map.44.block_ref.refs_1_), channel_id=1, source_target_pairs={{0,12},{4,8},{8,4},{12,0},{1,13},{5,9},{9,5},{13,1},{2,14},{6,10},... | collective-permute-start | bytes 589832 | tf_op jit(solution)/shard_map/ppermute | solution.py:296
  21.2 0.8 %collective-permute-done.1.far_ref.refs_4_ = bf16[2,4,64,128]{3,2,1,0:T(8,128)(2,1)S(1)} collective-permute-done((bf16[2,4,64,128]{3,2,1,0:T(8,128)(2,1)S(1)}, bf16[2,4,64,128]{3,2,1,0:T(8,128)(2,1)S(1)}, u32[]{:S(2)}, u32[]{:S(2)}) %collective-permute-start.1) | collective-permute-done | bytes 131104 | tf_op jit(solution)/shard_map/ppermute | solution.py:296
  22.0 0.1 shard_map.41.block_ref.refs_1_
  22.0 2.7 %collective-permute-start.5 = (bf16[2,2,192,128]{3,2,1,0:T(8,128)(2,1)S(1)}, bf16[2,2,192,128]{3,2,1,0:T(8,128)(2,1)S(1)}, u32[]{:S(2)}, u32[]{:S(2)}) collective-permute-start(bf16[2,2,192,128]{3,2,1,0:T(8,128)(2,1)S(1)} %shard_map.41.block_ref.refs_1_), channel_id=1, source_target_pairs={{0,12},{4,8},{8,4},{12,0},{1,13},{5,9},{9,5},{13,1},{2,14},{6,10},... | collective-permute-start | bytes 589832 | tf_op jit(solution)/shard_map/ppermute | solution.py:296
  24.7 6.2 %collective-permute-start.7 = (bf16[2,2,192,128]{3,2,1,0:T(8,128)(2,1)S(1)}, bf16[2,2,192,128]{3,2,1,0:T(8,128)(2,1)S(1)}, u32[]{:S(2)}, u32[]{:S(2)}) collective-permute-start(bf16[2,2,192,128]{3,2,1,0:T(8,128)(2,1)S(1)} %shard_map.41.block_ref.refs_1_), channel_id=1, source_target_pairs={{0,4},{4,0},{8,12},{12,8},{1,5},{5,1},{9,13},{13,9},{2,6},{6,2},{1... | collective-permute-start | bytes 589832 | tf_op jit(solution)/shard_map/ppermute | solution.py:292
  30.9 0.1 collective-permute-start.3
  31.0 2.0 %collective-permute-start.9 = (bf16[2,2,192,128]{3,2,1,0:T(8,128)(2,1)S(1)}, bf16[2,2,192,128]{3,2,1,0:T(8,128)(2,1)S(1)}, u32[]{:S(2)}, u32[]{:S(2)}) collective-permute-start(bf16[2,2,192,128]{3,2,1,0:T(8,128)(2,1)S(1)} %shard_map.44.block_ref.refs_1_), channel_id=1, source_target_pairs={{0,4},{4,0},{8,12},{12,8},{1,5},{5,1},{9,13},{13,9},{2,6},{6,2},{1... | collective-permute-start | bytes 589832 | tf_op jit(solution)/shard_map/ppermute | solution.py:292
  33.0 0.1 shard_map.45
  33.1 4.8 %collective-permute-start.11 = (bf16[2,2,192,128]{3,2,1,0:T(8,128)(2,1)S(1)}, bf16[2,2,192,128]{3,2,1,0:T(8,128)(2,1)S(1)}, u32[]{:S(2)}, u32[]{:S(2)}) collective-permute-start(bf16[2,2,192,128]{3,2,1,0:T(8,128)(2,1)S(1)} %shard_map.45), channel_id=1, source_target_pairs={{0,8},{12,4},{4,0},{8,12},{1,9},{13,5},{5,1},{9,13},{2,10},{14,6},... | collective-permute-start | bytes 589832 | tf_op jit(solution)/shard_map/ppermute | solution.py:300
  37.9 6.5 %collective-permute-start.6 = (bf16[2,2,192,128]{3,2,1,0:T(8,128)(2,1)S(1)}, bf16[2,2,192,128]{3,2,1,0:T(8,128)(2,1)S(1)}, u32[]{:S(2)}, u32[]{:S(2)}) collective-permute-start(bf16[2,2,192,128]{3,2,1,0:T(8,128)(2,1)S(1)} %shard_map.42), channel_id=1, source_target_pairs={{0,8},{12,4},{4,0},{8,12},{1,9},{13,5},{5,1},{9,13},{2,10},{14,6},... | collective-permute-start | bytes 589832 | tf_op jit(solution)/shard_map/ppermute | solution.py:300
  44.5 1.0 %shard_map.43.refs_2_ = f32[2,512,256]{2,1,0:T(8,128)S(1)} custom-call(bf16[2,512,1024]{2,1,0:T(8,128)(2,1)S(1)} %copy-done, bf16[2,4,64,128]{3,2,1,0:T(8,128)(2,1)S(1)} %shard_map.38.block_ref.refs_0_, bf16[2,2,192,128]{3,2,1,0:T(8,128)(2,1)S(1)} %shard_map.41.block_ref.refs_1_, bf16[2,4,64,128]{3,2,1,0:T(8,128)(2,1)S(1)} %collective-permute-done.2.refs_2_, ...), custom_call_target="tpu_custom_call" | custom-call | flops 6039797760 | tf_op jit(solution)/shard_map/pallas_call | solution.py:237
  45.5 1.1 %collective-permute-done.11.refs_7_ = bf16[2,2,192,128]{3,2,1,0:T(8,128)(2,1)S(1)} collective-permute-done((bf16[2,2,192,128]{3,2,1,0:T(8,128)(2,1)S(1)}, bf16[2,2,192,128]{3,2,1,0:T(8,128)(2,1)S(1)}, u32[]{:S(2)}, u32[]{:S(2)}) %collective-permute-start.11) | collective-permute-done | bytes 196640 | tf_op jit(solution)/shard_map/ppermute | solution.py:300
  46.6 2.2 %shard_map.46.refs_3_ = f32[4,2,512,128]{3,2,1,0:T(8,128)} custom-call(bf16[2,512,1024]{2,1,0:T(8,128)(2,1)S(1)} %copy-done, bf16[2,4,64,128]{3,2,1,0:T(8,128)(2,1)S(1)} %shard_map.38.block_ref.refs_0_, bf16[2,2,192,128]{3,2,1,0:T(8,128)(2,1)S(1)} %shard_map.44.block_ref.refs_1_, bf16[2,4,64,128]{3,2,1,0:T(8,128)(2,1)S(1)} %collective-permute-done.2.refs_2_, ...), custom_call_target="tpu_custom_call" | custom-call | flops 8053063680 | bytes 1048576 | tf_op jit(solution)/shard_map/pallas_call | solution.py:253
  48.9 1.5 %shard_map.47 = f32[4,2,512,128]{3,2,1,0:T(8,128)} custom-call(bf16[2,512,1024]{2,1,0:T(8,128)(2,1)S(1)} %copy-done, bf16[2,4,64,128]{3,2,1,0:T(8,128)(2,1)S(1)} %collective-permute-done.3.refs_6_.refs_0_, bf16[2,2,192,128]{3,2,1,0:T(8,128)(2,1)S(1)} %collective-permute-done.6.refs_1_, ...), custom_call_target="tpu_custom_call", output_to_operand_aliasing={{}: (4, {})} | custom-call | flops 2013265920 | bytes 1048576 | tf_op jit(solution)/shard_map/pallas_call | solution.py:253
  (21 shorter events, 0.3 us)
Async XLA Ops:
  0.0 0.7 %copy-start.1 = (bf16[2,8,64]{2,1,0:T(8,128)(2,1)S(1)}, bf16[2,8,64]{2,1,0:T(8,128)(2,1)}, u32[]{:S(2)}) copy-start(bf16[2,8,64]{2,1,0:T(8,128)(2,1)} %phase_ref.3) | copy-start | bytes 6148
  2.7 6.6 %collective-permute-start = (f16[528,128]{1,0:T(8,128)(2,1)S(1)}, f16[528,128]{1,0:T(8,128)(2,1)S(1)}, u32[]{:S(2)}, u32[]{:S(2)}) collective-permute-start(f16[528,128]{1,0:T(8,128)(2,1)S(1)} %convert_element_type.18), channel_id=1, source_target_pairs={{0,2},{2,0},{1,3},{3,1},{4,6},{6,4},{5,7},{7,5},{8,10},{10,8},{9,1... | collective-permute-start | bytes 405512 | tf_op jit(solution)/shard_map/ppermute | solution.py:283
  9.4 6.5 %collective-permute-start.8 = (f16[784,128]{1,0:T(8,128)(2,1)S(1)}, f16[784,128]{1,0:T(8,128)(2,1)S(1)}, u32[]{:S(2)}, u32[]{:S(2)}) collective-permute-start(f16[784,128]{1,0:T(8,128)(2,1)S(1)} %convert_element_type.22), channel_id=1, source_target_pairs={{0,2},{2,0},{1,3},{3,1},{4,6},{6,4},{5,7},{7,5},{8,10},{10,8},{9,1... | collective-permute-start | bytes 602120 | tf_op jit(solution)/shard_map/ppermute | solution.py:283
  11.2 10.0 %collective-permute-start.2 = (bf16[2,4,64,128]{3,2,1,0:T(8,128)(2,1)S(1)}, bf16[2,4,64,128]{3,2,1,0:T(8,128)(2,1)S(1)}, u32[]{:S(2)}, u32[]{:S(2)}) collective-permute-start(bf16[2,4,64,128]{3,2,1,0:T(8,128)(2,1)S(1)} %shard_map.38.block_ref.refs_0_), channel_id=1, source_target_pairs={{0,4},{4,0},{8,12},{12,8},{1,5},{5,1},{9,13},{13,9},{2,6},{6,2},{1... | collective-permute-start | bytes 393224 | tf_op jit(solution)/shard_map/ppermute | solution.py:292
  12.9 9.1 %collective-permute-start.1 = (bf16[2,4,64,128]{3,2,1,0:T(8,128)(2,1)S(1)}, bf16[2,4,64,128]{3,2,1,0:T(8,128)(2,1)S(1)}, u32[]{:S(2)}, u32[]{:S(2)}) collective-permute-start(bf16[2,4,64,128]{3,2,1,0:T(8,128)(2,1)S(1)} %shard_map.38.block_ref.refs_0_), channel_id=1, source_target_pairs={{0,12},{4,8},{8,4},{12,0},{1,13},{5,9},{9,5},{13,1},{2,14},{6,10},... | collective-permute-start | bytes 393224 | tf_op jit(solution)/shard_map/ppermute | solution.py:296
  15.4 5.8 %collective-permute-start.4 = (f16[784,128]{1,0:T(8,128)(2,1)S(1)}, f16[784,128]{1,0:T(8,128)(2,1)S(1)}, u32[]{:S(2)}, u32[]{:S(2)}) collective-permute-start(f16[784,128]{1,0:T(8,128)(2,1)S(1)} %convert_element_type.20), channel_id=1, source_target_pairs={{0,2},{2,0},{1,3},{3,1},{4,6},{6,4},{5,7},{7,5},{8,10},{10,8},{9,1... | collective-permute-start | bytes 602120 | tf_op jit(solution)/shard_map/ppermute | solution.py:283
  16.0 17.0 %collective-permute-start.10 = (bf16[2,2,192,128]{3,2,1,0:T(8,128)(2,1)S(1)}, bf16[2,2,192,128]{3,2,1,0:T(8,128)(2,1)S(1)}, u32[]{:S(2)}, u32[]{:S(2)}) collective-permute-start(bf16[2,2,192,128]{3,2,1,0:T(8,128)(2,1)S(1)} %shard_map.44.block_ref.refs_1_), channel_id=1, source_target_pairs={{0,12},{4,8},{8,4},{12,0},{1,13},{5,9},{9,5},{13,1},{2,14},{6,10},... | collective-permute-start | bytes 589832 | tf_op jit(solution)/shard_map/ppermute | solution.py:296
  22.0 22.5 %copy-start = (bf16[2,512,1024]{2,1,0:T(8,128)(2,1)S(1)}, bf16[2,512,1024]{2,1,0:T(8,128)(2,1)}, u32[]{:S(2)}) copy-start(bf16[2,512,1024]{2,1,0:T(8,128)(2,1)} %table_ref.5) | copy-start | bytes 6291460
  22.0 15.8 %collective-permute-start.5 = (bf16[2,2,192,128]{3,2,1,0:T(8,128)(2,1)S(1)}, bf16[2,2,192,128]{3,2,1,0:T(8,128)(2,1)S(1)}, u32[]{:S(2)}, u32[]{:S(2)}) collective-permute-start(bf16[2,2,192,128]{3,2,1,0:T(8,128)(2,1)S(1)} %shard_map.41.block_ref.refs_1_), channel_id=1, source_target_pairs={{0,12},{4,8},{8,4},{12,0},{1,13},{5,9},{9,5},{13,1},{2,14},{6,10},... | collective-permute-start | bytes 589832 | tf_op jit(solution)/shard_map/ppermute | solution.py:296
  24.7 19.7 %collective-permute-start.7 = (bf16[2,2,192,128]{3,2,1,0:T(8,128)(2,1)S(1)}, bf16[2,2,192,128]{3,2,1,0:T(8,128)(2,1)S(1)}, u32[]{:S(2)}, u32[]{:S(2)}) collective-permute-start(bf16[2,2,192,128]{3,2,1,0:T(8,128)(2,1)S(1)} %shard_map.41.block_ref.refs_1_), channel_id=1, source_target_pairs={{0,4},{4,0},{8,12},{12,8},{1,5},{5,1},{9,13},{13,9},{2,6},{6,2},{1... | collective-permute-start | bytes 589832 | tf_op jit(solution)/shard_map/ppermute | solution.py:292
  30.9 14.5 %collective-permute-start.3 = (bf16[2,4,64,128]{3,2,1,0:T(8,128)(2,1)S(1)}, bf16[2,4,64,128]{3,2,1,0:T(8,128)(2,1)S(1)}, u32[]{:S(2)}, u32[]{:S(2)}) collective-permute-start(bf16[2,4,64,128]{3,2,1,0:T(8,128)(2,1)S(1)} %shard_map.39), channel_id=1, source_target_pairs={{0,8},{12,4},{4,0},{8,12},{1,9},{13,5},{5,1},{9,13},{2,10},{14,6},... | collective-permute-start | bytes 393224 | tf_op jit(solution)/shard_map/ppermute | solution.py:300
  31.0 14.5 %collective-permute-start.9 = (bf16[2,2,192,128]{3,2,1,0:T(8,128)(2,1)S(1)}, bf16[2,2,192,128]{3,2,1,0:T(8,128)(2,1)S(1)}, u32[]{:S(2)}, u32[]{:S(2)}) collective-permute-start(bf16[2,2,192,128]{3,2,1,0:T(8,128)(2,1)S(1)} %shard_map.44.block_ref.refs_1_), channel_id=1, source_target_pairs={{0,4},{4,0},{8,12},{12,8},{1,5},{5,1},{9,13},{13,9},{2,6},{6,2},{1... | collective-permute-start | bytes 589832 | tf_op jit(solution)/shard_map/ppermute | solution.py:292
  33.1 13.6 %collective-permute-start.11 = (bf16[2,2,192,128]{3,2,1,0:T(8,128)(2,1)S(1)}, bf16[2,2,192,128]{3,2,1,0:T(8,128)(2,1)S(1)}, u32[]{:S(2)}, u32[]{:S(2)}) collective-permute-start(bf16[2,2,192,128]{3,2,1,0:T(8,128)(2,1)S(1)} %shard_map.45), channel_id=1, source_target_pairs={{0,8},{12,4},{4,0},{8,12},{1,9},{13,5},{5,1},{9,13},{2,10},{14,6},... | collective-permute-start | bytes 589832 | tf_op jit(solution)/shard_map/ppermute | solution.py:300
  37.9 10.9 %collective-permute-start.6 = (bf16[2,2,192,128]{3,2,1,0:T(8,128)(2,1)S(1)}, bf16[2,2,192,128]{3,2,1,0:T(8,128)(2,1)S(1)}, u32[]{:S(2)}, u32[]{:S(2)}) collective-permute-start(bf16[2,2,192,128]{3,2,1,0:T(8,128)(2,1)S(1)} %shard_map.42), channel_id=1, source_target_pairs={{0,8},{12,4},{4,0},{8,12},{1,9},{13,5},{5,1},{9,13},{2,10},{14,6},... | collective-permute-start | bytes 589832 | tf_op jit(solution)/shard_map/ppermute | solution.py:300

commit v3 on v2

v3 whole, which is shorter than its diff:
```python
import functools

import jax
import jax.numpy as jnp
from jax import lax
from jax.experimental import pallas as pl
from jax.experimental.pallas import tpu as pltpu
from jax.sharding import PartitionSpec as P

GROUP = 8
SIDE = 2
PIECES = 4
TAIL = 16
FULL = 32768.0
POWERS = (64, 32, 16, 8, 4, 2)
HEAD = (1, 4)
CUTS = (1, 3)
ADDCOST = [0, 10**10, 10**10]
GATES = {('block', 1): [('block', 0)], ('block', 2): [('near', 0), ('across', 0)], ('passed', 0): [('near', 0)], ('passed', 1): [('passed', 0)], ('received', 2, 0): [('block', 0)]}
MPIECES = (1, 1, 1)
SLICED = True
RESTGATE = ()
ECOST = 1
SPLIT = ()
LASTFINAL = False
RELCOST = [0, 0, 0]
PHON = 80
PARTS = 2
SMALL = 16 * 2**20
LARGE = 50 * 2**20
VMEM = pl.BlockSpec(memory_space=pltpu.VMEM)
HBM = pl.BlockSpec(memory_space=pltpu.HBM)


def pick(me, n, choices):
    out = choices[0]
    for i in range(1, n):
        out = jnp.where(me == i, choices[i], out)
    return out


def phase_rows(me, n_re, phase_ref):
    k_all, e_all = phase_ref.shape[1:]
    e_own, k_own = e_all // n_re, k_all // n_re
    width = GROUP * e_own
    tables = []
    for part in range(2):
        full = phase_ref[part].astype(jnp.float32)
        own = pick(me, n_re, [full[:, r * e_own : (r + 1) * e_own] for r in range(n_re)])
        tables.append(jnp.concatenate([own] * GROUP, 1))
    row = lax.broadcasted_iota(jnp.int32, (k_own * GROUP, width), 0) % GROUP
    column = lax.broadcasted_iota(jnp.int32, (k_own * GROUP, width), 1) // e_own
    spread = []
    for table in tables:
        groups = [table[r * k_own : (r + 1) * k_own] for r in range(n_re)]
        moved = [pick(me, n_re, groups[s:] + groups[:s]) for s in range(n_re)]
        spread.append([
            jnp.where(row == column, jnp.broadcast_to(m[:, None], (k_own, GROUP, width)).reshape(k_own * GROUP, width), 0.0)
            for m in moved
        ])
    cos, sin = spread
    left = jnp.concatenate([x for s in range(n_re) for x in (cos[s], sin[s])], 0)
    right = jnp.concatenate([x for s in range(n_re) for x in (-sin[s], cos[s])], 0)
    return left.astype(jnp.bfloat16), right.astype(jnp.bfloat16)


def electron_kernel(n_re, cuts, mcuts, pieces, start, phase_ref, g_ref, *refs):
    n, m = len(cuts), len(mcuts)
    own_refs, send_refs = refs[:n], refs[n : n + (n_re - 1) * m]
    g_vmem, left_ref, right_ref, sems = ([g_ref] if pieces == 0 else []) + list(refs[n + (n_re - 1) * m :])
    _, rows, e_own, b = g_vmem.shape
    size = rows // max(pieces, 1)
    copies = [
        pltpu.make_async_copy(g_ref.at[:, pl.ds(start + i * size, size)], g_vmem.at[:, pl.ds(i * size, size)], sems.at[i])
        for i in range(pieces)
    ]
    for copy in copies:
        copy.start()
    left_ref[...], right_ref[...] = phase_rows(lax.axis_index("re"), n_re, phase_ref)
    depth = GROUP * e_own
    step = SIDE * GROUP
    largest = jnp.zeros((GROUP, b), jnp.float32)
    for i in range(rows // step):
        if pieces and i * step % size == 0:
            copies[i * step // size].wait()
        groups = [pl.ds(i * step + j * GROUP, GROUP) for j in range(SIDE)]
        real = jnp.concatenate([g_vmem[0, at].reshape(depth, b) for at in groups], 1)
        imag = jnp.concatenate([g_vmem[1, at].reshape(depth, b) for at in groups], 1)
        out = jnp.dot(left_ref[...], real, preferred_element_type=jnp.float32)
        out += jnp.dot(right_ref[...], imag, preferred_element_type=jnp.float32)
        out = out.reshape(n_re, 2, -1, GROUP, SIDE * b)
        if n_re > 1:
            sent = jnp.max(jnp.abs(out[1:].reshape(-1, GROUP, SIDE * b)), 0)
            for j in range(SIDE):
                largest = jnp.maximum(largest, sent[:, j * b : (j + 1) * b])
        for j, at in enumerate(groups):
            first = 0
            for c, kept in enumerate(cuts):
                own_refs[c][:, :, at] = out[0, :, first : first + kept, :, j * b : (j + 1) * b]
                first += kept
            first = 0
            for c, kept in enumerate(mcuts):
                for s in range(1, n_re):
                    for part in range(2):
                        for k in range(kept):
                            row = (part * kept + k) * rows + i * step + j * GROUP
                            send_refs[(s - 1) * m + c][pl.ds(row, GROUP)] = out[s, part, first + k, :, j * b : (j + 1) * b]
                first += kept
    if n_re > 1:
        top = jnp.max(largest, keepdims=True)
        scale, exponent = jnp.ones((1, 1), jnp.float32), jnp.zeros((1, 1), jnp.float32)
        for bit in POWERS:
            fits = top * scale * 2.0**bit <= FULL
            scale = jnp.where(fits, scale * 2.0**bit, scale)
            exponent = jnp.where(fits, exponent + bit, exponent)
        for ref in send_refs:
            last = ref.shape[0] - TAIL
            ref[pl.ds(0, last)] = ref[pl.ds(0, last)] * scale
            ref[pl.ds(last, TAIL)] = jnp.broadcast_to(exponent, (TAIL, b))


def electron_sums(phase, g_wann, n_re, cuts, mcuts, start, rows):
    _, _, e_own, b = g_wann.shape
    k_all = phase.shape[1]
    pieces = 0 if start is None else PIECES if rows % (PIECES * SIDE * GROUP) == 0 else 1
    own = [jax.ShapeDtypeStruct((2, size, rows, b), jnp.float32) for size in cuts]
    send = [jax.ShapeDtypeStruct((2 * size * rows + TAIL, b), jnp.float32) for _ in range(n_re - 1) for size in mcuts]
    outs = pl.pallas_call(
        functools.partial(electron_kernel, n_re, cuts, mcuts, pieces, start),
        in_specs=[VMEM, HBM if pieces else VMEM],
        out_specs=[VMEM] * len(own + send),
        out_shape=own + send,
        scratch_shapes=([pltpu.VMEM((2, rows, e_own, b), g_wann.dtype)] if pieces else [])
        + [
            pltpu.VMEM((2 * k_all * GROUP, GROUP * e_own), jnp.bfloat16),
            pltpu.VMEM((2 * k_all * GROUP, GROUP * e_own), jnp.bfloat16),
            pltpu.SemaphoreType.DMA((max(pieces, 1),)),
        ],
        compiler_params=pltpu.CompilerParams(vmem_limit_bytes=LARGE if pieces else SMALL),
        cost_estimate=pl.CostEstimate(flops=ECOST * 8 * k_all * e_own * rows * b, bytes_accessed=4 * rows * e_own * b, transcendentals=0),
    )(phase, g_wann)
    return outs[: len(cuts)], [outs[len(cuts) + s * len(mcuts) : len(cuts) + (s + 1) * len(mcuts)] for s in range(n_re - 1)]


def add_kernel(pieces, own_ref, *refs):
    out_ref = refs[-1]
    _, kept, rows, _ = own_ref.shape
    totals = {(part, k): own_ref[part, k] for part in range(2) for k in range(kept)}
    for n, ref in enumerate(refs[:-1]):
        exponent = ref[pl.ds(ref.shape[0] - TAIL, 1)]
        factor = jnp.ones_like(exponent)
        for bit in POWERS:
            taken = exponent >= bit
            exponent = jnp.where(taken, exponent - bit, exponent)
            factor = jnp.where(taken, factor * 2.0**-bit, factor)
        size = kept // pieces
        for part in range(2):
            for k in range(size):
                to = part, n % pieces * size + k
                totals[to] = totals[to] + ref[pl.ds((part * size + k) * rows, rows)] * factor
    for to, total in totals.items():
        out_ref[to] = total.astype(out_ref.dtype)


def add_up(own, received, pieces, cost):
    return pl.pallas_call(
        functools.partial(add_kernel, pieces),
        in_specs=[VMEM] * (1 + len(received)),
        out_specs=VMEM,
        out_shape=jax.ShapeDtypeStruct(own.shape, jnp.bfloat16),
        compiler_params=pltpu.CompilerParams(vmem_limit_bytes=SMALL),
        cost_estimate=pl.CostEstimate(flops=cost, bytes_accessed=0, transcendentals=0),
    )(own, *received)


def origin(n, step):
    me = lax.axis_index("pb")
    return me ^ step if n == 4 else (me - step) % n


def relay_kernel(block_ref, far_ref, out_ref):
    me = lax.axis_index("pb")
    middle = (me == 1) | (me == 2)
    for c in range(2):
        out_ref[c] = jnp.where(middle, far_ref[c], block_ref[c])


def relay(block, far, cost):
    return pl.pallas_call(
        relay_kernel,
        in_specs=[VMEM, VMEM],
        out_specs=VMEM,
        out_shape=jax.ShapeDtypeStruct(block.shape, block.dtype),
        compiler_params=pltpu.CompilerParams(vmem_limit_bytes=SMALL),
        cost_estimate=pl.CostEstimate(flops=cost, bytes_accessed=0, transcendentals=0),
    )(block, far)


def after(x, *others):
    return lax.optimization_barrier((x, *others))[0] if others else x


def phonon_part(steps, n_pb, table_ref, refs, first, k, rows=slice(None)):
    total, refs = None, list(refs)
    p_own = table_ref.shape[2] // n_pb
    for n, (step, has_head) in enumerate(steps):
        if p_own % 128:
            at = pl.ds(step * p_own, p_own)
        else:
            at = pl.ds(pl.multiple_of(origin(n_pb, step) * p_own, p_own), p_own)
        head_ref = refs.pop(0) if has_head else None
        rest_ref = refs.pop(0)
        ahead, b = p_own - rest_ref.shape[2], rest_ref.shape[3]
        halves = []
        for c in range(2):
            head = head_ref[c, first + k] if has_head else jnp.zeros((ahead, b), rest_ref.dtype)
            halves.append(jnp.concatenate([head, rest_ref[c, k]], 0))
        real, imag = halves
        part = jnp.dot(table_ref[0, rows, at], jnp.concatenate([real, imag], 1), preferred_element_type=jnp.float32)
        part += jnp.dot(table_ref[1, rows, at], jnp.concatenate([-imag, real], 1), preferred_element_type=jnp.float32)
        total = part if total is None else total + part
    return total


def main_kernel(steps, n_pb, first, table_ref, *refs):
    out_ref = refs[-1]
    for k in range(out_ref.shape[0]):
        out_ref[k] = phonon_part(steps, n_pb, table_ref, refs[:-1], first, k)


def final_kernel(steps, n_pb, first, has_prior, table_ref, acc_ref, *refs):
    out_ref, staged, sems = refs[-3:]
    size, _, q, b = staged.shape
    copies = []
    for k in range(size):
        for h in range(PARTS):
            rows = pl.ds(h * (q // PARTS), q // PARTS)
            total = acc_ref[k, rows] + phonon_part(steps, n_pb, table_ref, refs[: -3 - has_prior], first, k, rows)
            staged[k, 0, rows] = total[:, :b]
            staged[k, 1, rows] = total[:, b:]
            copies.append(pltpu.make_async_copy(staged.at[k, :, rows], out_ref.at[first + k, :, rows], sems.at[k, h]))
            copies[-1].start()
    for copy in copies:
        copy.wait()


def kernel_inputs(blocks):
    steps = [(step, head is not None) for step, head, _ in blocks]
    return steps, [x for _, head, rest in blocks for x in (head, rest) if x is not None]


def phonon_main(n_pb, table, blocks, first):
    steps, flat = kernel_inputs(blocks)
    q = table.shape[1]
    _, size, rows, b = blocks[0][2].shape
    return pl.pallas_call(
        functools.partial(main_kernel, steps, n_pb, first),
        in_specs=[VMEM] * (1 + len(flat)),
        out_specs=VMEM,
        out_shape=jax.ShapeDtypeStruct((size, q, 2 * b), jnp.float32),
        compiler_params=pltpu.CompilerParams(vmem_limit_bytes=SMALL),
        cost_estimate=pl.CostEstimate(flops=PHON * q * rows * len(blocks) * b * size, bytes_accessed=0, transcendentals=0),
    )(table, *flat)


def phonon_final(n_pb, table, acc, blocks, prior, first, k_own):
    steps, flat = kernel_inputs(blocks)
    q = table.shape[1]
    _, size, rows, b = blocks[0][2].shape
    alias = [] if prior is None else [prior]
    return pl.pallas_call(
        functools.partial(final_kernel, steps, n_pb, first, len(alias)),
        in_specs=[VMEM] * (2 + len(flat)) + [HBM] * len(alias),
        out_specs=HBM,
        out_shape=jax.ShapeDtypeStruct((k_own, 2, q, b), jnp.float32),
        scratch_shapes=[pltpu.VMEM((size, 2, q, b), jnp.float32), pltpu.SemaphoreType.DMA((size, PARTS))],
        input_output_aliases={2 + len(flat): 0} if alias else {},
        compiler_params=pltpu.CompilerParams(vmem_limit_bytes=SMALL),
        cost_estimate=pl.CostEstimate(flops=PHON * q * rows * len(blocks) * b * size, bytes_accessed=size * q * b * 8, transcendentals=0),
    )(table, acc, *flat, *alias)


class Transfers:
    def __init__(self, n_re, n_pb, own, send):
        self.n_re, self.n_pb, self.own, self.send = n_re, n_pb, own, send
        self.made = {}

    def get(self, *what):
        if what not in self.made:
            self.made[what] = None
            self.made[what] = getattr(self, what[0])(*what[1:])
        return self.made[what]

    def gated(self, x, *what):
        return after(x, *[self.get(*other) for other in GATES.get(what, [])])

    def received(self, c, piece):
        out = []
        for s in range(1, self.n_re):
            message = self.gated(self.send[s - 1][c][piece].astype(jnp.float16), "received", c, piece)
            got = lax.ppermute(message, "re", [(i, (i + s) % self.n_re) for i in range(self.n_re)])
            out.append(got)
        return out

    def block(self, c):
        pieces = [self.get("received", c, i) for i in range(MPIECES[c])]
        received = [self.gated(got, "block", c).astype(jnp.float32) for several in zip(*pieces) for got in several]
        return add_up(self.own[c], received, MPIECES[c], ADDCOST[c])

    def near(self, c):
        block = self.gated(self.get("block", c), "near", c)
        return lax.ppermute(block, "pb", [(i, i ^ 1) for i in range(self.n_pb)])

    def across(self, c):
        block = self.gated(self.get("block", c), "across", c)
        pairs = [(i, i ^ 3) for i in range(self.n_pb)]
        return lax.ppermute(block, "pb", pairs[1:-1] if c in SPLIT else pairs)

    def ends(self, c):
        block = self.gated(self.get("block", c), "ends", c)
        return lax.ppermute(block, "pb", [(0, 3), (3, 0)])

    def passed(self, c):
        return relay(self.get("block", c), self.gated(self.get("across", c), "passed", c), RELCOST[c])

    def last(self, c):
        return lax.ppermute(self.get("passed", c), "pb", [(0, 2), (3, 1), (1, 0), (2, 3)])

    def shifted(self, c, s):
        return lax.ppermute(self.get("block", c), "pb", [(i, (i + s) % self.n_pb) for i in range(self.n_pb)])

    def main_blocks(self, c):
        if self.n_pb == 4:
            out = [(0, self.get("block", 0), self.get("block", c)), (1, self.get("near", 0), self.get("near", c))]
            if c in SPLIT:
                if LASTFINAL:
                    return out + [(3, None, self.get("across", c))]
                return out + [(2, self.get("last", 0), self.get("last", c)), (3, None, self.get("across", c))]
            return out + [(3, self.get("across", 0), self.get("across", c))]
        return [(s, self.shifted(0, s), self.shifted(c, s)) if s else (0, self.get("block", 0), self.get("block", c)) for s in range(self.n_pb - 1)]

    def final_blocks(self, c):
        if self.n_pb == 4:
            if c in SPLIT:
                out = [(2, self.get("last", 0), self.get("last", c))] if LASTFINAL else []
                return out + [(3, self.get("across", 0), self.get("ends", c))]
            return [(2, self.get("last", 0), self.get("last", c))]
        s = self.n_pb - 1
        return [(s, self.shifted(0, s), self.shifted(c, s))]

    def acc(self, c):
        return phonon_main(self.n_pb, self.table, self.get("main_blocks", c), self.firsts[c])


def body(n_re, n_pb, g_wann, phonon_phase, electron_phase):
    k_own = electron_phase.shape[1] // n_re
    p_own = g_wann.shape[1]
    cuts = [k_own * c // sum(CUTS) for c in CUTS]
    ahead = p_own * HEAD[0] // HEAD[1] // (2 * GROUP) * (2 * GROUP)
    if SLICED:
        own, send = electron_sums(electron_phase, g_wann[:, :ahead], n_re, [k_own], [k_own], None, ahead)
    else:
        own, send = electron_sums(electron_phase, g_wann, n_re, [k_own], [k_own], 0, ahead)
    table = phonon_phase
    if p_own % 128 != 0:
        order = jnp.stack([origin(n_pb, step) for step in range(n_pb)])
        table = table.reshape(2, -1, n_pb, p_own)[:, :, order].reshape(table.shape)
    transfers = Transfers(n_re, n_pb, own, [[a] for a in send])
    mcuts = [size // MPIECES[1 + c] for c, size in enumerate(cuts) for _ in range(MPIECES[1 + c])]
    rest = electron_sums(after(electron_phase, transfers.get(*RESTGATE) if RESTGATE else own[0]), g_wann, n_re, cuts, mcuts, ahead, p_own - ahead)
    at = [sum(MPIECES[1 : 1 + c]) for c in range(len(cuts) + 1)]
    transfers.own = own + rest[0]
    transfers.send = [[a] + [b[at[c] : at[c + 1]] for c in range(len(cuts))] for a, b in zip(send, rest[1])]
    transfers.table = table
    transfers.firsts = [None] + [sum(cuts[:c]) for c in range(len(cuts))]
    result = None
    for c in range(1, 1 + len(cuts)):
        acc = transfers.get("acc", c)
        result = phonon_final(n_pb, table, acc, transfers.get("final_blocks", c), result, transfers.firsts[c], k_own)
    return result


def solution(mesh):
    return jax.shard_map(
        functools.partial(body, mesh.shape["re"], mesh.shape["pb"]),
        mesh=mesh,
        in_specs=(P(None, "pb", ("grp", "re"), "ka"), P(None, "pb", None), P()),
        out_specs=P(("grp", "re"), None, "pb", "ka"),
        check_vma=False,
    )
```

time: 50.5 us -> 48.5 us (0.960)
  starting transfers between devices: 36.9 us -> 21.4 us
  waiting for transfers between devices: 2.89 us -> 17.3 us
  Pallas kernels: 9.6 us -> 8.11 us
  local copies, waits for them, and re-layouts: 0.69 us -> 1.32 us
    ppermute x6, waiting for transfers between devices: 1.93 us -> 12.4 us  [the longest x3 10.3 us: last(): lax.ppermute(self.get('passed', c), 'pb', [(0, 2), (3, 1), (1, 0), (2, 3)])]
    ppermute x3, starting transfers between devices: 9.81 us -> 1.11 us  [near(): return lax.ppermute(block, 'pb', [(i, i ^ 1) for i in range(self.n_pb)])]
    ppermute x6, starting transfers between devices: 21.7 us -> 15.6 us  [the longest x3 9.88 us: across(): return lax.ppermute(block, 'pb', pairs[1:-1] if c in SPLIT else pairs)]
    ppermute x3, waiting for transfers between devices: 0.01 us -> 3.99 us  [near(): return lax.ppermute(block, 'pb', [(i, i ^ 1) for i in range(self.n_pb)])]
    pallas_call x8 -> x9, Pallas kernels: 9.45 us -> 7.96 us  [the longest x2 3.19 us: electron_sums(): pl.pallas_call(functools.partial(electron_kernel, n_re, cuts, mcuts, piec...]
    slice x0 -> x1, local copies, waits for them, and re-layouts: none -> 1.31 us  [body(): g_wann[:, :ahead]]
    ppermute x3, starting transfers between devices: 5.35 us -> 4.65 us  [received(): lax.ppermute(message, 're', [(i, (i + s) % self.n_re) for i in range(self...]
    unnamed x4, local copies, waits for them, and re-layouts: 0.69 us -> 0.01 us
  transfers between devices with their start and end apart: 12 -> 12, of which waited for: 3 -> 6; matrix products, arithmetic and copies ran while one was open for 0% -> 0% of each run, Pallas kernels for 12% -> 12%
where the time goes in v3:
time: 48.5 us; the launch traced here: 48.4 us
  starting transfers between devices  21.4 us (44%)
  waiting for transfers between devices  17.3 us (36%)
  Pallas kernels  8.11 us (17%)
  local copies, waits for them, and re-layouts  1.32 us (3%)
    ppermute x3, waiting for transfers between devices, last(): lax.ppermute(self.get('passed', c), 'pb', [(0, 2), (3, 1), (1, 0), (2, 3)])  10.3 us
    ppermute x3, starting transfers between devices, across(): return lax.ppermute(block, 'pb', pairs[1:-1] if c in SPLIT else pairs)  9.88 us
    ppermute x3, starting transfers between devices, last(): lax.ppermute(self.get('passed', c), 'pb', [(0, 2), (3, 1), (1, 0), (2, 3)])  5.77 us
    ppermute x3, starting transfers between devices, received(): lax.ppermute(message, 're', [(i, (i + s) % self.n_re) for i in range(self...  4.65 us
    ppermute x3, waiting for transfers between devices, near(): return lax.ppermute(block, 'pb', [(i, i ^ 1) for i in range(self.n_pb)])  3.99 us
    pallas_call x2, Pallas kernels, electron_sums(): pl.pallas_call(functools.partial(electron_kernel, n_re, cuts, mcuts, piec...  3.19 us
    pallas_call x2, Pallas kernels, phonon_final(): pl.pallas_call(functools.partial(final_kernel, steps, n_pb, first, len(al...  2.63 us
    ppermute x3, waiting for transfers between devices, across(): return lax.ppermute(block, 'pb', pairs[1:-1] if c in SPLIT else pairs)  2.18 us
  transfers between devices with their start and end apart: 12, of which 6 were waited for; matrix products, arithmetic and copies ran while one was open for 0% of the time, Pallas kernels for 12%

profile of v3, /device:TPU:0, one launch (start us, length us, event | category | flops | bytes accessed | tf_op | source)
XLA Modules:
  0.0 48.4 jit_solution(16565639086140551123)
XLA Ops:
  0.0 1.3 %slice.3.g_ref = bf16[2,64,32,128]{3,2,1,0:T(8,128)(2,1)S(1)} slice(bf16[2,256,32,128]{3,2,1,0:T(8,128)(2,1)} %g_ref.1), slice={[0:2], [0:64], [0:32], [0:128]} | slice | bytes 2097152 | tf_op jit(solution)/shard_map/slice | solution.py:361
  1.3 0.6 %shard_map.37 = (f32[2,4,64,128]{3,2,1,0:T(8,128)S(1)}, f32[528,128]{1,0:T(8,128)S(1)}) custom-call(bf16[2,8,64]{2,1,0:T(8,128)(2,1)S(1)} %copy-done.1, bf16[2,64,32,128]{3,2,1,0:T(8,128)(2,1)S(1)} %slice.3.g_ref), custom_call_target="tpu_custom_call" | custom-call | flops 16777216 | bytes 1048576 | tf_op jit(solution)/shard_map/pallas_call | solution.py:128
  2.0 3.0 %collective-permute-start = (f16[528,128]{1,0:T(8,128)(2,1)S(1)}, f16[528,128]{1,0:T(8,128)(2,1)S(1)}, u32[]{:S(2)}, u32[]{:S(2)}) collective-permute-start(f16[528,128]{1,0:T(8,128)(2,1)S(1)} %convert_element_type.18), channel_id=1, source_target_pairs={{0,2},{2,0},{1,3},{3,1},{4,6},{6,4},{5,7},{7,5},{8,10},{10,8},{9,1... | collective-permute-start | bytes 405512 | tf_op jit(solution)/shard_map/ppermute | solution.py:301
  5.0 2.6 %shard_map.39 = (f32[2,1,192,128]{3,2,1,0:T(8,128)S(1)}, f32[2,3,192,128]{3,2,1,0:T(8,128)S(1)}, f32[400,128]{1,0:T(8,128)S(1)}, f32[1168,128]{1,0:T(8,128)S(1)}) custom-call(bf16[2,8,64]{2,1,0:T(8,128)(2,1)S(1)} %copy-done.1, bf16[2,256,32,128]{3,2,1,0:T(8,128)(2,1)} %g_ref.1), custom_call_target="tpu_custom_call" | custom-call | flops 50331648 | bytes 3145728 | tf_op jit(solution)/shard_map/pallas_call | solution.py:128
  7.6 0.1 collective-permute-start.8
  7.7 0.8 %collective-permute-done = f16[528,128]{1,0:T(8,128)(2,1)S(1)} collective-permute-done((f16[528,128]{1,0:T(8,128)(2,1)S(1)}, f16[528,128]{1,0:T(8,128)(2,1)S(1)}, u32[]{:S(2)}, u32[]{:S(2)}) %collective-permute-start) | collective-permute-done | bytes 135200 | tf_op jit(solution)/shard_map/ppermute | solution.py:301
  8.6 3.9 %collective-permute-start.3 = (bf16[2,4,64,128]{3,2,1,0:T(8,128)(2,1)S(1)}, bf16[2,4,64,128]{3,2,1,0:T(8,128)(2,1)S(1)}, u32[]{:S(2)}, u32[]{:S(2)}) collective-permute-start(bf16[2,4,64,128]{3,2,1,0:T(8,128)(2,1)S(1)} %shard_map.38.refs_0_.block_ref), channel_id=1, source_target_pairs={{0,12},{4,8},{8,4},{12,0},{1,13},{5,9},{9,5},{13,1},{2,14},{6,10},... | collective-permute-start | bytes 393224 | tf_op jit(solution)/shard_map/ppermute | solution.py:317
  12.6 1.6 %collective-permute-start.1 = (f16[1168,128]{1,0:T(8,128)(2,1)S(1)}, f16[1168,128]{1,0:T(8,128)(2,1)S(1)}, u32[]{:S(2)}, u32[]{:S(2)}) collective-permute-start(f16[1168,128]{1,0:T(8,128)(2,1)S(1)} %convert_element_type.20), channel_id=1, source_target_pairs={{0,2},{2,0},{1,3},{3,1},{4,6},{6,4},{5,7},{7,5},{8,10},{10,8},{9,1... | collective-permute-start | bytes 897032 | tf_op jit(solution)/shard_map/ppermute | solution.py:301
  14.1 2.5 %collective-permute-start.10 = (bf16[2,1,192,128]{3,2,1,0:T(8,128)(2,1)S(1)}, bf16[2,1,192,128]{3,2,1,0:T(8,128)(2,1)S(1)}, u32[]{:S(2)}, u32[]{:S(2)}) collective-permute-start(bf16[2,1,192,128]{3,2,1,0:T(8,128)(2,1)S(1)} %shard_map.44.refs_1_.block_ref), channel_id=1, source_target_pairs={{0,12},{4,8},{8,4},{12,0},{1,13},{5,9},{9,5},{13,1},{2,14},{6,10},... | collective-permute-start | bytes 294920 | tf_op jit(solution)/shard_map/ppermute | solution.py:317
  16.6 4.0 %collective-permute-done.2.refs_2_ = bf16[2,4,64,128]{3,2,1,0:T(8,128)(2,1)S(1)} collective-permute-done((bf16[2,4,64,128]{3,2,1,0:T(8,128)(2,1)S(1)}, bf16[2,4,64,128]{3,2,1,0:T(8,128)(2,1)S(1)}, u32[]{:S(2)}, u32[]{:S(2)}) %collective-permute-start.2) | collective-permute-done | bytes 131104 | tf_op jit(solution)/shard_map/ppermute | solution.py:312
  20.7 0.7 %collective-permute-start.6 = (bf16[2,4,64,128]{3,2,1,0:T(8,128)(2,1)S(1)}, bf16[2,4,64,128]{3,2,1,0:T(8,128)(2,1)S(1)}, u32[]{:S(2)}, u32[]{:S(2)}) collective-permute-start(bf16[2,4,64,128]{3,2,1,0:T(8,128)(2,1)S(1)} %shard_map.42), channel_id=1, source_target_pairs={{0,8},{12,4},{4,0},{8,12},{1,9},{13,5},{5,1},{9,13},{2,10},{14,6},... | collective-permute-start | bytes 393224 | tf_op jit(solution)/shard_map/ppermute | solution.py:327
  21.4 0.3 collective-permute-done.10.refs_5_.far_ref
  21.7 0.7 %collective-permute-start.11 = (bf16[2,1,192,128]{3,2,1,0:T(8,128)(2,1)S(1)}, bf16[2,1,192,128]{3,2,1,0:T(8,128)(2,1)S(1)}, u32[]{:S(2)}, u32[]{:S(2)}) collective-permute-start(bf16[2,1,192,128]{3,2,1,0:T(8,128)(2,1)S(1)} %shard_map.46), channel_id=1, source_target_pairs={{0,8},{12,4},{4,0},{8,12},{1,9},{13,5},{5,1},{9,13},{2,10},{14,6},... | collective-permute-start | bytes 294920 | tf_op jit(solution)/shard_map/ppermute | solution.py:327
  22.5 0.1 shard_map.40.refs_1_.block_ref
  22.6 3.5 %collective-permute-start.5 = (bf16[2,3,192,128]{3,2,1,0:T(8,128)(2,1)S(1)}, bf16[2,3,192,128]{3,2,1,0:T(8,128)(2,1)S(1)}, u32[]{:S(2)}, u32[]{:S(2)}) collective-permute-start(bf16[2,3,192,128]{3,2,1,0:T(8,128)(2,1)S(1)} %shard_map.40.refs_1_.block_ref), channel_id=1, source_target_pairs={{0,12},{4,8},{8,4},{12,0},{1,13},{5,9},{9,5},{13,1},{2,14},{6,10},... | collective-permute-start | bytes 884744 | tf_op jit(solution)/shard_map/ppermute | solution.py:317
  26.1 1.1 %collective-permute-start.4 = (bf16[2,3,192,128]{3,2,1,0:T(8,128)(2,1)S(1)}, bf16[2,3,192,128]{3,2,1,0:T(8,128)(2,1)S(1)}, u32[]{:S(2)}, u32[]{:S(2)}) collective-permute-start(bf16[2,3,192,128]{3,2,1,0:T(8,128)(2,1)S(1)} %shard_map.40.refs_1_.block_ref), channel_id=1, source_target_pairs={{0,4},{4,0},{8,12},{12,8},{1,5},{5,1},{9,13},{13,9},{2,6},{6,2},{1... | collective-permute-start | bytes 884744 | tf_op jit(solution)/shard_map/ppermute | solution.py:312
  27.2 0.6 %shard_map.45.acc_ref = f32[1,512,256]{2,1,0:T(8,128)S(1)} custom-call(bf16[2,512,1024]{2,1,0:T(8,128)(2,1)S(1)} %copy-done, bf16[2,4,64,128]{3,2,1,0:T(8,128)(2,1)S(1)} %shard_map.38.refs_0_.block_ref, bf16[2,1,192,128]{3,2,1,0:T(8,128)(2,1)S(1)} %shard_map.44.refs_1_.block_ref, bf16[2,4,64,128]{3,2,1,0:T(8,128)(2,1)S(1)} %collective-permute-done.2.refs_2_, ...), custom_call_target="tpu_custom_call" | custom-call | flops 3019898880 | tf_op jit(solution)/shard_map/pallas_call | solution.py:256
  27.8 6.3 %collective-permute-done.11.refs_1_ = bf16[2,1,192,128]{3,2,1,0:T(8,128)(2,1)S(1)} collective-permute-done((bf16[2,1,192,128]{3,2,1,0:T(8,128)(2,1)S(1)}, bf16[2,1,192,128]{3,2,1,0:T(8,128)(2,1)S(1)}, u32[]{:S(2)}, u32[]{:S(2)}) %collective-permute-start.11) | collective-permute-done | bytes 98336 | tf_op jit(solution)/shard_map/ppermute | solution.py:327
  34.1 1.1 %shard_map.47.refs_2_ = f32[4,2,512,128]{3,2,1,0:T(8,128)} custom-call(bf16[2,512,1024]{2,1,0:T(8,128)(2,1)S(1)} %copy-done, f32[1,512,256]{2,1,0:T(8,128)S(1)} %shard_map.45.acc_ref, bf16[2,4,64,128]{3,2,1,0:T(8,128)(2,1)S(1)} %collective-permute-done.6.refs_0_, bf16[2,1,192,128]{3,2,1,0:T(8,128)(2,1)S(1)} %collective-permute-done.11.refs_1_), custom_call_target="tpu_custom_call" | custom-call | flops 1006632960 | bytes 524288 | tf_op jit(solution)/shard_map/pallas_call | solution.py:271
  35.2 1.9 %collective-permute-done.5.refs_5_.far_ref = bf16[2,3,192,128]{3,2,1,0:T(8,128)(2,1)S(1)} collective-permute-done((bf16[2,3,192,128]{3,2,1,0:T(8,128)(2,1)S(1)}, bf16[2,3,192,128]{3,2,1,0:T(8,128)(2,1)S(1)}, u32[]{:S(2)}, u32[]{:S(2)}) %collective-permute-start.5) | collective-permute-done | bytes 294944 | tf_op jit(solution)/shard_map/ppermute | solution.py:317
  37.2 4.3 %collective-permute-start.7 = (bf16[2,3,192,128]{3,2,1,0:T(8,128)(2,1)S(1)}, bf16[2,3,192,128]{3,2,1,0:T(8,128)(2,1)S(1)}, u32[]{:S(2)}, u32[]{:S(2)}) collective-permute-start(bf16[2,3,192,128]{3,2,1,0:T(8,128)(2,1)S(1)} %shard_map.43), channel_id=1, source_target_pairs={{0,8},{12,4},{4,0},{8,12},{1,9},{13,5},{5,1},{9,13},{2,10},{14,6},... | collective-permute-start | bytes 884744 | tf_op jit(solution)/shard_map/ppermute | solution.py:327
  41.5 1.4 %shard_map.41.acc_ref = f32[3,512,256]{2,1,0:T(8,128)S(1)} custom-call(bf16[2,512,1024]{2,1,0:T(8,128)(2,1)S(1)} %copy-done, bf16[2,4,64,128]{3,2,1,0:T(8,128)(2,1)S(1)} %shard_map.38.refs_0_.block_ref, bf16[2,3,192,128]{3,2,1,0:T(8,128)(2,1)S(1)} %shard_map.40.refs_1_.block_ref, bf16[2,4,64,128]{3,2,1,0:T(8,128)(2,1)S(1)} %collective-permute-done.2.refs_2_, ...), custom_call_target="tpu_custom_call" | custom-call | flops 9059696640 | tf_op jit(solution)/shard_map/pallas_call | solution.py:256
  42.9 4.0 %collective-permute-done.7.refs_1_ = bf16[2,3,192,128]{3,2,1,0:T(8,128)(2,1)S(1)} collective-permute-done((bf16[2,3,192,128]{3,2,1,0:T(8,128)(2,1)S(1)}, bf16[2,3,192,128]{3,2,1,0:T(8,128)(2,1)S(1)}, u32[]{:S(2)}, u32[]{:S(2)}) %collective-permute-start.7) | collective-permute-done | bytes 294944 | tf_op jit(solution)/shard_map/ppermute | solution.py:327
  46.9 1.5 %shard_map.48 = f32[4,2,512,128]{3,2,1,0:T(8,128)} custom-call(bf16[2,512,1024]{2,1,0:T(8,128)(2,1)S(1)} %copy-done, f32[3,512,256]{2,1,0:T(8,128)S(1)} %shard_map.41.acc_ref, bf16[2,4,64,128]{3,2,1,0:T(8,128)(2,1)S(1)} %collective-permute-done.6.refs_0_, ...), custom_call_target="tpu_custom_call", output_to_operand_aliasing={{}: (4, {})} | custom-call | flops 3019898880 | bytes 1572864 | tf_op jit(solution)/shard_map/pallas_call | solution.py:271
  (23 shorter events, 0.4 us)
Async XLA Ops:
  0.0 1.3 %copy-start.1 = (bf16[2,8,64]{2,1,0:T(8,128)(2,1)S(1)}, bf16[2,8,64]{2,1,0:T(8,128)(2,1)}, u32[]{:S(2)}) copy-start(bf16[2,8,64]{2,1,0:T(8,128)(2,1)} %phase_ref.2) | copy-start | bytes 6148
  2.0 6.6 %collective-permute-start = (f16[528,128]{1,0:T(8,128)(2,1)S(1)}, f16[528,128]{1,0:T(8,128)(2,1)S(1)}, u32[]{:S(2)}, u32[]{:S(2)}) collective-permute-start(f16[528,128]{1,0:T(8,128)(2,1)S(1)} %convert_element_type.18), channel_id=1, source_target_pairs={{0,2},{2,0},{1,3},{3,1},{4,6},{6,4},{5,7},{7,5},{8,10},{10,8},{9,1... | collective-permute-start | bytes 405512 | tf_op jit(solution)/shard_map/ppermute | solution.py:301
  7.6 4.9 %collective-permute-start.8 = (f16[400,128]{1,0:T(8,128)(2,1)S(1)}, f16[400,128]{1,0:T(8,128)(2,1)S(1)}, u32[]{:S(2)}, u32[]{:S(2)}) collective-permute-start(f16[400,128]{1,0:T(8,128)(2,1)S(1)} %convert_element_type.22), channel_id=1, source_target_pairs={{0,2},{2,0},{1,3},{3,1},{4,6},{6,4},{5,7},{7,5},{8,10},{10,8},{9,1... | collective-permute-start | bytes 307208 | tf_op jit(solution)/shard_map/ppermute | solution.py:301
  8.6 8.0 %collective-permute-start.3 = (bf16[2,4,64,128]{3,2,1,0:T(8,128)(2,1)S(1)}, bf16[2,4,64,128]{3,2,1,0:T(8,128)(2,1)S(1)}, u32[]{:S(2)}, u32[]{:S(2)}) collective-permute-start(bf16[2,4,64,128]{3,2,1,0:T(8,128)(2,1)S(1)} %shard_map.38.refs_0_.block_ref), channel_id=1, source_target_pairs={{0,12},{4,8},{8,4},{12,0},{1,13},{5,9},{9,5},{13,1},{2,14},{6,10},... | collective-permute-start | bytes 393224 | tf_op jit(solution)/shard_map/ppermute | solution.py:317
  12.5 8.1 %collective-permute-start.2 = (bf16[2,4,64,128]{3,2,1,0:T(8,128)(2,1)S(1)}, bf16[2,4,64,128]{3,2,1,0:T(8,128)(2,1)S(1)}, u32[]{:S(2)}, u32[]{:S(2)}) collective-permute-start(bf16[2,4,64,128]{3,2,1,0:T(8,128)(2,1)S(1)} %shard_map.38.refs_0_.block_ref), channel_id=1, source_target_pairs={{0,4},{4,0},{8,12},{12,8},{1,5},{5,1},{9,13},{13,9},{2,6},{6,2},{1... | collective-permute-start | bytes 393224 | tf_op jit(solution)/shard_map/ppermute | solution.py:312
  12.6 9.9 %collective-permute-start.1 = (f16[1168,128]{1,0:T(8,128)(2,1)S(1)}, f16[1168,128]{1,0:T(8,128)(2,1)S(1)}, u32[]{:S(2)}, u32[]{:S(2)}) collective-permute-start(f16[1168,128]{1,0:T(8,128)(2,1)S(1)} %convert_element_type.20), channel_id=1, source_target_pairs={{0,2},{2,0},{1,3},{3,1},{4,6},{6,4},{5,7},{7,5},{8,10},{10,8},{9,1... | collective-permute-start | bytes 897032 | tf_op jit(solution)/shard_map/ppermute | solution.py:301
  14.1 7.5 %collective-permute-start.10 = (bf16[2,1,192,128]{3,2,1,0:T(8,128)(2,1)S(1)}, bf16[2,1,192,128]{3,2,1,0:T(8,128)(2,1)S(1)}, u32[]{:S(2)}, u32[]{:S(2)}) collective-permute-start(bf16[2,1,192,128]{3,2,1,0:T(8,128)(2,1)S(1)} %shard_map.44.refs_1_.block_ref), channel_id=1, source_target_pairs={{0,12},{4,8},{8,4},{12,0},{1,13},{5,9},{9,5},{13,1},{2,14},{6,10},... | collective-permute-start | bytes 294920 | tf_op jit(solution)/shard_map/ppermute | solution.py:317
  16.6 10.5 %collective-permute-start.9 = (bf16[2,1,192,128]{3,2,1,0:T(8,128)(2,1)S(1)}, bf16[2,1,192,128]{3,2,1,0:T(8,128)(2,1)S(1)}, u32[]{:S(2)}, u32[]{:S(2)}) collective-permute-start(bf16[2,1,192,128]{3,2,1,0:T(8,128)(2,1)S(1)} %shard_map.44.refs_1_.block_ref), channel_id=1, source_target_pairs={{0,4},{4,0},{8,12},{12,8},{1,5},{5,1},{9,13},{13,9},{2,6},{6,2},{1... | collective-permute-start | bytes 294920 | tf_op jit(solution)/shard_map/ppermute | solution.py:312
  20.7 13.4 %collective-permute-start.6 = (bf16[2,4,64,128]{3,2,1,0:T(8,128)(2,1)S(1)}, bf16[2,4,64,128]{3,2,1,0:T(8,128)(2,1)S(1)}, u32[]{:S(2)}, u32[]{:S(2)}) collective-permute-start(bf16[2,4,64,128]{3,2,1,0:T(8,128)(2,1)S(1)} %shard_map.42), channel_id=1, source_target_pairs={{0,8},{12,4},{4,0},{8,12},{1,9},{13,5},{5,1},{9,13},{2,10},{14,6},... | collective-permute-start | bytes 393224 | tf_op jit(solution)/shard_map/ppermute | solution.py:327
  21.7 12.4 %collective-permute-start.11 = (bf16[2,1,192,128]{3,2,1,0:T(8,128)(2,1)S(1)}, bf16[2,1,192,128]{3,2,1,0:T(8,128)(2,1)S(1)}, u32[]{:S(2)}, u32[]{:S(2)}) collective-permute-start(bf16[2,1,192,128]{3,2,1,0:T(8,128)(2,1)S(1)} %shard_map.46), channel_id=1, source_target_pairs={{0,8},{12,4},{4,0},{8,12},{1,9},{13,5},{5,1},{9,13},{2,10},{14,6},... | collective-permute-start | bytes 294920 | tf_op jit(solution)/shard_map/ppermute | solution.py:327
  22.5 4.7 %copy-start = (bf16[2,512,1024]{2,1,0:T(8,128)(2,1)S(1)}, bf16[2,512,1024]{2,1,0:T(8,128)(2,1)}, u32[]{:S(2)}) copy-start(bf16[2,512,1024]{2,1,0:T(8,128)(2,1)} %table_ref.7) | copy-start | bytes 6291460
  22.6 14.5 %collective-permute-start.5 = (bf16[2,3,192,128]{3,2,1,0:T(8,128)(2,1)S(1)}, bf16[2,3,192,128]{3,2,1,0:T(8,128)(2,1)S(1)}, u32[]{:S(2)}, u32[]{:S(2)}) collective-permute-start(bf16[2,3,192,128]{3,2,1,0:T(8,128)(2,1)S(1)} %shard_map.40.refs_1_.block_ref), channel_id=1, source_target_pairs={{0,12},{4,8},{8,4},{12,0},{1,13},{5,9},{9,5},{13,1},{2,14},{6,10},... | collective-permute-start | bytes 884744 | tf_op jit(solution)/shard_map/ppermute | solution.py:317
  26.1 15.4 %collective-permute-start.4 = (bf16[2,3,192,128]{3,2,1,0:T(8,128)(2,1)S(1)}, bf16[2,3,192,128]{3,2,1,0:T(8,128)(2,1)S(1)}, u32[]{:S(2)}, u32[]{:S(2)}) collective-permute-start(bf16[2,3,192,128]{3,2,1,0:T(8,128)(2,1)S(1)} %shard_map.40.refs_1_.block_ref), channel_id=1, source_target_pairs={{0,4},{4,0},{8,12},{12,8},{1,5},{5,1},{9,13},{13,9},{2,6},{6,2},{1... | collective-permute-start | bytes 884744 | tf_op jit(solution)/shard_map/ppermute | solution.py:312
  37.2 9.7 %collective-permute-start.7 = (bf16[2,3,192,128]{3,2,1,0:T(8,128)(2,1)S(1)}, bf16[2,3,192,128]{3,2,1,0:T(8,128)(2,1)S(1)}, u32[]{:S(2)}, u32[]{:S(2)}) collective-permute-start(bf16[2,3,192,128]{3,2,1,0:T(8,128)(2,1)S(1)} %shard_map.43), channel_id=1, source_target_pairs={{0,8},{12,4},{4,0},{8,12},{1,9},{13,5},{5,1},{9,13},{2,10},{14,6},... | collective-permute-start | bytes 884744 | tf_op jit(solution)/shard_map/ppermute | solution.py:327

commit v4 on v3

--- a/solution.py
+++ b/solution.py
@@ -14,16 +14,18 @@
 FULL = 32768.0
 POWERS = (64, 32, 16, 8, 4, 2)
 HEAD = (1, 4)
-CUTS = (1, 3)
-ADDCOST = [0, 10**10, 10**10]
-GATES = {('block', 1): [('block', 0)], ('block', 2): [('near', 0), ('across', 0)], ('passed', 0): [('near', 0)], ('passed', 1): [('passed', 0)], ('received', 2, 0): [('block', 0)]}
-MPIECES = (1, 1, 1)
-SLICED = True
-RESTGATE = ()
-ECOST = 1
-SPLIT = ()
-LASTFINAL = False
-RELCOST = [0, 0, 0]
+CUTS = (1, 1, 2)
+ADDCOST = (0, 10**10, 10**10, 10**10)
+GATES = {
+    ("received", 2): [("block", 0)],
+    ("block", 1): [("block", 0)],
+    ("block", 2): [("near", 0), ("across", 0)],
+    ("block", 3): [("near", 0), ("across", 0)],
+    ("passed", 1): [("passed", 0), ("block", 3)],
+    ("passed", 2): [("passed", 1)],
+    ("passed", 3): [("passed", 2)],
+}
+MCUTS = (1, 3)
 PHON = 80
 PARTS = 2
 SMALL = 16 * 2**20
@@ -137,34 +139,33 @@
             pltpu.SemaphoreType.DMA((max(pieces, 1),)),
         ],
         compiler_params=pltpu.CompilerParams(vmem_limit_bytes=LARGE if pieces else SMALL),
-        cost_estimate=pl.CostEstimate(flops=ECOST * 8 * k_all * e_own * rows * b, bytes_accessed=4 * rows * e_own * b, transcendentals=0),
+        cost_estimate=pl.CostEstimate(flops=8 * k_all * e_own * rows * b, bytes_accessed=4 * rows * e_own * b, transcendentals=0),
     )(phase, g_wann)
     return outs[: len(cuts)], [outs[len(cuts) + s * len(mcuts) : len(cuts) + (s + 1) * len(mcuts)] for s in range(n_re - 1)]
 
 
-def add_kernel(pieces, own_ref, *refs):
+def add_kernel(first, own_ref, *refs):
     out_ref = refs[-1]
     _, kept, rows, _ = own_ref.shape
     totals = {(part, k): own_ref[part, k] for part in range(2) for k in range(kept)}
-    for n, ref in enumerate(refs[:-1]):
+    for ref in refs[:-1]:
         exponent = ref[pl.ds(ref.shape[0] - TAIL, 1)]
         factor = jnp.ones_like(exponent)
         for bit in POWERS:
             taken = exponent >= bit
             exponent = jnp.where(taken, exponent - bit, exponent)
             factor = jnp.where(taken, factor * 2.0**-bit, factor)
-        size = kept // pieces
-        for part in range(2):
-            for k in range(size):
-                to = part, n % pieces * size + k
-                totals[to] = totals[to] + ref[pl.ds((part * size + k) * rows, rows)] * factor
+        carried = (ref.shape[0] - TAIL) // (2 * rows)
+        for part, k in totals:
+            at = pl.ds((part * carried + first + k) * rows, rows)
+            totals[part, k] = totals[part, k] + ref[at] * factor
     for to, total in totals.items():
         out_ref[to] = total.astype(out_ref.dtype)
 
 
-def add_up(own, received, pieces, cost):
+def add_up(own, received, first, cost):
     return pl.pallas_call(
-        functools.partial(add_kernel, pieces),
+        functools.partial(add_kernel, first),
         in_specs=[VMEM] * (1 + len(received)),
         out_specs=VMEM,
         out_shape=jax.ShapeDtypeStruct(own.shape, jnp.bfloat16),
@@ -185,14 +186,14 @@
         out_ref[c] = jnp.where(middle, far_ref[c], block_ref[c])
 
 
-def relay(block, far, cost):
+def relay(block, far):
     return pl.pallas_call(
         relay_kernel,
         in_specs=[VMEM, VMEM],
         out_specs=VMEM,
         out_shape=jax.ShapeDtypeStruct(block.shape, block.dtype),
         compiler_params=pltpu.CompilerParams(vmem_limit_bytes=SMALL),
-        cost_estimate=pl.CostEstimate(flops=cost, bytes_accessed=0, transcendentals=0),
+        cost_estimate=pl.CostEstimate(flops=0, bytes_accessed=0, transcendentals=0),
     )(block, far)
 
 
@@ -201,21 +202,14 @@
 
 
 def phonon_part(steps, n_pb, table_ref, refs, first, k, rows=slice(None)):
-    total, refs = None, list(refs)
+    total = None
     p_own = table_ref.shape[2] // n_pb
-    for n, (step, has_head) in enumerate(steps):
+    for step, head_ref, rest_ref in zip(steps, refs[::2], refs[1::2]):
         if p_own % 128:
             at = pl.ds(step * p_own, p_own)
         else:
             at = pl.ds(pl.multiple_of(origin(n_pb, step) * p_own, p_own), p_own)
-        head_ref = refs.pop(0) if has_head else None
-        rest_ref = refs.pop(0)
-        ahead, b = p_own - rest_ref.shape[2], rest_ref.shape[3]
-        halves = []
-        for c in range(2):
-            head = head_ref[c, first + k] if has_head else jnp.zeros((ahead, b), rest_ref.dtype)
-            halves.append(jnp.concatenate([head, rest_ref[c, k]], 0))
-        real, imag = halves
+        real, imag = [jnp.concatenate([head_ref[c, first + k], rest_ref[c, k]], 0) for c in range(2)]
         part = jnp.dot(table_ref[0, rows, at], jnp.concatenate([real, imag], 1), preferred_element_type=jnp.float32)
         part += jnp.dot(table_ref[1, rows, at], jnp.concatenate([-imag, real], 1), preferred_element_type=jnp.float32)
         total = part if total is None else total + part
@@ -245,8 +239,7 @@
 
 
 def kernel_inputs(blocks):
-    steps = [(step, head is not None) for step, head, _ in blocks]
-    return steps, [x for _, head, rest in blocks for x in (head, rest) if x is not None]
+    return [step for step, _, _ in blocks], [x for _, head, rest in blocks for x in (head, rest)]
 
 
 def phonon_main(n_pb, table, blocks, first):
@@ -284,6 +277,7 @@
     def __init__(self, n_re, n_pb, own, send):
         self.n_re, self.n_pb, self.own, self.send = n_re, n_pb, own, send
         self.made = {}
+        self.steps = (0, 1, 3, 2) if n_pb == 4 else tuple(range(n_pb))
 
     def get(self, *what):
         if what not in self.made:
@@ -292,20 +286,20 @@
         return self.made[what]
 
     def gated(self, x, *what):
-        return after(x, *[self.get(*other) for other in GATES.get(what, [])])
-
-    def received(self, c, piece):
+        gates = GATES.get(what, []) if self.n_pb == 4 else []
+        return after(x, *[self.get(*other) for other in gates])
+
+    def received(self, m):
         out = []
         for s in range(1, self.n_re):
-            message = self.gated(self.send[s - 1][c][piece].astype(jnp.float16), "received", c, piece)
-            got = lax.ppermute(message, "re", [(i, (i + s) % self.n_re) for i in range(self.n_re)])
-            out.append(got)
+            message = self.gated(self.send[s - 1][m].astype(jnp.float16), "received", m)
+            out.append(lax.ppermute(message, "re", [(i, (i + s) % self.n_re) for i in range(self.n_re)]))
         return out
 
     def block(self, c):
-        pieces = [self.get("received", c, i) for i in range(MPIECES[c])]
-        received = [self.gated(got, "block", c).astype(jnp.float32) for several in zip(*pieces) for got in several]
-        return add_up(self.own[c], received, MPIECES[c], ADDCOST[c])
+        m, first = self.carrier[c]
+        received = [self.gated(got, "block", c).astype(jnp.float32) for got in self.get("received", m)]
+        return add_up(self.own[c], received, first, ADDCOST[c])
 
     def near(self, c):
         block = self.gated(self.get("block", c), "near", c)
@@ -313,15 +307,10 @@
 
     def across(self, c):
         block = self.gated(self.get("block", c), "across", c)
-        pairs = [(i, i ^ 3) for i in range(self.n_pb)]
-        return lax.ppermute(block, "pb", pairs[1:-1] if c in SPLIT else pairs)
-
-    def ends(self, c):
-        block = self.gated(self.get("block", c), "ends", c)
-        return lax.ppermute(block, "pb", [(0, 3), (3, 0)])
+        return lax.ppermute(block, "pb", [(i, i ^ 3) for i in range(self.n_pb)])
 
     def passed(self, c):
-        return relay(self.get("block", c), self.gated(self.get("across", c), "passed", c), RELCOST[c])
+        return relay(self.get("block", c), self.gated(self.get("across", c), "passed", c))
 
     def last(self, c):
         return lax.ppermute(self.get("passed", c), "pb", [(0, 2), (3, 1), (1, 0), (2, 3)])
@@ -329,27 +318,18 @@
     def shifted(self, c, s):
         return lax.ppermute(self.get("block", c), "pb", [(i, (i + s) % self.n_pb) for i in range(self.n_pb)])
 
-    def main_blocks(self, c):
+    def step(self, c, s):
+        if s == 0:
+            return self.get("block", c)
         if self.n_pb == 4:
-            out = [(0, self.get("block", 0), self.get("block", c)), (1, self.get("near", 0), self.get("near", c))]
-            if c in SPLIT:
-                if LASTFINAL:
-                    return out + [(3, None, self.get("across", c))]
-                return out + [(2, self.get("last", 0), self.get("last", c)), (3, None, self.get("across", c))]
-            return out + [(3, self.get("across", 0), self.get("across", c))]
-        return [(s, self.shifted(0, s), self.shifted(c, s)) if s else (0, self.get("block", 0), self.get("block", c)) for s in range(self.n_pb - 1)]
-
-    def final_blocks(self, c):
-        if self.n_pb == 4:
-            if c in SPLIT:
-                out = [(2, self.get("last", 0), self.get("last", c))] if LASTFINAL else []
-                return out + [(3, self.get("across", 0), self.get("ends", c))]
-            return [(2, self.get("last", 0), self.get("last", c))]
-        s = self.n_pb - 1
-        return [(s, self.shifted(0, s), self.shifted(c, s))]
+            return self.get({1: "near", 2: "last", 3: "across"}[s], c)
+        return self.get("shifted", c, s)
+
+    def blocks(self, c, steps):
+        return [(s, self.step(0, s), self.step(c, s)) for s in steps]
 
     def acc(self, c):
-        return phonon_main(self.n_pb, self.table, self.get("main_blocks", c), self.firsts[c])
+        return phonon_main(self.n_pb, self.table, self.blocks(c, self.steps[:-1]), self.firsts[c])
 
 
 def body(n_re, n_pb, g_wann, phonon_phase, electron_phase):
@@ -357,26 +337,27 @@
     p_own = g_wann.shape[1]
     cuts = [k_own * c // sum(CUTS) for c in CUTS]
     ahead = p_own * HEAD[0] // HEAD[1] // (2 * GROUP) * (2 * GROUP)
-    if SLICED:
-        own, send = electron_sums(electron_phase, g_wann[:, :ahead], n_re, [k_own], [k_own], None, ahead)
-    else:
-        own, send = electron_sums(electron_phase, g_wann, n_re, [k_own], [k_own], 0, ahead)
+    own, send = electron_sums(electron_phase, g_wann[:, :ahead], n_re, [k_own], [k_own], None, ahead)
     table = phonon_phase
     if p_own % 128 != 0:
         order = jnp.stack([origin(n_pb, step) for step in range(n_pb)])
         table = table.reshape(2, -1, n_pb, p_own)[:, :, order].reshape(table.shape)
-    transfers = Transfers(n_re, n_pb, own, [[a] for a in send])
-    mcuts = [size // MPIECES[1 + c] for c, size in enumerate(cuts) for _ in range(MPIECES[1 + c])]
-    rest = electron_sums(after(electron_phase, transfers.get(*RESTGATE) if RESTGATE else own[0]), g_wann, n_re, cuts, mcuts, ahead, p_own - ahead)
-    at = [sum(MPIECES[1 : 1 + c]) for c in range(len(cuts) + 1)]
-    transfers.own = own + rest[0]
-    transfers.send = [[a] + [b[at[c] : at[c + 1]] for c in range(len(cuts))] for a, b in zip(send, rest[1])]
+    transfers = Transfers(n_re, n_pb, own, [list(a) for a in send])
+    transfers.carrier = [(0, 0)]
+    mcuts = [k_own * m // sum(MCUTS) for m in MCUTS]
+    for c in range(len(cuts)):
+        first = sum(cuts[:c])
+        m = max(m for m in range(len(mcuts)) if sum(mcuts[:m]) <= first)
+        transfers.carrier.append((1 + m, first - sum(mcuts[:m])))
+    rest = electron_sums(after(electron_phase, own[0]), g_wann, n_re, cuts, mcuts, ahead, p_own - ahead)
+    transfers.own = list(own) + list(rest[0])
+    transfers.send = [list(a) + list(b) for a, b in zip(send, rest[1])]
     transfers.table = table
     transfers.firsts = [None] + [sum(cuts[:c]) for c in range(len(cuts))]
     result = None
     for c in range(1, 1 + len(cuts)):
         acc = transfers.get("acc", c)
-        result = phonon_final(n_pb, table, acc, transfers.get("final_blocks", c), result, transfers.firsts[c], k_own)
+        result = phonon_final(n_pb, table, acc, transfers.blocks(c, transfers.steps[-1:]), result, transfers.firsts[c], k_own)
     return result
 
 

time: 48.5 us -> 47.6 us (0.981)
  waiting for transfers between devices: 17.3 us -> 5.34 us
  starting transfers between devices: 21.4 us -> 31.3 us
  Pallas kernels: 8.11 us -> 9.23 us
    ppermute x3 -> x4, starting transfers between devices: 5.77 us -> 14.4 us  [last(): lax.ppermute(self.get('passed', c), 'pb', [(0, 2), (3, 1), (1, 0), (2, 3)])]
    ppermute x3 -> x4, waiting for transfers between devices: 10.3 us -> 4.08 us  [last(): lax.ppermute(self.get('passed', c), 'pb', [(0, 2), (3, 1), (1, 0), (2, 3)])]
    ppermute x3 -> x4, waiting for transfers between devices: 3.99 us -> 0.01 us  [near(): return lax.ppermute(block, 'pb', [(i, i ^ 1) for i in range(self.n_pb)])]
    ppermute x3 -> x4, waiting for transfers between devices: 2.18 us -> 0.41 us  [across(): return lax.ppermute(block, 'pb', [(i, i ^ 3) for i in range(self.n_pb)])]
    pallas_call x2 -> x3, Pallas kernels: 2.63 us -> 3.56 us  [phonon_final(): pl.pallas_call(functools.partial(final_kernel, steps, n_pb, first, len(al...]
    ppermute x3 -> x4, starting transfers between devices: 9.88 us -> 10.5 us  [across(): return lax.ppermute(block, 'pb', [(i, i ^ 3) for i in range(self.n_pb)])]
    ppermute x3 -> x4, starting transfers between devices: 1.11 us -> 1.71 us  [near(): return lax.ppermute(block, 'pb', [(i, i ^ 1) for i in range(self.n_pb)])]
    pallas_call x2 -> x3, Pallas kernels: 1.98 us -> 2.14 us  [phonon_main(): pl.pallas_call(functools.partial(main_kernel, steps, n_pb, first), in_spe...]
  transfers between devices with their start and end apart: 12 -> 15, of which waited for: 6 -> 4; matrix products, arithmetic and copies ran while one was open for 0% -> 0% of each run, Pallas kernels for 12% -> 15%
where the time goes in v4:
time: 47.6 us; the launch traced here: 47.5 us
  starting transfers between devices  31.3 us (66%)
  Pallas kernels  9.23 us (19%)
  waiting for transfers between devices  5.34 us (11%)
  local copies, waits for them, and re-layouts  1.31 us (3%)
    ppermute x4, starting transfers between devices, last(): lax.ppermute(self.get('passed', c), 'pb', [(0, 2), (3, 1), (1, 0), (2, 3)])  14.4 us
    ppermute x4, starting transfers between devices, across(): return lax.ppermute(block, 'pb', [(i, i ^ 3) for i in range(self.n_pb)])  10.5 us
    ppermute x3, starting transfers between devices, received(): lax.ppermute(message, 're', [(i, (i + s) % self.n_re) for i in range(self...  4.65 us
    ppermute x4, waiting for transfers between devices, last(): lax.ppermute(self.get('passed', c), 'pb', [(0, 2), (3, 1), (1, 0), (2, 3)])  4.08 us
    pallas_call x3, Pallas kernels, phonon_final(): pl.pallas_call(functools.partial(final_kernel, steps, n_pb, first, len(al...  3.56 us
    pallas_call x2, Pallas kernels, electron_sums(): pl.pallas_call(functools.partial(electron_kernel, n_re, cuts, mcuts, piec...  3.19 us
    pallas_call x3, Pallas kernels, phonon_main(): pl.pallas_call(functools.partial(main_kernel, steps, n_pb, first), in_spe...  2.14 us
    ppermute x4, starting transfers between devices, near(): return lax.ppermute(block, 'pb', [(i, i ^ 1) for i in range(self.n_pb)])  1.71 us
  transfers between devices with their start and end apart: 15, of which 4 were waited for; matrix products, arithmetic and copies ran while one was open for 0% of the time, Pallas kernels for 15%

profile of v4, /device:TPU:0, one launch (start us, length us, event | category | flops | bytes accessed | tf_op | source)
XLA Modules:
  0.0 47.5 jit_solution(10682404422695286450)
XLA Ops:
  0.0 1.3 %slice.3.g_ref = bf16[2,64,32,128]{3,2,1,0:T(8,128)(2,1)S(1)} slice(bf16[2,256,32,128]{3,2,1,0:T(8,128)(2,1)} %g_ref.1), slice={[0:2], [0:64], [0:32], [0:128]} | slice | bytes 2097152 | tf_op jit(solution)/shard_map/slice | solution.py:340
  1.3 0.6 %shard_map.37 = (f32[2,4,64,128]{3,2,1,0:T(8,128)S(1)}, f32[528,128]{1,0:T(8,128)S(1)}) custom-call(bf16[2,8,64]{2,1,0:T(8,128)(2,1)S(1)} %copy-done.1, bf16[2,64,32,128]{3,2,1,0:T(8,128)(2,1)S(1)} %slice.3.g_ref), custom_call_target="tpu_custom_call" | custom-call | flops 16777216 | bytes 1048576 | tf_op jit(solution)/shard_map/pallas_call | solution.py:130
  2.0 3.0 %collective-permute-start = (f16[528,128]{1,0:T(8,128)(2,1)S(1)}, f16[528,128]{1,0:T(8,128)(2,1)S(1)}, u32[]{:S(2)}, u32[]{:S(2)}) collective-permute-start(f16[528,128]{1,0:T(8,128)(2,1)S(1)} %convert_element_type.19), channel_id=1, source_target_pairs={{0,2},{2,0},{1,3},{3,1},{4,6},{6,4},{5,7},{7,5},{8,10},{10,8},{9,1... | collective-permute-start | bytes 405512 | tf_op jit(solution)/shard_map/ppermute | solution.py:296
  5.0 2.6 %shard_map.39 = (f32[2,1,192,128]{3,2,1,0:T(8,128)S(1)}, f32[2,1,192,128]{3,2,1,0:T(8,128)S(1)}, f32[2,2,192,128]{3,2,1,0:T(8,128)S(1)}, f32[400,128]{1,0:T(8,128)S(1)}, f32[1168,128]{1,0:T(8,128)S(1)}) custom-call(bf16[2,8,64]{2,1,0:T(8,128)(2,1)S(1)} %copy-done.1, bf16[2,256,32,128]{3,2,1,0:T(8,128)(2,1)} %g_ref.1), custom_call_target="tpu_custom_call" | custom-call | flops 50331648 | bytes 3145728 | tf_op jit(solution)/shard_map/pallas_call | solution.py:130
  7.7 0.8 %collective-permute-done = f16[528,128]{1,0:T(8,128)(2,1)S(1)} collective-permute-done((f16[528,128]{1,0:T(8,128)(2,1)S(1)}, f16[528,128]{1,0:T(8,128)(2,1)S(1)}, u32[]{:S(2)}, u32[]{:S(2)}) %collective-permute-start) | collective-permute-done | bytes 135200 | tf_op jit(solution)/shard_map/ppermute | solution.py:296
  8.6 3.9 %collective-permute-start.3 = (bf16[2,4,64,128]{3,2,1,0:T(8,128)(2,1)S(1)}, bf16[2,4,64,128]{3,2,1,0:T(8,128)(2,1)S(1)}, u32[]{:S(2)}, u32[]{:S(2)}) collective-permute-start(bf16[2,4,64,128]{3,2,1,0:T(8,128)(2,1)S(1)} %shard_map.38.refs_0_.block_ref), channel_id=1, source_target_pairs={{0,12},{4,8},{8,4},{12,0},{1,13},{5,9},{9,5},{13,1},{2,14},{6,10},... | collective-permute-start | bytes 393224 | tf_op jit(solution)/shard_map/ppermute | solution.py:310
  12.6 1.6 %collective-permute-start.1 = (f16[1168,128]{1,0:T(8,128)(2,1)S(1)}, f16[1168,128]{1,0:T(8,128)(2,1)S(1)}, u32[]{:S(2)}, u32[]{:S(2)}) collective-permute-start(f16[1168,128]{1,0:T(8,128)(2,1)S(1)} %convert_element_type.21), channel_id=1, source_target_pairs={{0,2},{2,0},{1,3},{3,1},{4,6},{6,4},{5,7},{7,5},{8,10},{10,8},{9,1... | collective-permute-start | bytes 897032 | tf_op jit(solution)/shard_map/ppermute | solution.py:296
  14.1 2.5 %collective-permute-start.9 = (bf16[2,1,192,128]{3,2,1,0:T(8,128)(2,1)S(1)}, bf16[2,1,192,128]{3,2,1,0:T(8,128)(2,1)S(1)}, u32[]{:S(2)}, u32[]{:S(2)}) collective-permute-start(bf16[2,1,192,128]{3,2,1,0:T(8,128)(2,1)S(1)} %shard_map.44.block_ref.refs_1_), channel_id=1, source_target_pairs={{0,12},{4,8},{8,4},{12,0},{1,13},{5,9},{9,5},{13,1},{2,14},{6,10},... | collective-permute-start | bytes 294920 | tf_op jit(solution)/shard_map/ppermute | solution.py:310
  16.7 4.7 %collective-permute-start.6 = (bf16[2,4,64,128]{3,2,1,0:T(8,128)(2,1)S(1)}, bf16[2,4,64,128]{3,2,1,0:T(8,128)(2,1)S(1)}, u32[]{:S(2)}, u32[]{:S(2)}) collective-permute-start(bf16[2,4,64,128]{3,2,1,0:T(8,128)(2,1)S(1)} %shard_map.42), channel_id=1, source_target_pairs={{0,8},{12,4},{4,0},{8,12},{1,9},{13,5},{5,1},{9,13},{2,10},{14,6},... | collective-permute-start | bytes 393224 | tf_op jit(solution)/shard_map/ppermute | solution.py:316
  21.5 2.1 %collective-permute-start.7 = (bf16[2,1,192,128]{3,2,1,0:T(8,128)(2,1)S(1)}, bf16[2,1,192,128]{3,2,1,0:T(8,128)(2,1)S(1)}, u32[]{:S(2)}, u32[]{:S(2)}) collective-permute-start(bf16[2,1,192,128]{3,2,1,0:T(8,128)(2,1)S(1)} %shard_map.43.block_ref.refs_1_), channel_id=1, source_target_pairs={{0,12},{4,8},{8,4},{12,0},{1,13},{5,9},{9,5},{13,1},{2,14},{6,10},... | collective-permute-start | bytes 294920 | tf_op jit(solution)/shard_map/ppermute | solution.py:310
  23.7 2.4 %collective-permute-start.14 = (bf16[2,1,192,128]{3,2,1,0:T(8,128)(2,1)S(1)}, bf16[2,1,192,128]{3,2,1,0:T(8,128)(2,1)S(1)}, u32[]{:S(2)}, u32[]{:S(2)}) collective-permute-start(bf16[2,1,192,128]{3,2,1,0:T(8,128)(2,1)S(1)} %shard_map.45), channel_id=1, source_target_pairs={{0,8},{12,4},{4,0},{8,12},{1,9},{13,5},{5,1},{9,13},{2,10},{14,6},... | collective-permute-start | bytes 294920 | tf_op jit(solution)/shard_map/ppermute | solution.py:316
  26.1 0.6 %shard_map.49.acc_ref = f32[1,512,256]{2,1,0:T(8,128)S(1)} custom-call(bf16[2,512,1024]{2,1,0:T(8,128)(2,1)S(1)} %copy-done, bf16[2,4,64,128]{3,2,1,0:T(8,128)(2,1)S(1)} %shard_map.38.refs_0_.block_ref, bf16[2,1,192,128]{3,2,1,0:T(8,128)(2,1)S(1)} %shard_map.44.block_ref.refs_1_, bf16[2,4,64,128]{3,2,1,0:T(8,128)(2,1)S(1)} %collective-permute-done.2.refs_2_, ...), custom_call_target="tpu_custom_call" | custom-call | flops 3019898880 | tf_op jit(solution)/shard_map/pallas_call | solution.py:249
  26.7 2.1 %collective-permute-start.5 = (bf16[2,2,192,128]{3,2,1,0:T(8,128)(2,1)S(1)}, bf16[2,2,192,128]{3,2,1,0:T(8,128)(2,1)S(1)}, u32[]{:S(2)}, u32[]{:S(2)}) collective-permute-start(bf16[2,2,192,128]{3,2,1,0:T(8,128)(2,1)S(1)} %shard_map.40.refs_1_.block_ref), channel_id=1, source_target_pairs={{0,12},{4,8},{8,4},{12,0},{1,13},{5,9},{9,5},{13,1},{2,14},{6,10},... | collective-permute-start | bytes 589832 | tf_op jit(solution)/shard_map/ppermute | solution.py:310
  28.8 0.4 collective-permute-done.7.far_ref.refs_5_
  29.1 1.7 %collective-permute-start.4 = (bf16[2,2,192,128]{3,2,1,0:T(8,128)(2,1)S(1)}, bf16[2,2,192,128]{3,2,1,0:T(8,128)(2,1)S(1)}, u32[]{:S(2)}, u32[]{:S(2)}) collective-permute-start(bf16[2,2,192,128]{3,2,1,0:T(8,128)(2,1)S(1)} %shard_map.40.refs_1_.block_ref), channel_id=1, source_target_pairs={{0,4},{4,0},{8,12},{12,8},{1,5},{5,1},{9,13},{13,9},{2,6},{6,2},{1... | collective-permute-start | bytes 589832 | tf_op jit(solution)/shard_map/ppermute | solution.py:306
  30.9 2.6 %collective-permute-start.12 = (bf16[2,1,192,128]{3,2,1,0:T(8,128)(2,1)S(1)}, bf16[2,1,192,128]{3,2,1,0:T(8,128)(2,1)S(1)}, u32[]{:S(2)}, u32[]{:S(2)}) collective-permute-start(bf16[2,1,192,128]{3,2,1,0:T(8,128)(2,1)S(1)} %shard_map.46), channel_id=1, source_target_pairs={{0,8},{12,4},{4,0},{8,12},{1,9},{13,5},{5,1},{9,13},{2,10},{14,6},... | collective-permute-start | bytes 294920 | tf_op jit(solution)/shard_map/ppermute | solution.py:316
  33.5 2.3 %collective-permute-done.14.refs_1_ = bf16[2,1,192,128]{3,2,1,0:T(8,128)(2,1)S(1)} collective-permute-done((bf16[2,1,192,128]{3,2,1,0:T(8,128)(2,1)S(1)}, bf16[2,1,192,128]{3,2,1,0:T(8,128)(2,1)S(1)}, u32[]{:S(2)}, u32[]{:S(2)}) %collective-permute-start.14) | collective-permute-done | bytes 98336 | tf_op jit(solution)/shard_map/ppermute | solution.py:316
  35.8 1.1 %shard_map.50.refs_2_ = f32[4,2,512,128]{3,2,1,0:T(8,128)} custom-call(bf16[2,512,1024]{2,1,0:T(8,128)(2,1)S(1)} %copy-done, f32[1,512,256]{2,1,0:T(8,128)S(1)} %shard_map.49.acc_ref, bf16[2,4,64,128]{3,2,1,0:T(8,128)(2,1)S(1)} %collective-permute-done.6.refs_0_, bf16[2,1,192,128]{3,2,1,0:T(8,128)(2,1)S(1)} %collective-permute-done.14.refs_1_), custom_call_target="tpu_custom_call" | custom-call | flops 1006632960 | bytes 524288 | tf_op jit(solution)/shard_map/pallas_call | solution.py:264
  36.9 0.6 %shard_map.48.acc_ref = f32[1,512,256]{2,1,0:T(8,128)S(1)} custom-call(bf16[2,512,1024]{2,1,0:T(8,128)(2,1)S(1)} %copy-done, bf16[2,4,64,128]{3,2,1,0:T(8,128)(2,1)S(1)} %shard_map.38.refs_0_.block_ref, bf16[2,1,192,128]{3,2,1,0:T(8,128)(2,1)S(1)} %shard_map.43.block_ref.refs_1_, bf16[2,4,64,128]{3,2,1,0:T(8,128)(2,1)S(1)} %collective-permute-done.2.refs_2_, ...), custom_call_target="tpu_custom_call" | custom-call | flops 3019898880 | tf_op jit(solution)/shard_map/pallas_call | solution.py:249
  37.6 4.6 %collective-permute-start.10 = (bf16[2,2,192,128]{3,2,1,0:T(8,128)(2,1)S(1)}, bf16[2,2,192,128]{3,2,1,0:T(8,128)(2,1)S(1)}, u32[]{:S(2)}, u32[]{:S(2)}) collective-permute-start(bf16[2,2,192,128]{3,2,1,0:T(8,128)(2,1)S(1)} %shard_map.47), channel_id=1, source_target_pairs={{0,8},{12,4},{4,0},{8,12},{1,9},{13,5},{5,1},{9,13},{2,10},{14,6},... | collective-permute-start | bytes 589832 | tf_op jit(solution)/shard_map/ppermute | solution.py:316
  42.2 1.0 %shard_map.41.acc_ref = f32[2,512,256]{2,1,0:T(8,128)S(1)} custom-call(bf16[2,512,1024]{2,1,0:T(8,128)(2,1)S(1)} %copy-done, bf16[2,4,64,128]{3,2,1,0:T(8,128)(2,1)S(1)} %shard_map.38.refs_0_.block_ref, bf16[2,2,192,128]{3,2,1,0:T(8,128)(2,1)S(1)} %shard_map.40.refs_1_.block_ref, bf16[2,4,64,128]{3,2,1,0:T(8,128)(2,1)S(1)} %collective-permute-done.2.refs_2_, ...), custom_call_target="tpu_custom_call" | custom-call | flops 6039797760 | tf_op jit(solution)/shard_map/pallas_call | solution.py:249
  43.2 1.1 %shard_map.51.refs_2_ = f32[4,2,512,128]{3,2,1,0:T(8,128)} custom-call(bf16[2,512,1024]{2,1,0:T(8,128)(2,1)S(1)} %copy-done, f32[1,512,256]{2,1,0:T(8,128)S(1)} %shard_map.48.acc_ref, bf16[2,4,64,128]{3,2,1,0:T(8,128)(2,1)S(1)} %collective-permute-done.6.refs_0_, ...), custom_call_target="tpu_custom_call", output_to_operand_aliasing={{}: (4, {})} | custom-call | flops 1006632960 | bytes 524288 | tf_op jit(solution)/shard_map/pallas_call | solution.py:264
  44.3 1.8 %collective-permute-done.10.refs_1_ = bf16[2,2,192,128]{3,2,1,0:T(8,128)(2,1)S(1)} collective-permute-done((bf16[2,2,192,128]{3,2,1,0:T(8,128)(2,1)S(1)}, bf16[2,2,192,128]{3,2,1,0:T(8,128)(2,1)S(1)}, u32[]{:S(2)}, u32[]{:S(2)}) %collective-permute-start.10) | collective-permute-done | bytes 196640 | tf_op jit(solution)/shard_map/ppermute | solution.py:316
  46.2 1.3 %shard_map.52 = f32[4,2,512,128]{3,2,1,0:T(8,128)} custom-call(bf16[2,512,1024]{2,1,0:T(8,128)(2,1)S(1)} %copy-done, f32[2,512,256]{2,1,0:T(8,128)S(1)} %shard_map.41.acc_ref, bf16[2,4,64,128]{3,2,1,0:T(8,128)(2,1)S(1)} %collective-permute-done.6.refs_0_, ...), custom_call_target="tpu_custom_call", output_to_operand_aliasing={{}: (4, {})} | custom-call | flops 2013265920 | bytes 1048576 | tf_op jit(solution)/shard_map/pallas_call | solution.py:264
  (33 shorter events, 0.7 us)
Async XLA Ops:
  0.0 1.3 %copy-start.1 = (bf16[2,8,64]{2,1,0:T(8,128)(2,1)S(1)}, bf16[2,8,64]{2,1,0:T(8,128)(2,1)}, u32[]{:S(2)}) copy-start(bf16[2,8,64]{2,1,0:T(8,128)(2,1)} %phase_ref.2) | copy-start | bytes 6148
  2.0 6.6 %collective-permute-start = (f16[528,128]{1,0:T(8,128)(2,1)S(1)}, f16[528,128]{1,0:T(8,128)(2,1)S(1)}, u32[]{:S(2)}, u32[]{:S(2)}) collective-permute-start(f16[528,128]{1,0:T(8,128)(2,1)S(1)} %convert_element_type.19), channel_id=1, source_target_pairs={{0,2},{2,0},{1,3},{3,1},{4,6},{6,4},{5,7},{7,5},{8,10},{10,8},{9,1... | collective-permute-start | bytes 405512 | tf_op jit(solution)/shard_map/ppermute | solution.py:296
  7.6 4.9 %collective-permute-start.8 = (f16[400,128]{1,0:T(8,128)(2,1)S(1)}, f16[400,128]{1,0:T(8,128)(2,1)S(1)}, u32[]{:S(2)}, u32[]{:S(2)}) collective-permute-start(f16[400,128]{1,0:T(8,128)(2,1)S(1)} %convert_element_type.23), channel_id=1, source_target_pairs={{0,2},{2,0},{1,3},{3,1},{4,6},{6,4},{5,7},{7,5},{8,10},{10,8},{9,1... | collective-permute-start | bytes 307208 | tf_op jit(solution)/shard_map/ppermute | solution.py:296
  8.6 8.0 %collective-permute-start.3 = (bf16[2,4,64,128]{3,2,1,0:T(8,128)(2,1)S(1)}, bf16[2,4,64,128]{3,2,1,0:T(8,128)(2,1)S(1)}, u32[]{:S(2)}, u32[]{:S(2)}) collective-permute-start(bf16[2,4,64,128]{3,2,1,0:T(8,128)(2,1)S(1)} %shard_map.38.refs_0_.block_ref), channel_id=1, source_target_pairs={{0,12},{4,8},{8,4},{12,0},{1,13},{5,9},{9,5},{13,1},{2,14},{6,10},... | collective-permute-start | bytes 393224 | tf_op jit(solution)/shard_map/ppermute | solution.py:310
  12.5 8.9 %collective-permute-start.2 = (bf16[2,4,64,128]{3,2,1,0:T(8,128)(2,1)S(1)}, bf16[2,4,64,128]{3,2,1,0:T(8,128)(2,1)S(1)}, u32[]{:S(2)}, u32[]{:S(2)}) collective-permute-start(bf16[2,4,64,128]{3,2,1,0:T(8,128)(2,1)S(1)} %shard_map.38.refs_0_.block_ref), channel_id=1, source_target_pairs={{0,4},{4,0},{8,12},{12,8},{1,5},{5,1},{9,13},{13,9},{2,6},{6,2},{1... | collective-permute-start | bytes 393224 | tf_op jit(solution)/shard_map/ppermute | solution.py:306
  12.6 8.8 %collective-permute-start.1 = (f16[1168,128]{1,0:T(8,128)(2,1)S(1)}, f16[1168,128]{1,0:T(8,128)(2,1)S(1)}, u32[]{:S(2)}, u32[]{:S(2)}) collective-permute-start(f16[1168,128]{1,0:T(8,128)(2,1)S(1)} %convert_element_type.21), channel_id=1, source_target_pairs={{0,2},{2,0},{1,3},{3,1},{4,6},{6,4},{5,7},{7,5},{8,10},{10,8},{9,1... | collective-permute-start | bytes 897032 | tf_op jit(solution)/shard_map/ppermute | solution.py:296
  14.1 9.5 %collective-permute-start.9 = (bf16[2,1,192,128]{3,2,1,0:T(8,128)(2,1)S(1)}, bf16[2,1,192,128]{3,2,1,0:T(8,128)(2,1)S(1)}, u32[]{:S(2)}, u32[]{:S(2)}) collective-permute-start(bf16[2,1,192,128]{3,2,1,0:T(8,128)(2,1)S(1)} %shard_map.44.block_ref.refs_1_), channel_id=1, source_target_pairs={{0,12},{4,8},{8,4},{12,0},{1,13},{5,9},{9,5},{13,1},{2,14},{6,10},... | collective-permute-start | bytes 294920 | tf_op jit(solution)/shard_map/ppermute | solution.py:310
  16.6 9.5 %collective-permute-start.13 = (bf16[2,1,192,128]{3,2,1,0:T(8,128)(2,1)S(1)}, bf16[2,1,192,128]{3,2,1,0:T(8,128)(2,1)S(1)}, u32[]{:S(2)}, u32[]{:S(2)}) collective-permute-start(bf16[2,1,192,128]{3,2,1,0:T(8,128)(2,1)S(1)} %shard_map.44.block_ref.refs_1_), channel_id=1, source_target_pairs={{0,4},{4,0},{8,12},{12,8},{1,5},{5,1},{9,13},{13,9},{2,6},{6,2},{1... | collective-permute-start | bytes 294920 | tf_op jit(solution)/shard_map/ppermute | solution.py:306
  16.7 14.2 %collective-permute-start.6 = (bf16[2,4,64,128]{3,2,1,0:T(8,128)(2,1)S(1)}, bf16[2,4,64,128]{3,2,1,0:T(8,128)(2,1)S(1)}, u32[]{:S(2)}, u32[]{:S(2)}) collective-permute-start(bf16[2,4,64,128]{3,2,1,0:T(8,128)(2,1)S(1)} %shard_map.42), channel_id=1, source_target_pairs={{0,8},{12,4},{4,0},{8,12},{1,9},{13,5},{5,1},{9,13},{2,10},{14,6},... | collective-permute-start | bytes 393224 | tf_op jit(solution)/shard_map/ppermute | solution.py:316
  21.5 7.6 %collective-permute-start.7 = (bf16[2,1,192,128]{3,2,1,0:T(8,128)(2,1)S(1)}, bf16[2,1,192,128]{3,2,1,0:T(8,128)(2,1)S(1)}, u32[]{:S(2)}, u32[]{:S(2)}) collective-permute-start(bf16[2,1,192,128]{3,2,1,0:T(8,128)(2,1)S(1)} %shard_map.43.block_ref.refs_1_), channel_id=1, source_target_pairs={{0,12},{4,8},{8,4},{12,0},{1,13},{5,9},{9,5},{13,1},{2,14},{6,10},... | collective-permute-start | bytes 294920 | tf_op jit(solution)/shard_map/ppermute | solution.py:310
  23.6 13.3 %collective-permute-start.11 = (bf16[2,1,192,128]{3,2,1,0:T(8,128)(2,1)S(1)}, bf16[2,1,192,128]{3,2,1,0:T(8,128)(2,1)S(1)}, u32[]{:S(2)}, u32[]{:S(2)}) collective-permute-start(bf16[2,1,192,128]{3,2,1,0:T(8,128)(2,1)S(1)} %shard_map.43.block_ref.refs_1_), channel_id=1, source_target_pairs={{0,4},{4,0},{8,12},{12,8},{1,5},{5,1},{9,13},{13,9},{2,6},{6,2},{1... | collective-permute-start | bytes 294920 | tf_op jit(solution)/shard_map/ppermute | solution.py:306
  23.6 2.6 %copy-start = (bf16[2,512,1024]{2,1,0:T(8,128)(2,1)S(1)}, bf16[2,512,1024]{2,1,0:T(8,128)(2,1)}, u32[]{:S(2)}) copy-start(bf16[2,512,1024]{2,1,0:T(8,128)(2,1)} %table_ref.11) | copy-start | bytes 6291460
  23.7 12.1 %collective-permute-start.14 = (bf16[2,1,192,128]{3,2,1,0:T(8,128)(2,1)S(1)}, bf16[2,1,192,128]{3,2,1,0:T(8,128)(2,1)S(1)}, u32[]{:S(2)}, u32[]{:S(2)}) collective-permute-start(bf16[2,1,192,128]{3,2,1,0:T(8,128)(2,1)S(1)} %shard_map.45), channel_id=1, source_target_pairs={{0,8},{12,4},{4,0},{8,12},{1,9},{13,5},{5,1},{9,13},{2,10},{14,6},... | collective-permute-start | bytes 294920 | tf_op jit(solution)/shard_map/ppermute | solution.py:316
  26.7 10.8 %collective-permute-start.5 = (bf16[2,2,192,128]{3,2,1,0:T(8,128)(2,1)S(1)}, bf16[2,2,192,128]{3,2,1,0:T(8,128)(2,1)S(1)}, u32[]{:S(2)}, u32[]{:S(2)}) collective-permute-start(bf16[2,2,192,128]{3,2,1,0:T(8,128)(2,1)S(1)} %shard_map.40.refs_1_.block_ref), channel_id=1, source_target_pairs={{0,12},{4,8},{8,4},{12,0},{1,13},{5,9},{9,5},{13,1},{2,14},{6,10},... | collective-permute-start | bytes 589832 | tf_op jit(solution)/shard_map/ppermute | solution.py:310
  29.1 13.1 %collective-permute-start.4 = (bf16[2,2,192,128]{3,2,1,0:T(8,128)(2,1)S(1)}, bf16[2,2,192,128]{3,2,1,0:T(8,128)(2,1)S(1)}, u32[]{:S(2)}, u32[]{:S(2)}) collective-permute-start(bf16[2,2,192,128]{3,2,1,0:T(8,128)(2,1)S(1)} %shard_map.40.refs_1_.block_ref), channel_id=1, source_target_pairs={{0,4},{4,0},{8,12},{12,8},{1,5},{5,1},{9,13},{13,9},{2,6},{6,2},{1... | collective-permute-start | bytes 589832 | tf_op jit(solution)/shard_map/ppermute | solution.py:306
  30.9 12.3 %collective-permute-start.12 = (bf16[2,1,192,128]{3,2,1,0:T(8,128)(2,1)S(1)}, bf16[2,1,192,128]{3,2,1,0:T(8,128)(2,1)S(1)}, u32[]{:S(2)}, u32[]{:S(2)}) collective-permute-start(bf16[2,1,192,128]{3,2,1,0:T(8,128)(2,1)S(1)} %shard_map.46), channel_id=1, source_target_pairs={{0,8},{12,4},{4,0},{8,12},{1,9},{13,5},{5,1},{9,13},{2,10},{14,6},... | collective-permute-start | bytes 294920 | tf_op jit(solution)/shard_map/ppermute | solution.py:316
  37.6 8.6 %collective-permute-start.10 = (bf16[2,2,192,128]{3,2,1,0:T(8,128)(2,1)S(1)}, bf16[2,2,192,128]{3,2,1,0:T(8,128)(2,1)S(1)}, u32[]{:S(2)}, u32[]{:S(2)}) collective-permute-start(bf16[2,2,192,128]{3,2,1,0:T(8,128)(2,1)S(1)} %shard_map.47), channel_id=1, source_target_pairs={{0,8},{12,4},{4,0},{8,12},{1,9},{13,5},{5,1},{9,13},{2,10},{14,6},... | collective-permute-start | bytes 589832 | tf_op jit(solution)/shard_map/ppermute | solution.py:316

commit v5 on v4

--- a/solution.py
+++ b/solution.py
@@ -17,13 +17,14 @@
 CUTS = (1, 1, 2)
 ADDCOST = (0, 10**10, 10**10, 10**10)
 GATES = {
-    ("received", 2): [("block", 0)],
     ("block", 1): [("block", 0)],
     ("block", 2): [("near", 0), ("across", 0)],
     ("block", 3): [("near", 0), ("across", 0)],
+    ("passed", 0): [("near", 0)],
     ("passed", 1): [("passed", 0), ("block", 3)],
     ("passed", 2): [("passed", 1)],
     ("passed", 3): [("passed", 2)],
+    ("received", 2): [("block", 0)],
 }
 MCUTS = (1, 3)
 PHON = 80
@@ -179,24 +180,6 @@
     return me ^ step if n == 4 else (me - step) % n
 
 
-def relay_kernel(block_ref, far_ref, out_ref):
-    me = lax.axis_index("pb")
-    middle = (me == 1) | (me == 2)
-    for c in range(2):
-        out_ref[c] = jnp.where(middle, far_ref[c], block_ref[c])
-
-
-def relay(block, far):
-    return pl.pallas_call(
-        relay_kernel,
-        in_specs=[VMEM, VMEM],
-        out_specs=VMEM,
-        out_shape=jax.ShapeDtypeStruct(block.shape, block.dtype),
-        compiler_params=pltpu.CompilerParams(vmem_limit_bytes=SMALL),
-        cost_estimate=pl.CostEstimate(flops=0, bytes_accessed=0, transcendentals=0),
-    )(block, far)
-
-
 def after(x, *others):
     return lax.optimization_barrier((x, *others))[0] if others else x
 
@@ -277,7 +260,7 @@
     def __init__(self, n_re, n_pb, own, send):
         self.n_re, self.n_pb, self.own, self.send = n_re, n_pb, own, send
         self.made = {}
-        self.steps = (0, 1, 3, 2) if n_pb == 4 else tuple(range(n_pb))
+        self.steps = tuple(range(n_pb))
 
     def get(self, *what):
         if what not in self.made:
@@ -307,13 +290,13 @@
 
     def across(self, c):
         block = self.gated(self.get("block", c), "across", c)
-        return lax.ppermute(block, "pb", [(i, i ^ 3) for i in range(self.n_pb)])
+        return lax.ppermute(block, "pb", [(i, i ^ 2) for i in range(self.n_pb)])
 
     def passed(self, c):
-        return relay(self.get("block", c), self.gated(self.get("across", c), "passed", c))
+        return self.gated(self.get("across", c), "passed", c)
 
     def last(self, c):
-        return lax.ppermute(self.get("passed", c), "pb", [(0, 2), (3, 1), (1, 0), (2, 3)])
+        return lax.ppermute(self.get("passed", c), "pb", [(i, i ^ 1) for i in range(self.n_pb)])
 
     def shifted(self, c, s):
         return lax.ppermute(self.get("block", c), "pb", [(i, (i + s) % self.n_pb) for i in range(self.n_pb)])
@@ -322,7 +305,7 @@
         if s == 0:
             return self.get("block", c)
         if self.n_pb == 4:
-            return self.get({1: "near", 2: "last", 3: "across"}[s], c)
+            return self.get({1: "near", 2: "across", 3: "last"}[s], c)
         return self.get("shifted", c, s)
 
     def blocks(self, c, steps):

time: 47.6 us -> 46.5 us (0.977)
  starting transfers between devices: 31.3 us -> 23 us
  waiting for transfers between devices: 5.34 us -> 12.7 us
    ppermute x8, starting transfers between devices: 24.9 us -> 14.4 us  [the longest x4 7.8 us: across(): return lax.ppermute(block, 'pb', [(i, i ^ 2) for i in range(self.n_pb)])]
    ppermute x8, waiting for transfers between devices: 4.5 us -> 10.9 us  [the longest x4 5.52 us: last(): lax.ppermute(self.get('passed', c), 'pb', [(i, i ^ 1) for i in range(self...]
    ppermute x4, starting transfers between devices: 1.71 us -> 3.96 us  [near(): return lax.ppermute(block, 'pb', [(i, i ^ 1) for i in range(self.n_pb)])]
    ppermute x4, waiting for transfers between devices: 0.01 us -> 1.02 us  [near(): return lax.ppermute(block, 'pb', [(i, i ^ 1) for i in range(self.n_pb)])]
  transfers between devices with their start and end apart: 15 -> 15, of which waited for: 4 -> 7; matrix products, arithmetic and copies ran while one was open for 0% -> 0% of each run, Pallas kernels for 15% -> 15%
where the time goes in v5:
time: 46.5 us; the launch traced here: 46.4 us
  starting transfers between devices  23 us (49%)
  waiting for transfers between devices  12.7 us (27%)
  Pallas kernels  9.08 us (20%)
  local copies, waits for them, and re-layouts  1.31 us (3%)
    ppermute x4, starting transfers between devices, across(): return lax.ppermute(block, 'pb', [(i, i ^ 2) for i in range(self.n_pb)])  7.8 us
    ppermute x4, starting transfers between devices, last(): lax.ppermute(self.get('passed', c), 'pb', [(i, i ^ 1) for i in range(self...  6.55 us
    ppermute x4, waiting for transfers between devices, last(): lax.ppermute(self.get('passed', c), 'pb', [(i, i ^ 1) for i in range(self...  5.52 us
    ppermute x4, waiting for transfers between devices, across(): return lax.ppermute(block, 'pb', [(i, i ^ 2) for i in range(self.n_pb)])  5.33 us
    ppermute x3, starting transfers between devices, received(): lax.ppermute(message, 're', [(i, (i + s) % self.n_re) for i in range(self...  4.65 us
    ppermute x4, starting transfers between devices, near(): return lax.ppermute(block, 'pb', [(i, i ^ 1) for i in range(self.n_pb)])  3.96 us
    pallas_call x3, Pallas kernels, phonon_final(): pl.pallas_call(functools.partial(final_kernel, steps, n_pb, first, len(al...  3.57 us
    pallas_call x2, Pallas kernels, electron_sums(): pl.pallas_call(functools.partial(electron_kernel, n_re, cuts, mcuts, piec...  3.19 us
  transfers between devices with their start and end apart: 15, of which 7 were waited for; matrix products, arithmetic and copies ran while one was open for 0% of the time, Pallas kernels for 15%

profile of v5, /device:TPU:0, one launch (start us, length us, event | category | flops | bytes accessed | tf_op | source)
XLA Modules:
  0.0 46.4 jit_solution(1961551825757833593)
XLA Ops:
  0.0 1.3 %slice.3.g_ref = bf16[2,64,32,128]{3,2,1,0:T(8,128)(2,1)S(1)} slice(bf16[2,256,32,128]{3,2,1,0:T(8,128)(2,1)} %g_ref.1), slice={[0:2], [0:64], [0:32], [0:128]} | slice | bytes 2097152 | tf_op jit(solution)/shard_map/slice | solution.py:323
  2.0 3.0 %collective-permute-start = (f16[528,128]{1,0:T(8,128)(2,1)S(1)}, f16[528,128]{1,0:T(8,128)(2,1)S(1)}, u32[]{:S(2)}, u32[]{:S(2)}) collective-permute-start(f16[528,128]{1,0:T(8,128)(2,1)S(1)} %convert_element_type.19), channel_id=1, source_target_pairs={{0,2},{2,0},{1,3},{3,1},{4,6},{6,4},{5,7},{7,5},{8,10},{10,8},{9,1... | collective-permute-start | bytes 405512 | tf_op jit(solution)/shard_map/ppermute | solution.py:279
  5.0 2.6 %shard_map.39 = (f32[2,1,192,128]{3,2,1,0:T(8,128)S(1)}, f32[2,1,192,128]{3,2,1,0:T(8,128)S(1)}, f32[2,2,192,128]{3,2,1,0:T(8,128)S(1)}, f32[400,128]{1,0:T(8,128)S(1)}, f32[1168,128]{1,0:T(8,128)S(1)}) custom-call(bf16[2,8,64]{2,1,0:T(8,128)(2,1)S(1)} %copy-done.1, bf16[2,256,32,128]{3,2,1,0:T(8,128)(2,1)} %g_ref.1), custom_call_target="tpu_custom_call" | custom-call | flops 50331648 | bytes 3145728 | tf_op jit(solution)/shard_map/pallas_call | solution.py:131
  7.7 0.8 %collective-permute-done = f16[528,128]{1,0:T(8,128)(2,1)S(1)} collective-permute-done((f16[528,128]{1,0:T(8,128)(2,1)S(1)}, f16[528,128]{1,0:T(8,128)(2,1)S(1)}, u32[]{:S(2)}, u32[]{:S(2)}) %collective-permute-start) | collective-permute-done | bytes 135200 | tf_op jit(solution)/shard_map/ppermute | solution.py:279
  8.6 1.9 %collective-permute-start.2 = (bf16[2,4,64,128]{3,2,1,0:T(8,128)(2,1)S(1)}, bf16[2,4,64,128]{3,2,1,0:T(8,128)(2,1)S(1)}, u32[]{:S(2)}, u32[]{:S(2)}) collective-permute-start(bf16[2,4,64,128]{3,2,1,0:T(8,128)(2,1)S(1)} %shard_map.38.refs_0_), channel_id=1, source_target_pairs={{0,4},{4,0},{8,12},{12,8},{1,5},{5,1},{9,13},{13,9},{2,6},{6,2},{1... | collective-permute-start | bytes 393224 | tf_op jit(solution)/shard_map/ppermute | solution.py:289
  10.5 2.6 %collective-permute-start.3 = (bf16[2,4,64,128]{3,2,1,0:T(8,128)(2,1)S(1)}, bf16[2,4,64,128]{3,2,1,0:T(8,128)(2,1)S(1)}, u32[]{:S(2)}, u32[]{:S(2)}) collective-permute-start(bf16[2,4,64,128]{3,2,1,0:T(8,128)(2,1)S(1)} %shard_map.38.refs_0_), channel_id=1, source_target_pairs={{0,8},{4,12},{8,0},{12,4},{1,9},{5,13},{9,1},{13,5},{2,10},{6,14},... | collective-permute-start | bytes 393224 | tf_op jit(solution)/shard_map/ppermute | solution.py:293
  13.1 1.6 %collective-permute-start.1 = (f16[1168,128]{1,0:T(8,128)(2,1)S(1)}, f16[1168,128]{1,0:T(8,128)(2,1)S(1)}, u32[]{:S(2)}, u32[]{:S(2)}) collective-permute-start(f16[1168,128]{1,0:T(8,128)(2,1)S(1)} %convert_element_type.21), channel_id=1, source_target_pairs={{0,2},{2,0},{1,3},{3,1},{4,6},{6,4},{5,7},{7,5},{8,10},{10,8},{9,1... | collective-permute-start | bytes 897032 | tf_op jit(solution)/shard_map/ppermute | solution.py:279
  14.7 0.9 %collective-permute-start.9 = (bf16[2,1,192,128]{3,2,1,0:T(8,128)(2,1)S(1)}, bf16[2,1,192,128]{3,2,1,0:T(8,128)(2,1)S(1)}, u32[]{:S(2)}, u32[]{:S(2)}) collective-permute-start(bf16[2,1,192,128]{3,2,1,0:T(8,128)(2,1)S(1)} %shard_map.43.refs_1_), channel_id=1, source_target_pairs={{0,8},{4,12},{8,0},{12,4},{1,9},{5,13},{9,1},{13,5},{2,10},{6,14},... | collective-permute-start | bytes 294920 | tf_op jit(solution)/shard_map/ppermute | solution.py:293
  15.6 1.6 %collective-permute-start.13 = (bf16[2,1,192,128]{3,2,1,0:T(8,128)(2,1)S(1)}, bf16[2,1,192,128]{3,2,1,0:T(8,128)(2,1)S(1)}, u32[]{:S(2)}, u32[]{:S(2)}) collective-permute-start(bf16[2,1,192,128]{3,2,1,0:T(8,128)(2,1)S(1)} %shard_map.43.refs_1_), channel_id=1, source_target_pairs={{0,4},{4,0},{8,12},{12,8},{1,5},{5,1},{9,13},{13,9},{2,6},{6,2},{1... | collective-permute-start | bytes 294920 | tf_op jit(solution)/shard_map/ppermute | solution.py:289
  17.2 2.7 %collective-permute-done.3.refs_4_ = bf16[2,4,64,128]{3,2,1,0:T(8,128)(2,1)S(1)} collective-permute-done((bf16[2,4,64,128]{3,2,1,0:T(8,128)(2,1)S(1)}, bf16[2,4,64,128]{3,2,1,0:T(8,128)(2,1)S(1)}, u32[]{:S(2)}, u32[]{:S(2)}) %collective-permute-start.3) | collective-permute-done | bytes 131104 | tf_op jit(solution)/shard_map/ppermute | solution.py:293
  19.9 1.3 %collective-permute-start.6 = (bf16[2,4,64,128]{3,2,1,0:T(8,128)(2,1)S(1)}, bf16[2,4,64,128]{3,2,1,0:T(8,128)(2,1)S(1)}, u32[]{:S(2)}, u32[]{:S(2)}) collective-permute-start(bf16[2,4,64,128]{3,2,1,0:T(8,128)(2,1)S(1)} %collective-permute-done.3.refs_4_), channel_id=1, source_target_pairs={{0,4},{4,0},{8,12},{12,8},{1,5},{5,1},{9,13},{13,9},{2,6},{6,2},{1... | collective-permute-start | bytes 393224 | tf_op jit(solution)/shard_map/ppermute | solution.py:299
  21.3 3.7 %collective-permute-start.7 = (bf16[2,1,192,128]{3,2,1,0:T(8,128)(2,1)S(1)}, bf16[2,1,192,128]{3,2,1,0:T(8,128)(2,1)S(1)}, u32[]{:S(2)}, u32[]{:S(2)}) collective-permute-start(bf16[2,1,192,128]{3,2,1,0:T(8,128)(2,1)S(1)} %shard_map.42.refs_1_), channel_id=1, source_target_pairs={{0,8},{4,12},{8,0},{12,4},{1,9},{5,13},{9,1},{13,5},{2,10},{6,14},... | collective-permute-start | bytes 294920 | tf_op jit(solution)/shard_map/ppermute | solution.py:293
  25.1 2.1 %collective-permute-start.14 = (bf16[2,1,192,128]{3,2,1,0:T(8,128)(2,1)S(1)}, bf16[2,1,192,128]{3,2,1,0:T(8,128)(2,1)S(1)}, u32[]{:S(2)}, u32[]{:S(2)}) collective-permute-start(bf16[2,1,192,128]{3,2,1,0:T(8,128)(2,1)S(1)} %collective-permute-done.9.refs_5_), channel_id=1, source_target_pairs={{0,4},{4,0},{8,12},{12,8},{1,5},{5,1},{9,13},{13,9},{2,6},{6,2},{1... | collective-permute-start | bytes 294920 | tf_op jit(solution)/shard_map/ppermute | solution.py:299
  28.3 2.6 %collective-permute-done.7.refs_5_ = bf16[2,1,192,128]{3,2,1,0:T(8,128)(2,1)S(1)} collective-permute-done((bf16[2,1,192,128]{3,2,1,0:T(8,128)(2,1)S(1)}, bf16[2,1,192,128]{3,2,1,0:T(8,128)(2,1)S(1)}, u32[]{:S(2)}, u32[]{:S(2)}) %collective-permute-start.7) | collective-permute-done | bytes 98336 | tf_op jit(solution)/shard_map/ppermute | solution.py:293
  31.4 1.5 %collective-permute-start.12 = (bf16[2,1,192,128]{3,2,1,0:T(8,128)(2,1)S(1)}, bf16[2,1,192,128]{3,2,1,0:T(8,128)(2,1)S(1)}, u32[]{:S(2)}, u32[]{:S(2)}) collective-permute-start(bf16[2,1,192,128]{3,2,1,0:T(8,128)(2,1)S(1)} %collective-permute-done.7.refs_5_), channel_id=1, source_target_pairs={{0,4},{4,0},{8,12},{12,8},{1,5},{5,1},{9,13},{13,9},{2,6},{6,2},{1... | collective-permute-start | bytes 294920 | tf_op jit(solution)/shard_map/ppermute | solution.py:299
  33.0 3.4 %collective-permute-done.14.refs_1_ = bf16[2,1,192,128]{3,2,1,0:T(8,128)(2,1)S(1)} collective-permute-done((bf16[2,1,192,128]{3,2,1,0:T(8,128)(2,1)S(1)}, bf16[2,1,192,128]{3,2,1,0:T(8,128)(2,1)S(1)}, u32[]{:S(2)}, u32[]{:S(2)}) %collective-permute-start.14) | collective-permute-done | bytes 98336 | tf_op jit(solution)/shard_map/ppermute | solution.py:299
  36.4 1.1 %shard_map.46.refs_2_ = f32[4,2,512,128]{3,2,1,0:T(8,128)} custom-call(bf16[2,512,1024]{2,1,0:T(8,128)(2,1)S(1)} %copy-done, f32[1,512,256]{2,1,0:T(8,128)S(1)} %shard_map.45.acc_ref, bf16[2,4,64,128]{3,2,1,0:T(8,128)(2,1)S(1)} %collective-permute-done.6.refs_0_, bf16[2,1,192,128]{3,2,1,0:T(8,128)(2,1)S(1)} %collective-permute-done.14.refs_1_), custom_call_target="tpu_custom_call" | custom-call | flops 1006632960 | bytes 524288 | tf_op jit(solution)/shard_map/pallas_call | solution.py:247
  38.2 1.7 %collective-permute-start.10 = (bf16[2,2,192,128]{3,2,1,0:T(8,128)(2,1)S(1)}, bf16[2,2,192,128]{3,2,1,0:T(8,128)(2,1)S(1)}, u32[]{:S(2)}, u32[]{:S(2)}) collective-permute-start(bf16[2,2,192,128]{3,2,1,0:T(8,128)(2,1)S(1)} %collective-permute-done.5.refs_5_), channel_id=1, source_target_pairs={{0,4},{4,0},{8,12},{12,8},{1,5},{5,1},{9,13},{13,9},{2,6},{6,2},{1... | collective-permute-start | bytes 589832 | tf_op jit(solution)/shard_map/ppermute | solution.py:299
  39.8 1.0 %collective-permute-done.4.refs_3_ = bf16[2,2,192,128]{3,2,1,0:T(8,128)(2,1)S(1)} collective-permute-done((bf16[2,2,192,128]{3,2,1,0:T(8,128)(2,1)S(1)}, bf16[2,2,192,128]{3,2,1,0:T(8,128)(2,1)S(1)}, u32[]{:S(2)}, u32[]{:S(2)}) %collective-permute-start.4) | collective-permute-done | bytes 196640 | tf_op jit(solution)/shard_map/ppermute | solution.py:289
  40.8 1.0 %shard_map.41.acc_ref = f32[2,512,256]{2,1,0:T(8,128)S(1)} custom-call(bf16[2,512,1024]{2,1,0:T(8,128)(2,1)S(1)} %copy-done, bf16[2,4,64,128]{3,2,1,0:T(8,128)(2,1)S(1)} %shard_map.38.refs_0_, bf16[2,2,192,128]{3,2,1,0:T(8,128)(2,1)S(1)} %shard_map.40.refs_1_, bf16[2,4,64,128]{3,2,1,0:T(8,128)(2,1)S(1)} %collective-permute-done.2.refs_2_, ...), custom_call_target="tpu_custom_call" | custom-call | flops 6039797760 | tf_op jit(solution)/shard_map/pallas_call | solution.py:232
  41.8 0.9 %collective-permute-done.12.refs_1_ = bf16[2,1,192,128]{3,2,1,0:T(8,128)(2,1)S(1)} collective-permute-done((bf16[2,1,192,128]{3,2,1,0:T(8,128)(2,1)S(1)}, bf16[2,1,192,128]{3,2,1,0:T(8,128)(2,1)S(1)}, u32[]{:S(2)}, u32[]{:S(2)}) %collective-permute-start.12) | collective-permute-done | bytes 98336 | tf_op jit(solution)/shard_map/ppermute | solution.py:299
  42.7 1.1 %shard_map.47.refs_2_ = f32[4,2,512,128]{3,2,1,0:T(8,128)} custom-call(bf16[2,512,1024]{2,1,0:T(8,128)(2,1)S(1)} %copy-done, f32[1,512,256]{2,1,0:T(8,128)S(1)} %shard_map.44.acc_ref, bf16[2,4,64,128]{3,2,1,0:T(8,128)(2,1)S(1)} %collective-permute-done.6.refs_0_, ...), custom_call_target="tpu_custom_call", output_to_operand_aliasing={{}: (4, {})} | custom-call | flops 1006632960 | bytes 524288 | tf_op jit(solution)/shard_map/pallas_call | solution.py:247
  43.9 1.2 %collective-permute-done.10.refs_1_ = bf16[2,2,192,128]{3,2,1,0:T(8,128)(2,1)S(1)} collective-permute-done((bf16[2,2,192,128]{3,2,1,0:T(8,128)(2,1)S(1)}, bf16[2,2,192,128]{3,2,1,0:T(8,128)(2,1)S(1)}, u32[]{:S(2)}, u32[]{:S(2)}) %collective-permute-start.10) | collective-permute-done | bytes 196640 | tf_op jit(solution)/shard_map/ppermute | solution.py:299
  45.0 1.3 %shard_map.48 = f32[4,2,512,128]{3,2,1,0:T(8,128)} custom-call(bf16[2,512,1024]{2,1,0:T(8,128)(2,1)S(1)} %copy-done, f32[2,512,256]{2,1,0:T(8,128)S(1)} %shard_map.41.acc_ref, bf16[2,4,64,128]{3,2,1,0:T(8,128)(2,1)S(1)} %collective-permute-done.6.refs_0_, ...), custom_call_target="tpu_custom_call", output_to_operand_aliasing={{}: (4, {})} | custom-call | flops 2013265920 | bytes 1048576 | tf_op jit(solution)/shard_map/pallas_call | solution.py:247
  (29 shorter events, 3.3 us)
Async XLA Ops:
  0.0 1.3 %copy-start.1 = (bf16[2,8,64]{2,1,0:T(8,128)(2,1)S(1)}, bf16[2,8,64]{2,1,0:T(8,128)(2,1)}, u32[]{:S(2)}) copy-start(bf16[2,8,64]{2,1,0:T(8,128)(2,1)} %phase_ref.2) | copy-start | bytes 6148
  2.0 6.6 %collective-permute-start = (f16[528,128]{1,0:T(8,128)(2,1)S(1)}, f16[528,128]{1,0:T(8,128)(2,1)S(1)}, u32[]{:S(2)}, u32[]{:S(2)}) collective-permute-start(f16[528,128]{1,0:T(8,128)(2,1)S(1)} %convert_element_type.19), channel_id=1, source_target_pairs={{0,2},{2,0},{1,3},{3,1},{4,6},{6,4},{5,7},{7,5},{8,10},{10,8},{9,1... | collective-permute-start | bytes 405512 | tf_op jit(solution)/shard_map/ppermute | solution.py:279
  7.6 5.5 %collective-permute-start.8 = (f16[400,128]{1,0:T(8,128)(2,1)S(1)}, f16[400,128]{1,0:T(8,128)(2,1)S(1)}, u32[]{:S(2)}, u32[]{:S(2)}) collective-permute-start(f16[400,128]{1,0:T(8,128)(2,1)S(1)} %convert_element_type.23), channel_id=1, source_target_pairs={{0,2},{2,0},{1,3},{3,1},{4,6},{6,4},{5,7},{7,5},{8,10},{10,8},{9,1... | collective-permute-start | bytes 307208 | tf_op jit(solution)/shard_map/ppermute | solution.py:279
  8.6 8.6 %collective-permute-start.2 = (bf16[2,4,64,128]{3,2,1,0:T(8,128)(2,1)S(1)}, bf16[2,4,64,128]{3,2,1,0:T(8,128)(2,1)S(1)}, u32[]{:S(2)}, u32[]{:S(2)}) collective-permute-start(bf16[2,4,64,128]{3,2,1,0:T(8,128)(2,1)S(1)} %shard_map.38.refs_0_), channel_id=1, source_target_pairs={{0,4},{4,0},{8,12},{12,8},{1,5},{5,1},{9,13},{13,9},{2,6},{6,2},{1... | collective-permute-start | bytes 393224 | tf_op jit(solution)/shard_map/ppermute | solution.py:289
  10.5 9.4 %collective-permute-start.3 = (bf16[2,4,64,128]{3,2,1,0:T(8,128)(2,1)S(1)}, bf16[2,4,64,128]{3,2,1,0:T(8,128)(2,1)S(1)}, u32[]{:S(2)}, u32[]{:S(2)}) collective-permute-start(bf16[2,4,64,128]{3,2,1,0:T(8,128)(2,1)S(1)} %shard_map.38.refs_0_), channel_id=1, source_target_pairs={{0,8},{4,12},{8,0},{12,4},{1,9},{5,13},{9,1},{13,5},{2,10},{6,14},... | collective-permute-start | bytes 393224 | tf_op jit(solution)/shard_map/ppermute | solution.py:293
  13.1 8.1 %collective-permute-start.1 = (f16[1168,128]{1,0:T(8,128)(2,1)S(1)}, f16[1168,128]{1,0:T(8,128)(2,1)S(1)}, u32[]{:S(2)}, u32[]{:S(2)}) collective-permute-start(f16[1168,128]{1,0:T(8,128)(2,1)S(1)} %convert_element_type.21), channel_id=1, source_target_pairs={{0,2},{2,0},{1,3},{3,1},{4,6},{6,4},{5,7},{7,5},{8,10},{10,8},{9,1... | collective-permute-start | bytes 897032 | tf_op jit(solution)/shard_map/ppermute | solution.py:279
  14.7 10.3 %collective-permute-start.9 = (bf16[2,1,192,128]{3,2,1,0:T(8,128)(2,1)S(1)}, bf16[2,1,192,128]{3,2,1,0:T(8,128)(2,1)S(1)}, u32[]{:S(2)}, u32[]{:S(2)}) collective-permute-start(bf16[2,1,192,128]{3,2,1,0:T(8,128)(2,1)S(1)} %shard_map.43.refs_1_), channel_id=1, source_target_pairs={{0,8},{4,12},{8,0},{12,4},{1,9},{5,13},{9,1},{13,5},{2,10},{6,14},... | collective-permute-start | bytes 294920 | tf_op jit(solution)/shard_map/ppermute | solution.py:293
  15.6 11.5 %collective-permute-start.13 = (bf16[2,1,192,128]{3,2,1,0:T(8,128)(2,1)S(1)}, bf16[2,1,192,128]{3,2,1,0:T(8,128)(2,1)S(1)}, u32[]{:S(2)}, u32[]{:S(2)}) collective-permute-start(bf16[2,1,192,128]{3,2,1,0:T(8,128)(2,1)S(1)} %shard_map.43.refs_1_), channel_id=1, source_target_pairs={{0,4},{4,0},{8,12},{12,8},{1,5},{5,1},{9,13},{13,9},{2,6},{6,2},{1... | collective-permute-start | bytes 294920 | tf_op jit(solution)/shard_map/ppermute | solution.py:289
  19.9 11.5 %collective-permute-start.6 = (bf16[2,4,64,128]{3,2,1,0:T(8,128)(2,1)S(1)}, bf16[2,4,64,128]{3,2,1,0:T(8,128)(2,1)S(1)}, u32[]{:S(2)}, u32[]{:S(2)}) collective-permute-start(bf16[2,4,64,128]{3,2,1,0:T(8,128)(2,1)S(1)} %collective-permute-done.3.refs_4_), channel_id=1, source_target_pairs={{0,4},{4,0},{8,12},{12,8},{1,5},{5,1},{9,13},{13,9},{2,6},{6,2},{1... | collective-permute-start | bytes 393224 | tf_op jit(solution)/shard_map/ppermute | solution.py:299
  21.3 9.7 %collective-permute-start.7 = (bf16[2,1,192,128]{3,2,1,0:T(8,128)(2,1)S(1)}, bf16[2,1,192,128]{3,2,1,0:T(8,128)(2,1)S(1)}, u32[]{:S(2)}, u32[]{:S(2)}) collective-permute-start(bf16[2,1,192,128]{3,2,1,0:T(8,128)(2,1)S(1)} %shard_map.42.refs_1_), channel_id=1, source_target_pairs={{0,8},{4,12},{8,0},{12,4},{1,9},{5,13},{9,1},{13,5},{2,10},{6,14},... | collective-permute-start | bytes 294920 | tf_op jit(solution)/shard_map/ppermute | solution.py:293
  25.0 12.6 %collective-permute-start.11 = (bf16[2,1,192,128]{3,2,1,0:T(8,128)(2,1)S(1)}, bf16[2,1,192,128]{3,2,1,0:T(8,128)(2,1)S(1)}, u32[]{:S(2)}, u32[]{:S(2)}) collective-permute-start(bf16[2,1,192,128]{3,2,1,0:T(8,128)(2,1)S(1)} %shard_map.42.refs_1_), channel_id=1, source_target_pairs={{0,4},{4,0},{8,12},{12,8},{1,5},{5,1},{9,13},{13,9},{2,6},{6,2},{1... | collective-permute-start | bytes 294920 | tf_op jit(solution)/shard_map/ppermute | solution.py:289
  25.0 2.2 %copy-start = (bf16[2,512,1024]{2,1,0:T(8,128)(2,1)S(1)}, bf16[2,512,1024]{2,1,0:T(8,128)(2,1)}, u32[]{:S(2)}) copy-start(bf16[2,512,1024]{2,1,0:T(8,128)(2,1)} %table_ref.11) | copy-start | bytes 6291460
  25.1 11.3 %collective-permute-start.14 = (bf16[2,1,192,128]{3,2,1,0:T(8,128)(2,1)S(1)}, bf16[2,1,192,128]{3,2,1,0:T(8,128)(2,1)S(1)}, u32[]{:S(2)}, u32[]{:S(2)}) collective-permute-start(bf16[2,1,192,128]{3,2,1,0:T(8,128)(2,1)S(1)} %collective-permute-done.9.refs_5_), channel_id=1, source_target_pairs={{0,4},{4,0},{8,12},{12,8},{1,5},{5,1},{9,13},{13,9},{2,6},{6,2},{1... | collective-permute-start | bytes 294920 | tf_op jit(solution)/shard_map/ppermute | solution.py:299
  27.7 10.4 %collective-permute-start.5 = (bf16[2,2,192,128]{3,2,1,0:T(8,128)(2,1)S(1)}, bf16[2,2,192,128]{3,2,1,0:T(8,128)(2,1)S(1)}, u32[]{:S(2)}, u32[]{:S(2)}) collective-permute-start(bf16[2,2,192,128]{3,2,1,0:T(8,128)(2,1)S(1)} %shard_map.40.refs_1_), channel_id=1, source_target_pairs={{0,8},{4,12},{8,0},{12,4},{1,9},{5,13},{9,1},{13,5},{2,10},{6,14},... | collective-permute-start | bytes 589832 | tf_op jit(solution)/shard_map/ppermute | solution.py:293
  31.0 9.9 %collective-permute-start.4 = (bf16[2,2,192,128]{3,2,1,0:T(8,128)(2,1)S(1)}, bf16[2,2,192,128]{3,2,1,0:T(8,128)(2,1)S(1)}, u32[]{:S(2)}, u32[]{:S(2)}) collective-permute-start(bf16[2,2,192,128]{3,2,1,0:T(8,128)(2,1)S(1)} %shard_map.40.refs_1_), channel_id=1, source_target_pairs={{0,4},{4,0},{8,12},{12,8},{1,5},{5,1},{9,13},{13,9},{2,6},{6,2},{1... | collective-permute-start | bytes 589832 | tf_op jit(solution)/shard_map/ppermute | solution.py:289
  31.4 11.3 %collective-permute-start.12 = (bf16[2,1,192,128]{3,2,1,0:T(8,128)(2,1)S(1)}, bf16[2,1,192,128]{3,2,1,0:T(8,128)(2,1)S(1)}, u32[]{:S(2)}, u32[]{:S(2)}) collective-permute-start(bf16[2,1,192,128]{3,2,1,0:T(8,128)(2,1)S(1)} %collective-permute-done.7.refs_5_), channel_id=1, source_target_pairs={{0,4},{4,0},{8,12},{12,8},{1,5},{5,1},{9,13},{13,9},{2,6},{6,2},{1... | collective-permute-start | bytes 294920 | tf_op jit(solution)/shard_map/ppermute | solution.py:299
  38.2 6.9 %collective-permute-start.10 = (bf16[2,2,192,128]{3,2,1,0:T(8,128)(2,1)S(1)}, bf16[2,2,192,128]{3,2,1,0:T(8,128)(2,1)S(1)}, u32[]{:S(2)}, u32[]{:S(2)}) collective-permute-start(bf16[2,2,192,128]{3,2,1,0:T(8,128)(2,1)S(1)} %collective-permute-done.5.refs_5_), channel_id=1, source_target_pairs={{0,4},{4,0},{8,12},{12,8},{1,5},{5,1},{9,13},{13,9},{2,6},{6,2},{1... | collective-permute-start | bytes 589832 | tf_op jit(solution)/shard_map/ppermute | solution.py:299

commit v6 on v5

--- a/solution.py
+++ b/solution.py
@@ -21,8 +21,8 @@
     ("block", 2): [("near", 0), ("across", 0)],
     ("block", 3): [("near", 0), ("across", 0)],
     ("passed", 0): [("near", 0)],
-    ("passed", 1): [("passed", 0), ("block", 3)],
-    ("passed", 2): [("passed", 1)],
+    ("passed", 1): [("passed", 0), ("block", 3), ("near", 1)],
+    ("passed", 2): [("passed", 1), ("near", 2)],
     ("passed", 3): [("passed", 2)],
     ("received", 2): [("block", 0)],
 }

time: 46.5 us -> 46.2 us (level)
  waiting for transfers between devices: 12.7 us -> 11.3 us
  starting transfers between devices: 23 us -> 24.1 us
    ppermute x4, waiting for transfers between devices: 5.33 us -> 0.16 us  [across(): return lax.ppermute(block, 'pb', [(i, i ^ 2) for i in range(self.n_pb)])]
    ppermute x4, waiting for transfers between devices: 1.02 us -> 5.91 us  [near(): return lax.ppermute(block, 'pb', [(i, i ^ 1) for i in range(self.n_pb)])]
    ppermute x4, starting transfers between devices: 6.55 us -> 8.91 us  [last(): lax.ppermute(self.get('passed', c), 'pb', [(i, i ^ 1) for i in range(self...]
    ppermute x4, waiting for transfers between devices: 5.52 us -> 4.43 us  [last(): lax.ppermute(self.get('passed', c), 'pb', [(i, i ^ 1) for i in range(self...]
    ppermute x4, starting transfers between devices: 3.96 us -> 2.99 us  [near(): return lax.ppermute(block, 'pb', [(i, i ^ 1) for i in range(self.n_pb)])]
where the time goes in v6:
time: 46.2 us; the launch traced here: 46.1 us
  starting transfers between devices  24.1 us (52%)
  waiting for transfers between devices  11.3 us (24%)
  Pallas kernels  9.07 us (20%)
  local copies, waits for them, and re-layouts  1.31 us (3%)
    ppermute x4, starting transfers between devices, last(): lax.ppermute(self.get('passed', c), 'pb', [(i, i ^ 1) for i in range(self...  8.91 us
    ppermute x4, starting transfers between devices, across(): return lax.ppermute(block, 'pb', [(i, i ^ 2) for i in range(self.n_pb)])  7.52 us
    ppermute x4, waiting for transfers between devices, near(): return lax.ppermute(block, 'pb', [(i, i ^ 1) for i in range(self.n_pb)])  5.91 us
    ppermute x3, starting transfers between devices, received(): lax.ppermute(message, 're', [(i, (i + s) % self.n_re) for i in range(self...  4.65 us
    ppermute x4, waiting for transfers between devices, last(): lax.ppermute(self.get('passed', c), 'pb', [(i, i ^ 1) for i in range(self...  4.43 us
    pallas_call x3, Pallas kernels, phonon_final(): pl.pallas_call(functools.partial(final_kernel, steps, n_pb, first, len(al...  3.56 us
    pallas_call x2, Pallas kernels, electron_sums(): pl.pallas_call(functools.partial(electron_kernel, n_re, cuts, mcuts, piec...  3.19 us
    ppermute x4, starting transfers between devices, near(): return lax.ppermute(block, 'pb', [(i, i ^ 1) for i in range(self.n_pb)])  2.99 us
  transfers between devices with their start and end apart: 15, of which 7 were waited for; matrix products, arithmetic and copies ran while one was open for 0% of the time, Pallas kernels for 15%

profile of v6, /device:TPU:0, one launch (start us, length us, event | category | flops | bytes accessed | tf_op | source)
XLA Modules:
  0.0 46.1 jit_solution(11194165794104492628)
XLA Ops:
  0.0 1.3 %slice.3.g_ref = bf16[2,64,32,128]{3,2,1,0:T(8,128)(2,1)S(1)} slice(bf16[2,256,32,128]{3,2,1,0:T(8,128)(2,1)} %g_ref.1), slice={[0:2], [0:64], [0:32], [0:128]} | slice | bytes 2097152 | tf_op jit(solution)/shard_map/slice | solution.py:323
  1.3 0.6 %shard_map.37 = (f32[2,4,64,128]{3,2,1,0:T(8,128)S(1)}, f32[528,128]{1,0:T(8,128)S(1)}) custom-call(bf16[2,8,64]{2,1,0:T(8,128)(2,1)S(1)} %copy-done.1, bf16[2,64,32,128]{3,2,1,0:T(8,128)(2,1)S(1)} %slice.3.g_ref), custom_call_target="tpu_custom_call" | custom-call | flops 16777216 | bytes 1048576 | tf_op jit(solution)/shard_map/pallas_call | solution.py:131
  2.0 3.0 %collective-permute-start = (f16[528,128]{1,0:T(8,128)(2,1)S(1)}, f16[528,128]{1,0:T(8,128)(2,1)S(1)}, u32[]{:S(2)}, u32[]{:S(2)}) collective-permute-start(f16[528,128]{1,0:T(8,128)(2,1)S(1)} %convert_element_type.19), channel_id=1, source_target_pairs={{0,2},{2,0},{1,3},{3,1},{4,6},{6,4},{5,7},{7,5},{8,10},{10,8},{9,1... | collective-permute-start | bytes 405512 | tf_op jit(solution)/shard_map/ppermute | solution.py:279
  5.0 2.6 %shard_map.39 = (f32[2,1,192,128]{3,2,1,0:T(8,128)S(1)}, f32[2,1,192,128]{3,2,1,0:T(8,128)S(1)}, f32[2,2,192,128]{3,2,1,0:T(8,128)S(1)}, f32[400,128]{1,0:T(8,128)S(1)}, f32[1168,128]{1,0:T(8,128)S(1)}) custom-call(bf16[2,8,64]{2,1,0:T(8,128)(2,1)S(1)} %copy-done.1, bf16[2,256,32,128]{3,2,1,0:T(8,128)(2,1)} %g_ref.1), custom_call_target="tpu_custom_call" | custom-call | flops 50331648 | bytes 3145728 | tf_op jit(solution)/shard_map/pallas_call | solution.py:131
  7.7 0.8 %collective-permute-done = f16[528,128]{1,0:T(8,128)(2,1)S(1)} collective-permute-done((f16[528,128]{1,0:T(8,128)(2,1)S(1)}, f16[528,128]{1,0:T(8,128)(2,1)S(1)}, u32[]{:S(2)}, u32[]{:S(2)}) %collective-permute-start) | collective-permute-done | bytes 135200 | tf_op jit(solution)/shard_map/ppermute | solution.py:279
  8.6 1.9 %collective-permute-start.2 = (bf16[2,4,64,128]{3,2,1,0:T(8,128)(2,1)S(1)}, bf16[2,4,64,128]{3,2,1,0:T(8,128)(2,1)S(1)}, u32[]{:S(2)}, u32[]{:S(2)}) collective-permute-start(bf16[2,4,64,128]{3,2,1,0:T(8,128)(2,1)S(1)} %shard_map.38.refs_0_), channel_id=1, source_target_pairs={{0,4},{4,0},{8,12},{12,8},{1,5},{5,1},{9,13},{13,9},{2,6},{6,2},{1... | collective-permute-start | bytes 393224 | tf_op jit(solution)/shard_map/ppermute | solution.py:289
  10.5 2.6 %collective-permute-start.3 = (bf16[2,4,64,128]{3,2,1,0:T(8,128)(2,1)S(1)}, bf16[2,4,64,128]{3,2,1,0:T(8,128)(2,1)S(1)}, u32[]{:S(2)}, u32[]{:S(2)}) collective-permute-start(bf16[2,4,64,128]{3,2,1,0:T(8,128)(2,1)S(1)} %shard_map.38.refs_0_), channel_id=1, source_target_pairs={{0,8},{4,12},{8,0},{12,4},{1,9},{5,13},{9,1},{13,5},{2,10},{6,14},... | collective-permute-start | bytes 393224 | tf_op jit(solution)/shard_map/ppermute | solution.py:293
  13.1 1.6 %collective-permute-start.1 = (f16[1168,128]{1,0:T(8,128)(2,1)S(1)}, f16[1168,128]{1,0:T(8,128)(2,1)S(1)}, u32[]{:S(2)}, u32[]{:S(2)}) collective-permute-start(f16[1168,128]{1,0:T(8,128)(2,1)S(1)} %convert_element_type.21), channel_id=1, source_target_pairs={{0,2},{2,0},{1,3},{3,1},{4,6},{6,4},{5,7},{7,5},{8,10},{10,8},{9,1... | collective-permute-start | bytes 897032 | tf_op jit(solution)/shard_map/ppermute | solution.py:279
  15.2 2.0 %collective-permute-start.9 = (bf16[2,1,192,128]{3,2,1,0:T(8,128)(2,1)S(1)}, bf16[2,1,192,128]{3,2,1,0:T(8,128)(2,1)S(1)}, u32[]{:S(2)}, u32[]{:S(2)}) collective-permute-start(bf16[2,1,192,128]{3,2,1,0:T(8,128)(2,1)S(1)} %shard_map.43.refs_1_), channel_id=1, source_target_pairs={{0,8},{4,12},{8,0},{12,4},{1,9},{5,13},{9,1},{13,5},{2,10},{6,14},... | collective-permute-start | bytes 294920 | tf_op jit(solution)/shard_map/ppermute | solution.py:293
  17.4 3.5 %collective-permute-start.6 = (bf16[2,4,64,128]{3,2,1,0:T(8,128)(2,1)S(1)}, bf16[2,4,64,128]{3,2,1,0:T(8,128)(2,1)S(1)}, u32[]{:S(2)}, u32[]{:S(2)}) collective-permute-start(bf16[2,4,64,128]{3,2,1,0:T(8,128)(2,1)S(1)} %collective-permute-done.3.refs_4_), channel_id=1, source_target_pairs={{0,4},{4,0},{8,12},{12,8},{1,5},{5,1},{9,13},{13,9},{2,6},{6,2},{1... | collective-permute-start | bytes 393224 | tf_op jit(solution)/shard_map/ppermute | solution.py:299
  21.0 0.6 %collective-permute-start.11 = (bf16[2,1,192,128]{3,2,1,0:T(8,128)(2,1)S(1)}, bf16[2,1,192,128]{3,2,1,0:T(8,128)(2,1)S(1)}, u32[]{:S(2)}, u32[]{:S(2)}) collective-permute-start(bf16[2,1,192,128]{3,2,1,0:T(8,128)(2,1)S(1)} %shard_map.42.refs_1_), channel_id=1, source_target_pairs={{0,4},{4,0},{8,12},{12,8},{1,5},{5,1},{9,13},{13,9},{2,6},{6,2},{1... | collective-permute-start | bytes 294920 | tf_op jit(solution)/shard_map/ppermute | solution.py:289
  21.5 2.6 %collective-permute-start.7 = (bf16[2,1,192,128]{3,2,1,0:T(8,128)(2,1)S(1)}, bf16[2,1,192,128]{3,2,1,0:T(8,128)(2,1)S(1)}, u32[]{:S(2)}, u32[]{:S(2)}) collective-permute-start(bf16[2,1,192,128]{3,2,1,0:T(8,128)(2,1)S(1)} %shard_map.42.refs_1_), channel_id=1, source_target_pairs={{0,8},{4,12},{8,0},{12,4},{1,9},{5,13},{9,1},{13,5},{2,10},{6,14},... | collective-permute-start | bytes 294920 | tf_op jit(solution)/shard_map/ppermute | solution.py:293
  24.2 1.6 %collective-permute-start.14 = (bf16[2,1,192,128]{3,2,1,0:T(8,128)(2,1)S(1)}, bf16[2,1,192,128]{3,2,1,0:T(8,128)(2,1)S(1)}, u32[]{:S(2)}, u32[]{:S(2)}) collective-permute-start(bf16[2,1,192,128]{3,2,1,0:T(8,128)(2,1)S(1)} %collective-permute-done.9.refs_5_), channel_id=1, source_target_pairs={{0,4},{4,0},{8,12},{12,8},{1,5},{5,1},{9,13},{13,9},{2,6},{6,2},{1... | collective-permute-start | bytes 294920 | tf_op jit(solution)/shard_map/ppermute | solution.py:299
  26.8 4.4 %collective-permute-done.11.refs_3_ = bf16[2,1,192,128]{3,2,1,0:T(8,128)(2,1)S(1)} collective-permute-done((bf16[2,1,192,128]{3,2,1,0:T(8,128)(2,1)S(1)}, bf16[2,1,192,128]{3,2,1,0:T(8,128)(2,1)S(1)}, u32[]{:S(2)}, u32[]{:S(2)}) %collective-permute-start.11) | collective-permute-done | bytes 98336 | tf_op jit(solution)/shard_map/ppermute | solution.py:289
  31.2 2.0 %collective-permute-start.13 = (bf16[2,1,192,128]{3,2,1,0:T(8,128)(2,1)S(1)}, bf16[2,1,192,128]{3,2,1,0:T(8,128)(2,1)S(1)}, u32[]{:S(2)}, u32[]{:S(2)}) collective-permute-start(bf16[2,1,192,128]{3,2,1,0:T(8,128)(2,1)S(1)} %collective-permute-done.7.refs_5_), channel_id=1, source_target_pairs={{0,4},{4,0},{8,12},{12,8},{1,5},{5,1},{9,13},{13,9},{2,6},{6,2},{1... | collective-permute-start | bytes 294920 | tf_op jit(solution)/shard_map/ppermute | solution.py:299
  33.2 1.7 %collective-permute-done.14.refs_1_ = bf16[2,1,192,128]{3,2,1,0:T(8,128)(2,1)S(1)} collective-permute-done((bf16[2,1,192,128]{3,2,1,0:T(8,128)(2,1)S(1)}, bf16[2,1,192,128]{3,2,1,0:T(8,128)(2,1)S(1)}, u32[]{:S(2)}, u32[]{:S(2)}) %collective-permute-start.14) | collective-permute-done | bytes 98336 | tf_op jit(solution)/shard_map/ppermute | solution.py:299
  35.0 1.1 %shard_map.46.refs_2_ = f32[4,2,512,128]{3,2,1,0:T(8,128)} custom-call(bf16[2,512,1024]{2,1,0:T(8,128)(2,1)S(1)} %copy-done, f32[1,512,256]{2,1,0:T(8,128)S(1)} %shard_map.45.acc_ref, bf16[2,4,64,128]{3,2,1,0:T(8,128)(2,1)S(1)} %collective-permute-done.6.refs_0_, bf16[2,1,192,128]{3,2,1,0:T(8,128)(2,1)S(1)} %collective-permute-done.14.refs_1_), custom_call_target="tpu_custom_call" | custom-call | flops 1006632960 | bytes 524288 | tf_op jit(solution)/shard_map/pallas_call | solution.py:247
  36.7 1.8 %collective-permute-start.12 = (bf16[2,2,192,128]{3,2,1,0:T(8,128)(2,1)S(1)}, bf16[2,2,192,128]{3,2,1,0:T(8,128)(2,1)S(1)}, u32[]{:S(2)}, u32[]{:S(2)}) collective-permute-start(bf16[2,2,192,128]{3,2,1,0:T(8,128)(2,1)S(1)} %collective-permute-done.5.refs_5_), channel_id=1, source_target_pairs={{0,4},{4,0},{8,12},{12,8},{1,5},{5,1},{9,13},{13,9},{2,6},{6,2},{1... | collective-permute-start | bytes 589832 | tf_op jit(solution)/shard_map/ppermute | solution.py:299
  38.5 1.5 %collective-permute-done.4.refs_3_ = bf16[2,2,192,128]{3,2,1,0:T(8,128)(2,1)S(1)} collective-permute-done((bf16[2,2,192,128]{3,2,1,0:T(8,128)(2,1)S(1)}, bf16[2,2,192,128]{3,2,1,0:T(8,128)(2,1)S(1)}, u32[]{:S(2)}, u32[]{:S(2)}) %collective-permute-start.4) | collective-permute-done | bytes 196640 | tf_op jit(solution)/shard_map/ppermute | solution.py:289
  40.0 1.0 %shard_map.41.acc_ref = f32[2,512,256]{2,1,0:T(8,128)S(1)} custom-call(bf16[2,512,1024]{2,1,0:T(8,128)(2,1)S(1)} %copy-done, bf16[2,4,64,128]{3,2,1,0:T(8,128)(2,1)S(1)} %shard_map.38.refs_0_, bf16[2,2,192,128]{3,2,1,0:T(8,128)(2,1)S(1)} %shard_map.40.refs_1_, bf16[2,4,64,128]{3,2,1,0:T(8,128)(2,1)S(1)} %collective-permute-done.2.refs_2_, ...), custom_call_target="tpu_custom_call" | custom-call | flops 6039797760 | tf_op jit(solution)/shard_map/pallas_call | solution.py:232
  40.9 1.1 %collective-permute-done.13.refs_1_ = bf16[2,1,192,128]{3,2,1,0:T(8,128)(2,1)S(1)} collective-permute-done((bf16[2,1,192,128]{3,2,1,0:T(8,128)(2,1)S(1)}, bf16[2,1,192,128]{3,2,1,0:T(8,128)(2,1)S(1)}, u32[]{:S(2)}, u32[]{:S(2)}) %collective-permute-start.13) | collective-permute-done | bytes 98336 | tf_op jit(solution)/shard_map/ppermute | solution.py:299
  42.1 1.1 %shard_map.47.refs_2_ = f32[4,2,512,128]{3,2,1,0:T(8,128)} custom-call(bf16[2,512,1024]{2,1,0:T(8,128)(2,1)S(1)} %copy-done, f32[1,512,256]{2,1,0:T(8,128)S(1)} %shard_map.44.acc_ref, bf16[2,4,64,128]{3,2,1,0:T(8,128)(2,1)S(1)} %collective-permute-done.6.refs_0_, ...), custom_call_target="tpu_custom_call", output_to_operand_aliasing={{}: (4, {})} | custom-call | flops 1006632960 | bytes 524288 | tf_op jit(solution)/shard_map/pallas_call | solution.py:247
  43.2 1.6 %collective-permute-done.12.refs_1_ = bf16[2,2,192,128]{3,2,1,0:T(8,128)(2,1)S(1)} collective-permute-done((bf16[2,2,192,128]{3,2,1,0:T(8,128)(2,1)S(1)}, bf16[2,2,192,128]{3,2,1,0:T(8,128)(2,1)S(1)}, u32[]{:S(2)}, u32[]{:S(2)}) %collective-permute-start.12) | collective-permute-done | bytes 196640 | tf_op jit(solution)/shard_map/ppermute | solution.py:299
  44.7 1.3 %shard_map.48 = f32[4,2,512,128]{3,2,1,0:T(8,128)} custom-call(bf16[2,512,1024]{2,1,0:T(8,128)(2,1)S(1)} %copy-done, f32[2,512,256]{2,1,0:T(8,128)S(1)} %shard_map.41.acc_ref, bf16[2,4,64,128]{3,2,1,0:T(8,128)(2,1)S(1)} %collective-permute-done.6.refs_0_, ...), custom_call_target="tpu_custom_call", output_to_operand_aliasing={{}: (4, {})} | custom-call | flops 2013265920 | bytes 1048576 | tf_op jit(solution)/shard_map/pallas_call | solution.py:247
  (29 shorter events, 2.6 us)
Async XLA Ops:
  0.0 1.3 %copy-start.1 = (bf16[2,8,64]{2,1,0:T(8,128)(2,1)S(1)}, bf16[2,8,64]{2,1,0:T(8,128)(2,1)}, u32[]{:S(2)}) copy-start(bf16[2,8,64]{2,1,0:T(8,128)(2,1)} %phase_ref.2) | copy-start | bytes 6148
  2.0 6.6 %collective-permute-start = (f16[528,128]{1,0:T(8,128)(2,1)S(1)}, f16[528,128]{1,0:T(8,128)(2,1)S(1)}, u32[]{:S(2)}, u32[]{:S(2)}) collective-permute-start(f16[528,128]{1,0:T(8,128)(2,1)S(1)} %convert_element_type.19), channel_id=1, source_target_pairs={{0,2},{2,0},{1,3},{3,1},{4,6},{6,4},{5,7},{7,5},{8,10},{10,8},{9,1... | collective-permute-start | bytes 405512 | tf_op jit(solution)/shard_map/ppermute | solution.py:279
  7.6 5.5 %collective-permute-start.8 = (f16[400,128]{1,0:T(8,128)(2,1)S(1)}, f16[400,128]{1,0:T(8,128)(2,1)S(1)}, u32[]{:S(2)}, u32[]{:S(2)}) collective-permute-start(f16[400,128]{1,0:T(8,128)(2,1)S(1)} %convert_element_type.23), channel_id=1, source_target_pairs={{0,2},{2,0},{1,3},{3,1},{4,6},{6,4},{5,7},{7,5},{8,10},{10,8},{9,1... | collective-permute-start | bytes 307208 | tf_op jit(solution)/shard_map/ppermute | solution.py:279
  8.6 8.6 %collective-permute-start.2 = (bf16[2,4,64,128]{3,2,1,0:T(8,128)(2,1)S(1)}, bf16[2,4,64,128]{3,2,1,0:T(8,128)(2,1)S(1)}, u32[]{:S(2)}, u32[]{:S(2)}) collective-permute-start(bf16[2,4,64,128]{3,2,1,0:T(8,128)(2,1)S(1)} %shard_map.38.refs_0_), channel_id=1, source_target_pairs={{0,4},{4,0},{8,12},{12,8},{1,5},{5,1},{9,13},{13,9},{2,6},{6,2},{1... | collective-permute-start | bytes 393224 | tf_op jit(solution)/shard_map/ppermute | solution.py:289
  10.5 6.9 %collective-permute-start.3 = (bf16[2,4,64,128]{3,2,1,0:T(8,128)(2,1)S(1)}, bf16[2,4,64,128]{3,2,1,0:T(8,128)(2,1)S(1)}, u32[]{:S(2)}, u32[]{:S(2)}) collective-permute-start(bf16[2,4,64,128]{3,2,1,0:T(8,128)(2,1)S(1)} %shard_map.38.refs_0_), channel_id=1, source_target_pairs={{0,8},{4,12},{8,0},{12,4},{1,9},{5,13},{9,1},{13,5},{2,10},{6,14},... | collective-permute-start | bytes 393224 | tf_op jit(solution)/shard_map/ppermute | solution.py:293
  13.1 7.7 %collective-permute-start.1 = (f16[1168,128]{1,0:T(8,128)(2,1)S(1)}, f16[1168,128]{1,0:T(8,128)(2,1)S(1)}, u32[]{:S(2)}, u32[]{:S(2)}) collective-permute-start(f16[1168,128]{1,0:T(8,128)(2,1)S(1)} %convert_element_type.21), channel_id=1, source_target_pairs={{0,2},{2,0},{1,3},{3,1},{4,6},{6,4},{5,7},{7,5},{8,10},{10,8},{9,1... | collective-permute-start | bytes 897032 | tf_op jit(solution)/shard_map/ppermute | solution.py:279
  14.7 9.5 %collective-permute-start.10 = (bf16[2,1,192,128]{3,2,1,0:T(8,128)(2,1)S(1)}, bf16[2,1,192,128]{3,2,1,0:T(8,128)(2,1)S(1)}, u32[]{:S(2)}, u32[]{:S(2)}) collective-permute-start(bf16[2,1,192,128]{3,2,1,0:T(8,128)(2,1)S(1)} %shard_map.43.refs_1_), channel_id=1, source_target_pairs={{0,4},{4,0},{8,12},{12,8},{1,5},{5,1},{9,13},{13,9},{2,6},{6,2},{1... | collective-permute-start | bytes 294920 | tf_op jit(solution)/shard_map/ppermute | solution.py:289
  15.2 9.0 %collective-permute-start.9 = (bf16[2,1,192,128]{3,2,1,0:T(8,128)(2,1)S(1)}, bf16[2,1,192,128]{3,2,1,0:T(8,128)(2,1)S(1)}, u32[]{:S(2)}, u32[]{:S(2)}) collective-permute-start(bf16[2,1,192,128]{3,2,1,0:T(8,128)(2,1)S(1)} %shard_map.43.refs_1_), channel_id=1, source_target_pairs={{0,8},{4,12},{8,0},{12,4},{1,9},{5,13},{9,1},{13,5},{2,10},{6,14},... | collective-permute-start | bytes 294920 | tf_op jit(solution)/shard_map/ppermute | solution.py:293
  17.4 15.9 %collective-permute-start.6 = (bf16[2,4,64,128]{3,2,1,0:T(8,128)(2,1)S(1)}, bf16[2,4,64,128]{3,2,1,0:T(8,128)(2,1)S(1)}, u32[]{:S(2)}, u32[]{:S(2)}) collective-permute-start(bf16[2,4,64,128]{3,2,1,0:T(8,128)(2,1)S(1)} %collective-permute-done.3.refs_4_), channel_id=1, source_target_pairs={{0,4},{4,0},{8,12},{12,8},{1,5},{5,1},{9,13},{13,9},{2,6},{6,2},{1... | collective-permute-start | bytes 393224 | tf_op jit(solution)/shard_map/ppermute | solution.py:299
  21.0 10.2 %collective-permute-start.11 = (bf16[2,1,192,128]{3,2,1,0:T(8,128)(2,1)S(1)}, bf16[2,1,192,128]{3,2,1,0:T(8,128)(2,1)S(1)}, u32[]{:S(2)}, u32[]{:S(2)}) collective-permute-start(bf16[2,1,192,128]{3,2,1,0:T(8,128)(2,1)S(1)} %shard_map.42.refs_1_), channel_id=1, source_target_pairs={{0,4},{4,0},{8,12},{12,8},{1,5},{5,1},{9,13},{13,9},{2,6},{6,2},{1... | collective-permute-start | bytes 294920 | tf_op jit(solution)/shard_map/ppermute | solution.py:289
  21.5 9.7 %collective-permute-start.7 = (bf16[2,1,192,128]{3,2,1,0:T(8,128)(2,1)S(1)}, bf16[2,1,192,128]{3,2,1,0:T(8,128)(2,1)S(1)}, u32[]{:S(2)}, u32[]{:S(2)}) collective-permute-start(bf16[2,1,192,128]{3,2,1,0:T(8,128)(2,1)S(1)} %shard_map.42.refs_1_), channel_id=1, source_target_pairs={{0,8},{4,12},{8,0},{12,4},{1,9},{5,13},{9,1},{13,5},{2,10},{6,14},... | collective-permute-start | bytes 294920 | tf_op jit(solution)/shard_map/ppermute | solution.py:293
  24.1 1.7 %copy-start = (bf16[2,512,1024]{2,1,0:T(8,128)(2,1)S(1)}, bf16[2,512,1024]{2,1,0:T(8,128)(2,1)}, u32[]{:S(2)}) copy-start(bf16[2,512,1024]{2,1,0:T(8,128)(2,1)} %table_ref.11) | copy-start | bytes 6291460
  24.2 10.8 %collective-permute-start.14 = (bf16[2,1,192,128]{3,2,1,0:T(8,128)(2,1)S(1)}, bf16[2,1,192,128]{3,2,1,0:T(8,128)(2,1)S(1)}, u32[]{:S(2)}, u32[]{:S(2)}) collective-permute-start(bf16[2,1,192,128]{3,2,1,0:T(8,128)(2,1)S(1)} %collective-permute-done.9.refs_5_), channel_id=1, source_target_pairs={{0,4},{4,0},{8,12},{12,8},{1,5},{5,1},{9,13},{13,9},{2,6},{6,2},{1... | collective-permute-start | bytes 294920 | tf_op jit(solution)/shard_map/ppermute | solution.py:299
  26.4 10.3 %collective-permute-start.5 = (bf16[2,2,192,128]{3,2,1,0:T(8,128)(2,1)S(1)}, bf16[2,2,192,128]{3,2,1,0:T(8,128)(2,1)S(1)}, u32[]{:S(2)}, u32[]{:S(2)}) collective-permute-start(bf16[2,2,192,128]{3,2,1,0:T(8,128)(2,1)S(1)} %shard_map.40.refs_1_), channel_id=1, source_target_pairs={{0,8},{4,12},{8,0},{12,4},{1,9},{5,13},{9,1},{13,5},{2,10},{6,14},... | collective-permute-start | bytes 589832 | tf_op jit(solution)/shard_map/ppermute | solution.py:293
  31.2 8.8 %collective-permute-start.4 = (bf16[2,2,192,128]{3,2,1,0:T(8,128)(2,1)S(1)}, bf16[2,2,192,128]{3,2,1,0:T(8,128)(2,1)S(1)}, u32[]{:S(2)}, u32[]{:S(2)}) collective-permute-start(bf16[2,2,192,128]{3,2,1,0:T(8,128)(2,1)S(1)} %shard_map.40.refs_1_), channel_id=1, source_target_pairs={{0,4},{4,0},{8,12},{12,8},{1,5},{5,1},{9,13},{13,9},{2,6},{6,2},{1... | collective-permute-start | bytes 589832 | tf_op jit(solution)/shard_map/ppermute | solution.py:289
  31.2 10.9 %collective-permute-start.13 = (bf16[2,1,192,128]{3,2,1,0:T(8,128)(2,1)S(1)}, bf16[2,1,192,128]{3,2,1,0:T(8,128)(2,1)S(1)}, u32[]{:S(2)}, u32[]{:S(2)}) collective-permute-start(bf16[2,1,192,128]{3,2,1,0:T(8,128)(2,1)S(1)} %collective-permute-done.7.refs_5_), channel_id=1, source_target_pairs={{0,4},{4,0},{8,12},{12,8},{1,5},{5,1},{9,13},{13,9},{2,6},{6,2},{1... | collective-permute-start | bytes 294920 | tf_op jit(solution)/shard_map/ppermute | solution.py:299
  36.7 8.1 %collective-permute-start.12 = (bf16[2,2,192,128]{3,2,1,0:T(8,128)(2,1)S(1)}, bf16[2,2,192,128]{3,2,1,0:T(8,128)(2,1)S(1)}, u32[]{:S(2)}, u32[]{:S(2)}) collective-permute-start(bf16[2,2,192,128]{3,2,1,0:T(8,128)(2,1)S(1)} %collective-permute-done.5.refs_5_), channel_id=1, source_target_pairs={{0,4},{4,0},{8,12},{12,8},{1,5},{5,1},{9,13},{13,9},{2,6},{6,2},{1... | collective-permute-start | bytes 589832 | tf_op jit(solution)/shard_map/ppermute | solution.py:299

commit v7 on v6

--- a/solution.py
+++ b/solution.py
@@ -28,7 +28,7 @@
 }
 MCUTS = (1, 3)
 PHON = 80
-PARTS = 2
+PARTS = 4
 SMALL = 16 * 2**20
 LARGE = 50 * 2**20
 VMEM = pl.BlockSpec(memory_space=pltpu.VMEM)

time: 46.2 us -> 46.2 us (level)
  no operation moved by 1% of the time
where the time goes in v7:
time: 46.2 us; the launch traced here: 46 us
  starting transfers between devices  24.1 us (52%)
  waiting for transfers between devices  11.4 us (25%)
  Pallas kernels  8.91 us (19%)
  local copies, waits for them, and re-layouts  1.31 us (3%)
    ppermute x4, starting transfers between devices, last(): lax.ppermute(self.get('passed', c), 'pb', [(i, i ^ 1) for i in range(self...  8.97 us
    ppermute x4, starting transfers between devices, across(): return lax.ppermute(block, 'pb', [(i, i ^ 2) for i in range(self.n_pb)])  7.52 us
    ppermute x4, waiting for transfers between devices, near(): return lax.ppermute(block, 'pb', [(i, i ^ 1) for i in range(self.n_pb)])  5.91 us
    ppermute x3, starting transfers between devices, received(): lax.ppermute(message, 're', [(i, (i + s) % self.n_re) for i in range(self...  4.65 us
    ppermute x4, waiting for transfers between devices, last(): lax.ppermute(self.get('passed', c), 'pb', [(i, i ^ 1) for i in range(self...  4.48 us
    pallas_call x3, Pallas kernels, phonon_final(): pl.pallas_call(functools.partial(final_kernel, steps, n_pb, first, len(al...  3.4 us
    pallas_call x2, Pallas kernels, electron_sums(): pl.pallas_call(functools.partial(electron_kernel, n_re, cuts, mcuts, piec...  3.19 us
    ppermute x4, starting transfers between devices, near(): return lax.ppermute(block, 'pb', [(i, i ^ 1) for i in range(self.n_pb)])  2.99 us
  transfers between devices with their start and end apart: 15, of which 7 were waited for; matrix products, arithmetic and copies ran while one was open for 0% of the time, Pallas kernels for 15%

profile of v7, /device:TPU:0, one launch (start us, length us, event | category | flops | bytes accessed | tf_op | source)
XLA Modules:
  0.0 46.0 jit_solution(12221404861598175786)
XLA Ops:
  0.0 1.3 %slice.3.g_ref = bf16[2,64,32,128]{3,2,1,0:T(8,128)(2,1)S(1)} slice(bf16[2,256,32,128]{3,2,1,0:T(8,128)(2,1)} %g_ref.1), slice={[0:2], [0:64], [0:32], [0:128]} | slice | bytes 2097152 | tf_op jit(solution)/shard_map/slice | solution.py:323
  1.3 0.6 %shard_map.37 = (f32[2,4,64,128]{3,2,1,0:T(8,128)S(1)}, f32[528,128]{1,0:T(8,128)S(1)}) custom-call(bf16[2,8,64]{2,1,0:T(8,128)(2,1)S(1)} %copy-done.1, bf16[2,64,32,128]{3,2,1,0:T(8,128)(2,1)S(1)} %slice.3.g_ref), custom_call_target="tpu_custom_call" | custom-call | flops 16777216 | bytes 1048576 | tf_op jit(solution)/shard_map/pallas_call | solution.py:131
  2.0 3.0 %collective-permute-start = (f16[528,128]{1,0:T(8,128)(2,1)S(1)}, f16[528,128]{1,0:T(8,128)(2,1)S(1)}, u32[]{:S(2)}, u32[]{:S(2)}) collective-permute-start(f16[528,128]{1,0:T(8,128)(2,1)S(1)} %convert_element_type.19), channel_id=1, source_target_pairs={{0,2},{2,0},{1,3},{3,1},{4,6},{6,4},{5,7},{7,5},{8,10},{10,8},{9,1... | collective-permute-start | bytes 405512 | tf_op jit(solution)/shard_map/ppermute | solution.py:279
  5.0 2.6 %shard_map.39 = (f32[2,1,192,128]{3,2,1,0:T(8,128)S(1)}, f32[2,1,192,128]{3,2,1,0:T(8,128)S(1)}, f32[2,2,192,128]{3,2,1,0:T(8,128)S(1)}, f32[400,128]{1,0:T(8,128)S(1)}, f32[1168,128]{1,0:T(8,128)S(1)}) custom-call(bf16[2,8,64]{2,1,0:T(8,128)(2,1)S(1)} %copy-done.1, bf16[2,256,32,128]{3,2,1,0:T(8,128)(2,1)} %g_ref.1), custom_call_target="tpu_custom_call" | custom-call | flops 50331648 | bytes 3145728 | tf_op jit(solution)/shard_map/pallas_call | solution.py:131
  7.7 0.8 %collective-permute-done = f16[528,128]{1,0:T(8,128)(2,1)S(1)} collective-permute-done((f16[528,128]{1,0:T(8,128)(2,1)S(1)}, f16[528,128]{1,0:T(8,128)(2,1)S(1)}, u32[]{:S(2)}, u32[]{:S(2)}) %collective-permute-start) | collective-permute-done | bytes 135200 | tf_op jit(solution)/shard_map/ppermute | solution.py:279
  8.6 1.9 %collective-permute-start.2 = (bf16[2,4,64,128]{3,2,1,0:T(8,128)(2,1)S(1)}, bf16[2,4,64,128]{3,2,1,0:T(8,128)(2,1)S(1)}, u32[]{:S(2)}, u32[]{:S(2)}) collective-permute-start(bf16[2,4,64,128]{3,2,1,0:T(8,128)(2,1)S(1)} %shard_map.38.refs_0_), channel_id=1, source_target_pairs={{0,4},{4,0},{8,12},{12,8},{1,5},{5,1},{9,13},{13,9},{2,6},{6,2},{1... | collective-permute-start | bytes 393224 | tf_op jit(solution)/shard_map/ppermute | solution.py:289
  10.5 2.6 %collective-permute-start.3 = (bf16[2,4,64,128]{3,2,1,0:T(8,128)(2,1)S(1)}, bf16[2,4,64,128]{3,2,1,0:T(8,128)(2,1)S(1)}, u32[]{:S(2)}, u32[]{:S(2)}) collective-permute-start(bf16[2,4,64,128]{3,2,1,0:T(8,128)(2,1)S(1)} %shard_map.38.refs_0_), channel_id=1, source_target_pairs={{0,8},{4,12},{8,0},{12,4},{1,9},{5,13},{9,1},{13,5},{2,10},{6,14},... | collective-permute-start | bytes 393224 | tf_op jit(solution)/shard_map/ppermute | solution.py:293
  13.1 1.6 %collective-permute-start.1 = (f16[1168,128]{1,0:T(8,128)(2,1)S(1)}, f16[1168,128]{1,0:T(8,128)(2,1)S(1)}, u32[]{:S(2)}, u32[]{:S(2)}) collective-permute-start(f16[1168,128]{1,0:T(8,128)(2,1)S(1)} %convert_element_type.21), channel_id=1, source_target_pairs={{0,2},{2,0},{1,3},{3,1},{4,6},{6,4},{5,7},{7,5},{8,10},{10,8},{9,1... | collective-permute-start | bytes 897032 | tf_op jit(solution)/shard_map/ppermute | solution.py:279
  15.2 2.0 %collective-permute-start.9 = (bf16[2,1,192,128]{3,2,1,0:T(8,128)(2,1)S(1)}, bf16[2,1,192,128]{3,2,1,0:T(8,128)(2,1)S(1)}, u32[]{:S(2)}, u32[]{:S(2)}) collective-permute-start(bf16[2,1,192,128]{3,2,1,0:T(8,128)(2,1)S(1)} %shard_map.43.refs_1_), channel_id=1, source_target_pairs={{0,8},{4,12},{8,0},{12,4},{1,9},{5,13},{9,1},{13,5},{2,10},{6,14},... | collective-permute-start | bytes 294920 | tf_op jit(solution)/shard_map/ppermute | solution.py:293
  17.4 3.5 %collective-permute-start.6 = (bf16[2,4,64,128]{3,2,1,0:T(8,128)(2,1)S(1)}, bf16[2,4,64,128]{3,2,1,0:T(8,128)(2,1)S(1)}, u32[]{:S(2)}, u32[]{:S(2)}) collective-permute-start(bf16[2,4,64,128]{3,2,1,0:T(8,128)(2,1)S(1)} %collective-permute-done.3.refs_4_), channel_id=1, source_target_pairs={{0,4},{4,0},{8,12},{12,8},{1,5},{5,1},{9,13},{13,9},{2,6},{6,2},{1... | collective-permute-start | bytes 393224 | tf_op jit(solution)/shard_map/ppermute | solution.py:299
  21.0 0.6 %collective-permute-start.11 = (bf16[2,1,192,128]{3,2,1,0:T(8,128)(2,1)S(1)}, bf16[2,1,192,128]{3,2,1,0:T(8,128)(2,1)S(1)}, u32[]{:S(2)}, u32[]{:S(2)}) collective-permute-start(bf16[2,1,192,128]{3,2,1,0:T(8,128)(2,1)S(1)} %shard_map.42.refs_1_), channel_id=1, source_target_pairs={{0,4},{4,0},{8,12},{12,8},{1,5},{5,1},{9,13},{13,9},{2,6},{6,2},{1... | collective-permute-start | bytes 294920 | tf_op jit(solution)/shard_map/ppermute | solution.py:289
  21.5 2.6 %collective-permute-start.7 = (bf16[2,1,192,128]{3,2,1,0:T(8,128)(2,1)S(1)}, bf16[2,1,192,128]{3,2,1,0:T(8,128)(2,1)S(1)}, u32[]{:S(2)}, u32[]{:S(2)}) collective-permute-start(bf16[2,1,192,128]{3,2,1,0:T(8,128)(2,1)S(1)} %shard_map.42.refs_1_), channel_id=1, source_target_pairs={{0,8},{4,12},{8,0},{12,4},{1,9},{5,13},{9,1},{13,5},{2,10},{6,14},... | collective-permute-start | bytes 294920 | tf_op jit(solution)/shard_map/ppermute | solution.py:293
  24.2 1.6 %collective-permute-start.14 = (bf16[2,1,192,128]{3,2,1,0:T(8,128)(2,1)S(1)}, bf16[2,1,192,128]{3,2,1,0:T(8,128)(2,1)S(1)}, u32[]{:S(2)}, u32[]{:S(2)}) collective-permute-start(bf16[2,1,192,128]{3,2,1,0:T(8,128)(2,1)S(1)} %collective-permute-done.9.refs_5_), channel_id=1, source_target_pairs={{0,4},{4,0},{8,12},{12,8},{1,5},{5,1},{9,13},{13,9},{2,6},{6,2},{1... | collective-permute-start | bytes 294920 | tf_op jit(solution)/shard_map/ppermute | solution.py:299
  26.8 4.4 %collective-permute-done.11.refs_3_ = bf16[2,1,192,128]{3,2,1,0:T(8,128)(2,1)S(1)} collective-permute-done((bf16[2,1,192,128]{3,2,1,0:T(8,128)(2,1)S(1)}, bf16[2,1,192,128]{3,2,1,0:T(8,128)(2,1)S(1)}, u32[]{:S(2)}, u32[]{:S(2)}) %collective-permute-start.11) | collective-permute-done | bytes 98336 | tf_op jit(solution)/shard_map/ppermute | solution.py:289
  31.2 2.0 %collective-permute-start.13 = (bf16[2,1,192,128]{3,2,1,0:T(8,128)(2,1)S(1)}, bf16[2,1,192,128]{3,2,1,0:T(8,128)(2,1)S(1)}, u32[]{:S(2)}, u32[]{:S(2)}) collective-permute-start(bf16[2,1,192,128]{3,2,1,0:T(8,128)(2,1)S(1)} %collective-permute-done.7.refs_5_), channel_id=1, source_target_pairs={{0,4},{4,0},{8,12},{12,8},{1,5},{5,1},{9,13},{13,9},{2,6},{6,2},{1... | collective-permute-start | bytes 294920 | tf_op jit(solution)/shard_map/ppermute | solution.py:299
  33.2 1.7 %collective-permute-done.14.refs_1_ = bf16[2,1,192,128]{3,2,1,0:T(8,128)(2,1)S(1)} collective-permute-done((bf16[2,1,192,128]{3,2,1,0:T(8,128)(2,1)S(1)}, bf16[2,1,192,128]{3,2,1,0:T(8,128)(2,1)S(1)}, u32[]{:S(2)}, u32[]{:S(2)}) %collective-permute-start.14) | collective-permute-done | bytes 98336 | tf_op jit(solution)/shard_map/ppermute | solution.py:299
  35.0 1.1 %shard_map.46.refs_2_ = f32[4,2,512,128]{3,2,1,0:T(8,128)} custom-call(bf16[2,512,1024]{2,1,0:T(8,128)(2,1)S(1)} %copy-done, f32[1,512,256]{2,1,0:T(8,128)S(1)} %shard_map.45.acc_ref, bf16[2,4,64,128]{3,2,1,0:T(8,128)(2,1)S(1)} %collective-permute-done.6.refs_0_, bf16[2,1,192,128]{3,2,1,0:T(8,128)(2,1)S(1)} %collective-permute-done.14.refs_1_), custom_call_target="tpu_custom_call" | custom-call | flops 1006632960 | bytes 524288 | tf_op jit(solution)/shard_map/pallas_call | solution.py:247
  36.6 1.8 %collective-permute-start.12 = (bf16[2,2,192,128]{3,2,1,0:T(8,128)(2,1)S(1)}, bf16[2,2,192,128]{3,2,1,0:T(8,128)(2,1)S(1)}, u32[]{:S(2)}, u32[]{:S(2)}) collective-permute-start(bf16[2,2,192,128]{3,2,1,0:T(8,128)(2,1)S(1)} %collective-permute-done.5.refs_5_), channel_id=1, source_target_pairs={{0,4},{4,0},{8,12},{12,8},{1,5},{5,1},{9,13},{13,9},{2,6},{6,2},{1... | collective-permute-start | bytes 589832 | tf_op jit(solution)/shard_map/ppermute | solution.py:299
  38.5 1.5 %collective-permute-done.4.refs_3_ = bf16[2,2,192,128]{3,2,1,0:T(8,128)(2,1)S(1)} collective-permute-done((bf16[2,2,192,128]{3,2,1,0:T(8,128)(2,1)S(1)}, bf16[2,2,192,128]{3,2,1,0:T(8,128)(2,1)S(1)}, u32[]{:S(2)}, u32[]{:S(2)}) %collective-permute-start.4) | collective-permute-done | bytes 196640 | tf_op jit(solution)/shard_map/ppermute | solution.py:289
  40.0 1.0 %shard_map.41.acc_ref = f32[2,512,256]{2,1,0:T(8,128)S(1)} custom-call(bf16[2,512,1024]{2,1,0:T(8,128)(2,1)S(1)} %copy-done, bf16[2,4,64,128]{3,2,1,0:T(8,128)(2,1)S(1)} %shard_map.38.refs_0_, bf16[2,2,192,128]{3,2,1,0:T(8,128)(2,1)S(1)} %shard_map.40.refs_1_, bf16[2,4,64,128]{3,2,1,0:T(8,128)(2,1)S(1)} %collective-permute-done.2.refs_2_, ...), custom_call_target="tpu_custom_call" | custom-call | flops 6039797760 | tf_op jit(solution)/shard_map/pallas_call | solution.py:232
  40.9 1.1 %collective-permute-done.13.refs_1_ = bf16[2,1,192,128]{3,2,1,0:T(8,128)(2,1)S(1)} collective-permute-done((bf16[2,1,192,128]{3,2,1,0:T(8,128)(2,1)S(1)}, bf16[2,1,192,128]{3,2,1,0:T(8,128)(2,1)S(1)}, u32[]{:S(2)}, u32[]{:S(2)}) %collective-permute-start.13) | collective-permute-done | bytes 98336 | tf_op jit(solution)/shard_map/ppermute | solution.py:299
  42.1 1.1 %shard_map.47.refs_2_ = f32[4,2,512,128]{3,2,1,0:T(8,128)} custom-call(bf16[2,512,1024]{2,1,0:T(8,128)(2,1)S(1)} %copy-done, f32[1,512,256]{2,1,0:T(8,128)S(1)} %shard_map.44.acc_ref, bf16[2,4,64,128]{3,2,1,0:T(8,128)(2,1)S(1)} %collective-permute-done.6.refs_0_, ...), custom_call_target="tpu_custom_call", output_to_operand_aliasing={{}: (4, {})} | custom-call | flops 1006632960 | bytes 524288 | tf_op jit(solution)/shard_map/pallas_call | solution.py:247
  43.1 1.6 %collective-permute-done.12.refs_1_ = bf16[2,2,192,128]{3,2,1,0:T(8,128)(2,1)S(1)} collective-permute-done((bf16[2,2,192,128]{3,2,1,0:T(8,128)(2,1)S(1)}, bf16[2,2,192,128]{3,2,1,0:T(8,128)(2,1)S(1)}, u32[]{:S(2)}, u32[]{:S(2)}) %collective-permute-start.12) | collective-permute-done | bytes 196640 | tf_op jit(solution)/shard_map/ppermute | solution.py:299
  44.7 1.3 %shard_map.48 = f32[4,2,512,128]{3,2,1,0:T(8,128)} custom-call(bf16[2,512,1024]{2,1,0:T(8,128)(2,1)S(1)} %copy-done, f32[2,512,256]{2,1,0:T(8,128)S(1)} %shard_map.41.acc_ref, bf16[2,4,64,128]{3,2,1,0:T(8,128)(2,1)S(1)} %collective-permute-done.6.refs_0_, ...), custom_call_target="tpu_custom_call", output_to_operand_aliasing={{}: (4, {})} | custom-call | flops 2013265920 | bytes 1048576 | tf_op jit(solution)/shard_map/pallas_call | solution.py:247
  (29 shorter events, 2.7 us)
Async XLA Ops:
  0.0 1.3 %copy-start.1 = (bf16[2,8,64]{2,1,0:T(8,128)(2,1)S(1)}, bf16[2,8,64]{2,1,0:T(8,128)(2,1)}, u32[]{:S(2)}) copy-start(bf16[2,8,64]{2,1,0:T(8,128)(2,1)} %phase_ref.2) | copy-start | bytes 6148
  2.0 6.6 %collective-permute-start = (f16[528,128]{1,0:T(8,128)(2,1)S(1)}, f16[528,128]{1,0:T(8,128)(2,1)S(1)}, u32[]{:S(2)}, u32[]{:S(2)}) collective-permute-start(f16[528,128]{1,0:T(8,128)(2,1)S(1)} %convert_element_type.19), channel_id=1, source_target_pairs={{0,2},{2,0},{1,3},{3,1},{4,6},{6,4},{5,7},{7,5},{8,10},{10,8},{9,1... | collective-permute-start | bytes 405512 | tf_op jit(solution)/shard_map/ppermute | solution.py:279
  7.6 5.5 %collective-permute-start.8 = (f16[400,128]{1,0:T(8,128)(2,1)S(1)}, f16[400,128]{1,0:T(8,128)(2,1)S(1)}, u32[]{:S(2)}, u32[]{:S(2)}) collective-permute-start(f16[400,128]{1,0:T(8,128)(2,1)S(1)} %convert_element_type.23), channel_id=1, source_target_pairs={{0,2},{2,0},{1,3},{3,1},{4,6},{6,4},{5,7},{7,5},{8,10},{10,8},{9,1... | collective-permute-start | bytes 307208 | tf_op jit(solution)/shard_map/ppermute | solution.py:279
  8.6 8.6 %collective-permute-start.2 = (bf16[2,4,64,128]{3,2,1,0:T(8,128)(2,1)S(1)}, bf16[2,4,64,128]{3,2,1,0:T(8,128)(2,1)S(1)}, u32[]{:S(2)}, u32[]{:S(2)}) collective-permute-start(bf16[2,4,64,128]{3,2,1,0:T(8,128)(2,1)S(1)} %shard_map.38.refs_0_), channel_id=1, source_target_pairs={{0,4},{4,0},{8,12},{12,8},{1,5},{5,1},{9,13},{13,9},{2,6},{6,2},{1... | collective-permute-start | bytes 393224 | tf_op jit(solution)/shard_map/ppermute | solution.py:289
  10.5 6.9 %collective-permute-start.3 = (bf16[2,4,64,128]{3,2,1,0:T(8,128)(2,1)S(1)}, bf16[2,4,64,128]{3,2,1,0:T(8,128)(2,1)S(1)}, u32[]{:S(2)}, u32[]{:S(2)}) collective-permute-start(bf16[2,4,64,128]{3,2,1,0:T(8,128)(2,1)S(1)} %shard_map.38.refs_0_), channel_id=1, source_target_pairs={{0,8},{4,12},{8,0},{12,4},{1,9},{5,13},{9,1},{13,5},{2,10},{6,14},... | collective-permute-start | bytes 393224 | tf_op jit(solution)/shard_map/ppermute | solution.py:293
  13.1 7.7 %collective-permute-start.1 = (f16[1168,128]{1,0:T(8,128)(2,1)S(1)}, f16[1168,128]{1,0:T(8,128)(2,1)S(1)}, u32[]{:S(2)}, u32[]{:S(2)}) collective-permute-start(f16[1168,128]{1,0:T(8,128)(2,1)S(1)} %convert_element_type.21), channel_id=1, source_target_pairs={{0,2},{2,0},{1,3},{3,1},{4,6},{6,4},{5,7},{7,5},{8,10},{10,8},{9,1... | collective-permute-start | bytes 897032 | tf_op jit(solution)/shard_map/ppermute | solution.py:279
  14.7 9.5 %collective-permute-start.10 = (bf16[2,1,192,128]{3,2,1,0:T(8,128)(2,1)S(1)}, bf16[2,1,192,128]{3,2,1,0:T(8,128)(2,1)S(1)}, u32[]{:S(2)}, u32[]{:S(2)}) collective-permute-start(bf16[2,1,192,128]{3,2,1,0:T(8,128)(2,1)S(1)} %shard_map.43.refs_1_), channel_id=1, source_target_pairs={{0,4},{4,0},{8,12},{12,8},{1,5},{5,1},{9,13},{13,9},{2,6},{6,2},{1... | collective-permute-start | bytes 294920 | tf_op jit(solution)/shard_map/ppermute | solution.py:289
  15.2 9.0 %collective-permute-start.9 = (bf16[2,1,192,128]{3,2,1,0:T(8,128)(2,1)S(1)}, bf16[2,1,192,128]{3,2,1,0:T(8,128)(2,1)S(1)}, u32[]{:S(2)}, u32[]{:S(2)}) collective-permute-start(bf16[2,1,192,128]{3,2,1,0:T(8,128)(2,1)S(1)} %shard_map.43.refs_1_), channel_id=1, source_target_pairs={{0,8},{4,12},{8,0},{12,4},{1,9},{5,13},{9,1},{13,5},{2,10},{6,14},... | collective-permute-start | bytes 294920 | tf_op jit(solution)/shard_map/ppermute | solution.py:293
  17.4 15.9 %collective-permute-start.6 = (bf16[2,4,64,128]{3,2,1,0:T(8,128)(2,1)S(1)}, bf16[2,4,64,128]{3,2,1,0:T(8,128)(2,1)S(1)}, u32[]{:S(2)}, u32[]{:S(2)}) collective-permute-start(bf16[2,4,64,128]{3,2,1,0:T(8,128)(2,1)S(1)} %collective-permute-done.3.refs_4_), channel_id=1, source_target_pairs={{0,4},{4,0},{8,12},{12,8},{1,5},{5,1},{9,13},{13,9},{2,6},{6,2},{1... | collective-permute-start | bytes 393224 | tf_op jit(solution)/shard_map/ppermute | solution.py:299
  21.0 10.2 %collective-permute-start.11 = (bf16[2,1,192,128]{3,2,1,0:T(8,128)(2,1)S(1)}, bf16[2,1,192,128]{3,2,1,0:T(8,128)(2,1)S(1)}, u32[]{:S(2)}, u32[]{:S(2)}) collective-permute-start(bf16[2,1,192,128]{3,2,1,0:T(8,128)(2,1)S(1)} %shard_map.42.refs_1_), channel_id=1, source_target_pairs={{0,4},{4,0},{8,12},{12,8},{1,5},{5,1},{9,13},{13,9},{2,6},{6,2},{1... | collective-permute-start | bytes 294920 | tf_op jit(solution)/shard_map/ppermute | solution.py:289
  21.5 9.7 %collective-permute-start.7 = (bf16[2,1,192,128]{3,2,1,0:T(8,128)(2,1)S(1)}, bf16[2,1,192,128]{3,2,1,0:T(8,128)(2,1)S(1)}, u32[]{:S(2)}, u32[]{:S(2)}) collective-permute-start(bf16[2,1,192,128]{3,2,1,0:T(8,128)(2,1)S(1)} %shard_map.42.refs_1_), channel_id=1, source_target_pairs={{0,8},{4,12},{8,0},{12,4},{1,9},{5,13},{9,1},{13,5},{2,10},{6,14},... | collective-permute-start | bytes 294920 | tf_op jit(solution)/shard_map/ppermute | solution.py:293
  24.1 1.7 %copy-start = (bf16[2,512,1024]{2,1,0:T(8,128)(2,1)S(1)}, bf16[2,512,1024]{2,1,0:T(8,128)(2,1)}, u32[]{:S(2)}) copy-start(bf16[2,512,1024]{2,1,0:T(8,128)(2,1)} %table_ref.11) | copy-start | bytes 6291460
  24.2 10.8 %collective-permute-start.14 = (bf16[2,1,192,128]{3,2,1,0:T(8,128)(2,1)S(1)}, bf16[2,1,192,128]{3,2,1,0:T(8,128)(2,1)S(1)}, u32[]{:S(2)}, u32[]{:S(2)}) collective-permute-start(bf16[2,1,192,128]{3,2,1,0:T(8,128)(2,1)S(1)} %collective-permute-done.9.refs_5_), channel_id=1, source_target_pairs={{0,4},{4,0},{8,12},{12,8},{1,5},{5,1},{9,13},{13,9},{2,6},{6,2},{1... | collective-permute-start | bytes 294920 | tf_op jit(solution)/shard_map/ppermute | solution.py:299
  26.4 10.2 %collective-permute-start.5 = (bf16[2,2,192,128]{3,2,1,0:T(8,128)(2,1)S(1)}, bf16[2,2,192,128]{3,2,1,0:T(8,128)(2,1)S(1)}, u32[]{:S(2)}, u32[]{:S(2)}) collective-permute-start(bf16[2,2,192,128]{3,2,1,0:T(8,128)(2,1)S(1)} %shard_map.40.refs_1_), channel_id=1, source_target_pairs={{0,8},{4,12},{8,0},{12,4},{1,9},{5,13},{9,1},{13,5},{2,10},{6,14},... | collective-permute-start | bytes 589832 | tf_op jit(solution)/shard_map/ppermute | solution.py:293
  31.2 8.8 %collective-permute-start.4 = (bf16[2,2,192,128]{3,2,1,0:T(8,128)(2,1)S(1)}, bf16[2,2,192,128]{3,2,1,0:T(8,128)(2,1)S(1)}, u32[]{:S(2)}, u32[]{:S(2)}) collective-permute-start(bf16[2,2,192,128]{3,2,1,0:T(8,128)(2,1)S(1)} %shard_map.40.refs_1_), channel_id=1, source_target_pairs={{0,4},{4,0},{8,12},{12,8},{1,5},{5,1},{9,13},{13,9},{2,6},{6,2},{1... | collective-permute-start | bytes 589832 | tf_op jit(solution)/shard_map/ppermute | solution.py:289
  31.2 10.9 %collective-permute-start.13 = (bf16[2,1,192,128]{3,2,1,0:T(8,128)(2,1)S(1)}, bf16[2,1,192,128]{3,2,1,0:T(8,128)(2,1)S(1)}, u32[]{:S(2)}, u32[]{:S(2)}) collective-permute-start(bf16[2,1,192,128]{3,2,1,0:T(8,128)(2,1)S(1)} %collective-permute-done.7.refs_5_), channel_id=1, source_target_pairs={{0,4},{4,0},{8,12},{12,8},{1,5},{5,1},{9,13},{13,9},{2,6},{6,2},{1... | collective-permute-start | bytes 294920 | tf_op jit(solution)/shard_map/ppermute | solution.py:299
  36.6 8.1 %collective-permute-start.12 = (bf16[2,2,192,128]{3,2,1,0:T(8,128)(2,1)S(1)}, bf16[2,2,192,128]{3,2,1,0:T(8,128)(2,1)S(1)}, u32[]{:S(2)}, u32[]{:S(2)}) collective-permute-start(bf16[2,2,192,128]{3,2,1,0:T(8,128)(2,1)S(1)} %collective-permute-done.5.refs_5_), channel_id=1, source_target_pairs={{0,4},{4,0},{8,12},{12,8},{1,5},{5,1},{9,13},{13,9},{2,6},{6,2},{1... | collective-permute-start | bytes 589832 | tf_op jit(solution)/shard_map/ppermute | solution.py:299
